TPU v7x, 256 devices: a whole 4x4x8 slice. The times are simulated.
256 devices in a mesh: blk: 64 (over y, z_hi, x, core), head: 4 (over z_lo).
Axes of the slice: x: 4, y: 4, z: 8 (z_hi: 2, z_lo: 4; z = z_hi * 4 + z_lo), core: 2. Of those that a mesh axis runs over, the one named last changes fastest.
Arguments:
- query_in: bfloat16 [8192, 2048], P(('blk', 'head')), may hold values from -6 to 6
- key_in: bfloat16 [8192, 2048], P(('blk', 'head')), may hold values from -6 to 6
- value_in: bfloat16 [8192, 2048], P(('blk', 'head')), may hold values from -6 to 6
- saved_out: bfloat16 [8192, 2048], P(('blk', 'head')), may hold values from -0.59765625 to 0.59765625
- grad_out: bfloat16 [8192, 2048], P(('blk', 'head')), may hold values from -6 to 6
- saved_lse: float32 [8192, 16], P('blk', 'head'), may hold values from 3 to 6
- row_block: int32 [8192], replicated, may hold values from 0 to 15, as said below
- row_copy: int32 [8192], replicated, may hold values from 0 to 1, as said below
Outputs:
- grad_query: bfloat16 [8192, 2048], P(('blk', 'head'))
- grad_key: bfloat16 [8192, 2048], P(('blk', 'head'))
- grad_value: bfloat16 [8192, 2048], P(('blk', 'head'))
Inputs may be any that keep to these rules, and one draw needn't show every extreme that they name: `row_block`: rows g * 2 * 256 to (g + 1) * 2 * 256 - 1 all carry one block id, and each of the 16 ids is carried by exactly one such run. `row_copy`: in each aligned run of 128 rows exactly 64 rows are 1.
All inputs are finite; a program needn't handle non-finite values.
Results may differ from a plain program's by a relative error of at most 0.0085.
Values may be sent and summed in bfloat16 or wider, within the bound.
No kernel may reach another device: no remote copies, remote signals or barrier semaphores. Data moves between devices by JAX's collectives and lax.ppermute only.
A program may use at most 192 MiB of HBM per device.

v0:
```python
import jax
import jax.numpy as jnp
from jax import lax
from jax.experimental import pallas as pl
from jax.experimental.pallas import tpu as pltpu
from jax.sharding import Mesh
from jax.sharding import PartitionSpec as P

HD = 128
RUN = 128
HALF = RUN // 2
AXES = ("y", "zh", "xh", "xl", "c", "zl")
SIZES = (4, 2, 2, 2, 2, 4)
HEAD_AXES = ("zl", "zh", "xl")
QUERY_AXES = ("xh", "c")
RUNS = 4
SCALE = HD**-0.5
LOG2E = 1.4426950408889634
OFF = 1e30
F32 = jnp.float32
BF16 = jnp.bfloat16
VMEM = pl.BlockSpec(memory_space=pltpu.VMEM)
HBM = pl.BlockSpec(memory_space=pltpu.HBM)
SMEM = pl.BlockSpec(memory_space=pltpu.SMEM)


def iota(shape, axis):
    return lax.broadcasted_iota(jnp.int32, shape, axis)


def split_two(x):
    high = x.astype(BF16).astype(F32)
    return high, x - high


def contract(a, b, dim_a, dim_b):
    return lax.dot_general(a, b, (((dim_a,), (dim_b,)), ((), ())), preferred_element_type=F32)


def call(body, out_shape, args, smem=(), hbm=(), scratch=(), limit=32 << 20, cost=None):
    return pl.pallas_call(
        body,
        out_shape=out_shape,
        in_specs=[SMEM if i in smem else HBM if i in hbm else VMEM for i in range(len(args))],
        out_specs=jax.tree.map(lambda _: VMEM, out_shape),
        scratch_shapes=list(scratch),
        compiler_params=pltpu.CompilerParams(vmem_limit_bytes=limit),
        cost_estimate=cost,
    )(*args)


def pack_kernel(q_in, k_in, v_in, o_in, g_in, lse_in, out_ref, q_ref, k_ref, v_ref, o_ref, g_ref, lse_ref, sems):
    pairs = ((g_in, g_ref), (o_in, o_ref), (lse_in, lse_ref), (q_in, q_ref), (k_in, k_ref), (v_in, v_ref))
    copies = [pltpu.make_async_copy(a, b, sems.at[i]) for i, (a, b) in enumerate(pairs)]
    for copy in copies:
        copy.start()
    rows = q_ref.shape[0]
    for copy in copies[:3]:
        copy.wait()
    lane = iota((rows, 128), 1)
    delta = jnp.zeros((rows, 128), F32)
    for h in range(16):
        cols = slice(h * HD, (h + 1) * HD)
        term = g_ref[:, cols].astype(F32) * o_ref[:, cols].astype(F32)
        delta = jnp.where(lane == h, jnp.sum(term, axis=1, keepdims=True), delta)
    delta = jnp.concatenate([delta, jnp.zeros((128 - rows, 128), F32)], axis=0).T
    delta_high, delta_low = split_two(delta)
    lse_high, lse_low = split_two(lse_ref[...])
    row = iota((16, 128), 0)
    for copy in copies[3:]:
        copy.wait()
    for h in range(16):
        j = h % 4
        cols = slice(h * HD, (h + 1) * HD)
        for i, ref in enumerate((q_ref, g_ref, k_ref, v_ref)):
            out_ref[h, i * rows : (i + 1) * rows, :] = ref[:, cols]
        stats = jnp.where(row == 0, lse_high[j : j + 1], 0.0)
        stats = jnp.where(row == 1, lse_low[j : j + 1], stats)
        stats = jnp.where(row == 2, delta_high[h : h + 1], stats)
        stats = jnp.where(row == 3, delta_low[h : h + 1], stats)
        out_ref[h, 4 * rows : 4 * rows + 16, :] = stats.astype(BF16)


def placing(copy_ref, j):
    zh, xl = divmod(j, 2)
    shard = ((lax.axis_index("y") * 2 + zh) * 4 + lax.axis_index("xh") * 2 + xl) * 2 + lax.axis_index("c")
    copy = jnp.broadcast_to(copy_ref[pl.ds(shard, 1), :], (8, RUN)).astype(F32)
    upto = (iota((RUN, RUN), 0) <= iota((RUN, RUN), 1)).astype(BF16)
    count = contract(copy.astype(BF16), upto, 1, 0)
    index = iota((8, RUN), 1).astype(F32)
    place = jnp.where(copy > 0.5, HALF - 1.0 + count, index - count)
    place = jnp.broadcast_to(place[0:1], (RUN, RUN)).astype(jnp.int32)
    return (iota((RUN, RUN), 0) == place).astype(F32)


def sort_kernel(got_ref, copy_ref, qd_ref, kv_ref, kvn_ref):
    zl = lax.axis_index("zl")
    row = iota((16, RUN), 0)
    stats = []
    for j in range(RUNS):
        zh, xl = divmod(j, 2)
        one_hot = placing(copy_ref, j).astype(BF16)
        parts = [
            jnp.concatenate([got_ref[4 * z + j, 32 * i : 32 * i + 32, :] for z in range(4)], axis=0)
            for i in range(4)
        ]
        moved = contract(one_hot, jnp.concatenate(parts, axis=1), 1, 0).astype(BF16)
        qd_ref[256 * zh + 64 * xl : 256 * zh + 64 * xl + 64, :] = moved[:HALF, :256]
        qd_ref[256 * zh + 128 + 64 * xl : 256 * zh + 192 + 64 * xl, :] = moved[HALF:, :256]
        kvn_ref[128 * zh + 64 * xl : 128 * zh + 64 * xl + 64, :] = moved[:HALF, 256:]
        for y in range(4):
            kv_ref[y, 128 * zh + 64 * xl : 128 * zh + 64 * xl + 64, :] = moved[HALF:, 256:]
        lse = got_ref[4 * zl + j, 128:144, :].astype(F32)
        delta = jnp.concatenate(
            [got_ref[4 * z + j, 128:144, :].astype(F32)[:, :32] for z in range(4)], axis=1
        )
        both = jnp.where(row < 2, lse, delta).astype(BF16)
        stats.append(contract(both, one_hot, 1, 1))
    halves = []
    for zh in range(2):
        a, b = stats[2 * zh], stats[2 * zh + 1]
        halves.append(
            jnp.concatenate([a[:8, :HALF], b[:8, :HALF], a[:8, HALF:], b[:8, HALF:]], axis=1)
        )
    qd_ref[512:528, :] = jnp.concatenate(halves, axis=0).astype(BF16)


def attend_kernel(
    ids_ref, qd0, qd1, qd2, qd3, kv_ref, kvn_ref,
    dq_keep, dq_send, dkv_ref, dkvn_ref,
    q_all, g_all, lse_all, delta_all, k_all, kt_all, v_all, dk_all, dv_all,
):
    y, xh = lax.axis_index("y"), lax.axis_index("xh")
    for m, ref in enumerate((qd0, qd1, qd2, qd3)):
        stats = ref[512:528, :].astype(F32)
        for zh in range(2):
            block, at = zh * 2 + m // 2, 256 * (m % 2)
            q_all[block, at : at + 256, :] = ref[256 * zh : 256 * zh + 256, :HD]
            g_all[block, at : at + 256, :] = ref[256 * zh : 256 * zh + 256, HD:]
            s = 8 * zh
            lse_all[block, :, at : at + 256] = (stats[s : s + 1] + stats[s + 1 : s + 2]) * LOG2E
            delta_all[block, :, at : at + 256] = stats[s + 2 : s + 3] + stats[s + 3 : s + 4]
    for first, ref in ((0, kvn_ref.at[:128]), (1152, kvn_ref.at[128:])) + tuple(
        (128 + 256 * d, kv_ref.at[d]) for d in range(4)
    ):
        size = ref.shape[0]
        k = ref[:, :HD]
        k_all[first : first + size, :] = k
        v_all[first : first + size, :] = ref[:, HD:]
        kt_all[:, first : first + size] = k.astype(F32).T.astype(BF16)

    clean = iota((1, 512), 1) // 128 % 2 == 1
    for block in (1, 3, 0, 2):
        zh, other = divmod(block, 2)
        own_id = ids_ref[(y * 2 + zh) * 2 + (xh ^ other)]
        lse, delta = lse_all[block], delta_all[block]
        limits = []
        for n in range(8):
            key_id = ids_ref[2 * n + xh]
            noisy_off = jnp.where(key_id < own_id, 0.0, OFF)
            clean_off = jnp.where(key_id <= own_id, 0.0, OFF)
            limits.append(lse + jnp.where(clean, clean_off, noisy_off))
        first, last = 128, 1152
        if not other:
            own_noisy = lse + jnp.where(clean, OFF, 0.0)
            limits = limits + [own_noisy] if zh else [own_noisy] + limits
            first, last = (128, 1280) if zh else (0, 1152)
        q, g = q_all[block], g_all[block]
        scores = contract(k_all[first:last, :], q, 1, 1)
        weights = jnp.concatenate(
            [jnp.exp2(scores[128 * i : 128 * i + 128] * (SCALE * LOG2E) - row) for i, row in enumerate(limits)],
            axis=0,
        )
        dweights = contract(v_all[first:last, :], g, 1, 1)
        dscores = (weights * (dweights - delta)).astype(BF16)
        dv = contract(weights.astype(BF16), g, 1, 0)
        dk = contract(dscores, q, 1, 0)
        if block == 1:
            dk_all[first:last, :] = dk
            dv_all[first:last, :] = dv
            zeros = jnp.zeros((128, HD), F32)
            for ref in (dk_all, dv_all):
                ref[:128, :] = zeros
                ref[1152:, :] = zeros
        else:
            dk_all[first:last, :] += dk
            dv_all[first:last, :] += dv
        dq = contract(kt_all[:, first:last], dscores, 1, 0).T * SCALE
        dq_keep[other, 256 * zh : 256 * zh + 256, :] = dq[:256]
        dq_send[other, 256 * zh : 256 * zh + 256, :] = dq[256:].astype(BF16)
    for first, ref in ((0, dkvn_ref.at[:128]), (1152, dkvn_ref.at[128:])) + tuple(
        (128 + 256 * d, dkv_ref.at[d]) for d in range(4)
    ):
        size = ref.shape[0]
        ref[:, :HD] = (dk_all[first : first + size, :] * SCALE).astype(BF16)
        ref[:, HD:] = dv_all[first : first + size, :].astype(BF16)


def add_kernel(keep_ref, got_ref, out_ref):
    out_ref[...] = (keep_ref[1] + got_ref[1].astype(F32)).astype(BF16)


def unsort_kernel(keep_ref, got_core, got_chip, got_dkv, dkvn_ref, copy_ref, out_ref):
    dq = (keep_ref[0] + got_core[0].astype(F32) + got_chip[...].astype(F32)).astype(BF16)
    dkv = [got_dkv[y].astype(F32) for y in range(4)]
    dkv = (dkv[0] + dkv[1] + dkv[2] + dkv[3]).astype(BF16)
    for j in range(RUNS):
        zh, xl = divmod(j, 2)
        one_hot = placing(copy_ref, j).T.astype(BF16)
        at = 64 * xl
        queries = jnp.concatenate(
            [dq[256 * zh + at : 256 * zh + at + 64], dq[256 * zh + 128 + at : 256 * zh + 192 + at]], axis=0
        )
        keys = jnp.concatenate(
            [dkvn_ref[128 * zh + at : 128 * zh + at + 64, :], dkv[128 * zh + at : 128 * zh + at + 64]], axis=0
        )
        moved = contract(one_hot, jnp.concatenate([queries, keys], axis=1), 1, 0).astype(BF16)
        for z in range(4):
            for i in range(3):
                out_ref[4 * z + j, 32 * i : 32 * i + 32, :] = moved[32 * z : 32 * z + 32, HD * i : HD * (i + 1)]


def unpack_kernel(got_ref, dq_ref, dk_ref, dv_ref):
    rows = dq_ref.shape[0]
    for h in range(16):
        for i, ref in enumerate((dq_ref, dk_ref, dv_ref)):
            ref[:, h * HD : (h + 1) * HD] = got_ref[h, i * rows : (i + 1) * rows, :]


def swap(x, mask):
    return lax.ppermute(x, QUERY_AXES, [(i, i ^ mask) for i in range(4)])


def shape(dims, dtype=BF16):
    return jax.ShapeDtypeStruct(dims, dtype)


def per_device(query_in, key_in, value_in, saved_out, grad_out, saved_lse, row_block, row_copy):
    copies = row_copy.reshape(-1, RUN)
    ids = row_block[:: 4 * RUN]
    rows = query_in.shape[0]
    packed = call(
        pack_kernel,
        shape((16, 4 * rows + 16, HD)),
        (query_in, key_in, value_in, saved_out, grad_out, saved_lse.T),
        hbm=range(6),
        limit=62 << 20,
        scratch=[pltpu.VMEM(query_in.shape, BF16)] * 5 + [pltpu.VMEM((4, 128), F32), pltpu.SemaphoreType.DMA((6,))],
    )
    got = lax.all_to_all(packed, HEAD_AXES, 0, 0, tiled=True)
    qd, kv, kvn = call(
        sort_kernel, (shape((528, 256)), shape((4, 256, 256)), shape((256, 256))), (got, copies)
    )
    qd2 = swap(qd, 2)
    kvs = lax.all_to_all(kv, "y", 0, 0, tiled=True)
    qd1 = swap(qd, 1)
    qd3 = swap(qd2, 1)
    outs = (shape((2, 512, HD), F32), shape((2, 512, HD)), shape((4, 256, 256)), shape((256, 256)))
    scratch = (
        pltpu.VMEM((4, 512, HD), BF16), pltpu.VMEM((4, 512, HD), BF16),
        pltpu.VMEM((4, 1, 512), F32), pltpu.VMEM((4, 1, 512), F32),
        pltpu.VMEM((1280, HD), BF16), pltpu.VMEM((HD, 1280), BF16), pltpu.VMEM((1280, HD), BF16),
        pltpu.VMEM((1280, HD), F32), pltpu.VMEM((1280, HD), F32),
    )
    dq_keep, dq_send, dkv, dkvn = call(
        attend_kernel, outs, (ids, qd, qd1, qd2, qd3, kvs, kvn), smem=(0,), scratch=scratch
    )
    dq_core = swap(dq_send, 1)
    dkvs = lax.all_to_all(dkv, "y", 0, 0, tiled=True)
    dq_chip = swap(call(add_kernel, shape((512, HD)), (dq_keep, dq_core)), 2)
    back = call(unsort_kernel, shape((16, 3 * rows, HD)), (dq_keep, dq_core, dq_chip, dkvs, dkvn, copies))
    back = lax.all_to_all(back, HEAD_AXES, 0, 0, tiled=True)
    return call(unpack_kernel, (shape((rows, 16 * HD)),) * 3, (back,))


def solution(mesh):
    fine = Mesh(mesh.devices.reshape(SIZES), AXES)
    whole = P(AXES, None)
    return jax.shard_map(
        per_device,
        mesh=fine,
        in_specs=(whole, whole, whole, whole, whole, P(AXES[:5], AXES[5]), P(), P()),
        out_specs=(whole, whole, whole),
        check_vma=False,
    )
```

profile of v0, /device:TPU:1, one launch (start us, length us, event | category | flops | bytes accessed | tf_op | source)
XLA Modules:
  0.0 88.1 jit_solution(866446599778746755)
XLA Ops:
  0.6 2.1 %shard_map.103 = bf16[16,144,128]{2,1,0:T(8,128)(2,1)} custom-call(bf16[32,2048]{1,0:T(8,128)(2,1)} %q_in.1, bf16[32,2048]{1,0:T(8,128)(2,1)} %k_in.1, bf16[32,2048]{1,0:T(8,128)(2,1)} %v_in.1, bf16[32,2048]{1,0:T(8,128)(2,1)} %o_in.1, bf16[32,2048]{1,0:T(8,128)(2,1)} %g_in.1, f32[4,128]{1,0:T(4,128)} %bitcast.4), custom_call_target="tpu_custom_call" | custom-call | tf_op jit(solution)/shard_map/pallas_call | solution.py:41
  2.8 0.0 copy-start
  2.8 27.7 %all_to_all.20.got_ref = bf16[16,144,128]{2,1,0:T(8,128)(2,1)S(1)} all-to-all(bf16[16,144,128]{2,1,0:T(8,128)(2,1)} %shard_map.103), channel_id=1, replica_groups=mesh['y'=4,'zh'=2,'xh'=2,'xl'=2,'c'=2,'zl'=4] {'zl','zh','xl'}, dimensions={0} | all-to-all | bytes 1179648 | tf_op jit(solution)/shard_map/all_to_all | solution.py:250
  30.5 0.0 copy-done
  30.5 1.6 %shard_map.104 = (bf16[528,256]{1,0:T(8,128)(2,1)S(1)}, bf16[4,256,256]{2,1,0:T(8,128)(2,1)}, bf16[256,256]{1,0:T(8,128)(2,1)S(1)}) custom-call(bf16[16,144,128]{2,1,0:T(8,128)(2,1)S(1)} %all_to_all.20.got_ref, s32[64,128]{1,0:T(8,128)S(1)} %bitcast.2), custom_call_target="tpu_custom_call" | custom-call | tf_op jit(solution)/shard_map/pallas_call | solution.py:41
  32.1 2.4 %collective-permute-start.1 = (bf16[528,256]{1,0:T(8,128)(2,1)S(1)}, bf16[528,256]{1,0:T(8,128)(2,1)S(1)}, u32[]{:S(2)}, u32[]{:S(2)}) collective-permute-start(bf16[528,256]{1,0:T(8,128)(2,1)S(1)} %get-tuple-element.10.qd0), channel_id=1, source_target_pairs={{0,16},{4,20},{16,0},{20,4},{1,17},{5,21},{17,1},{21,5},{2,18},{6,... | collective-permute-start | bytes 811016 | tf_op jit(solution)/shard_map/ppermute | solution.py:231
  34.5 4.2 %all-to-all-start.1 = ((bf16[4,256,256]{2,1,0:T(8,128)(2,1)}), bf16[4,256,256]{2,1,0:T(8,128)(2,1)S(1)}, u32[]{:S(2)}, u32[]{:S(2)}) async-start(bf16[4,256,256]{2,1,0:T(8,128)(2,1)} %get-tuple-element.11), calls=%async_computation.1 | async-start | bytes 1048576 | tf_op jit(solution)/shard_map/all_to_all | solution.py:255
  38.7 3.5 %collective-permute-start = (bf16[528,256]{1,0:T(8,128)(2,1)S(1)}, bf16[528,256]{1,0:T(8,128)(2,1)S(1)}, u32[]{:S(2)}, u32[]{:S(2)}) collective-permute-start(bf16[528,256]{1,0:T(8,128)(2,1)S(1)} %get-tuple-element.10.qd0), channel_id=1, source_target_pairs={{0,4},{4,0},{16,20},{20,16},{1,5},{5,1},{17,21},{21,17},{2,6},{6,2... | collective-permute-start | bytes 811016 | tf_op jit(solution)/shard_map/ppermute | solution.py:231
  42.2 0.0 collective-permute-done.1.qd2
  42.2 0.8 collective-permute-start.2
  43.0 0.8 slice.3.ids_ref
  43.8 0.0 collective-permute-done.qd1
  43.8 1.8 %all-to-all-done.1.kv_ref = bf16[4,256,256]{2,1,0:T(8,128)(2,1)S(1)} async-done(((bf16[4,256,256]{2,1,0:T(8,128)(2,1)}), bf16[4,256,256]{2,1,0:T(8,128)(2,1)S(1)}, u32[]{:S(2)}, u32[]{:S(2)}) %all-to-all-start.1) | async-done | bytes 524320 | tf_op jit(solution)/shard_map/all_to_all | solution.py:255
  45.6 0.0 collective-permute-done.2.qd3
  45.6 6.7 %shard_map.105 = (f32[2,512,128]{2,1,0:T(8,128)S(1)}, bf16[2,512,128]{2,1,0:T(8,128)(2,1)S(1)}, bf16[4,256,256]{2,1,0:T(8,128)(2,1)}, bf16[256,256]{1,0:T(8,128)(2,1)S(1)}) custom-call(s32[16]{0:T(128)S(1)} %slice.3.ids_ref, bf16[528,256]{1,0:T(8,128)(2,1)S(1)} %get-tuple-element.10.qd0, bf16[528,256]{1,0:T(8,128)(2,1)S(1)} %collective-permute-done.qd1, ...), custom_call_target="tpu_custom_call" | custom-call | tf_op jit(solution)/shard_map/pallas_call | solution.py:41
  52.3 4.7 %collective-permute-start.3 = (bf16[2,512,128]{2,1,0:T(8,128)(2,1)S(1)}, bf16[2,512,128]{2,1,0:T(8,128)(2,1)S(1)}, u32[]{:S(2)}, u32[]{:S(2)}) collective-permute-start(bf16[2,512,128]{2,1,0:T(8,128)(2,1)S(1)} %get-tuple-element.14), channel_id=1, source_target_pairs={{0,4},{4,0},{16,20},{20,16},{1,5},{5,1},{17,21},{21,17},{2,6},{6,2... | collective-permute-start | bytes 786440 | tf_op jit(solution)/shard_map/ppermute | solution.py:231
  57.0 3.5 %all-to-all-start.2 = ((bf16[4,256,256]{2,1,0:T(8,128)(2,1)}), bf16[4,256,256]{2,1,0:T(8,128)(2,1)S(1)}, u32[]{:S(2)}, u32[]{:S(2)}) async-start(bf16[4,256,256]{2,1,0:T(8,128)(2,1)} %get-tuple-element.15), calls=%async_computation.2 | async-start | bytes 1048576 | tf_op jit(solution)/shard_map/all_to_all | solution.py:269
  60.5 0.0 collective-permute-done.3.got_ref.got_core
  60.5 0.6 collective-permute-start.4
  61.1 9.0 %all-to-all-done.2.got_dkv = bf16[4,256,256]{2,1,0:T(8,128)(2,1)S(1)} async-done(((bf16[4,256,256]{2,1,0:T(8,128)(2,1)}), bf16[4,256,256]{2,1,0:T(8,128)(2,1)S(1)}, u32[]{:S(2)}, u32[]{:S(2)}) %all-to-all-start.2) | async-done | bytes 524320 | tf_op jit(solution)/shard_map/all_to_all | solution.py:269
  70.1 0.0 collective-permute-done.4.got_chip
  70.1 1.1 %shard_map.107 = bf16[16,96,128]{2,1,0:T(8,128)(2,1)S(1)} custom-call(f32[2,512,128]{2,1,0:T(8,128)S(1)} %get-tuple-element.13.keep_ref, bf16[2,512,128]{2,1,0:T(8,128)(2,1)S(1)} %collective-permute-done.3.got_ref.got_core, bf16[512,128]{1,0:T(8,128)(2,1)S(1)} %collective-permute-done.4.got_chip, bf16[4,256,256]{2,1,0:T(8,128)(2,1)S(1)} %all-to-all-done.2.got_dkv, ...), custom_call_target="tpu_custom_call" | custom-call | tf_op jit(solution)/shard_map/pallas_call | solution.py:41
  71.2 16.1 %all_to_all.21.got_ref = bf16[16,96,128]{2,1,0:T(8,128)(2,1)S(1)} all-to-all(bf16[16,96,128]{2,1,0:T(8,128)(2,1)S(1)} %shard_map.107), channel_id=1, replica_groups=mesh['y'=4,'zh'=2,'xh'=2,'xl'=2,'c'=2,'zl'=4] {'zl','zh','xl'}, dimensions={0} | all-to-all | bytes 786432 | tf_op jit(solution)/shard_map/all_to_all | solution.py:272
  87.3 0.8 shard_map.108
  (1 shorter events, 0.0 us)
Async XLA Ops:
  2.8 27.7 %copy-start = (s32[8192]{0:T(1024)S(1)}, s32[8192]{0:T(1024)}, u32[]{:S(2)}) copy-start(s32[8192]{0:T(1024)} %param.15) | copy-start | bytes 98308
  32.1 10.2 %collective-permute-start.1 = (bf16[528,256]{1,0:T(8,128)(2,1)S(1)}, bf16[528,256]{1,0:T(8,128)(2,1)S(1)}, u32[]{:S(2)}, u32[]{:S(2)}) collective-permute-start(bf16[528,256]{1,0:T(8,128)(2,1)S(1)} %get-tuple-element.10.qd0), channel_id=1, source_target_pairs={{0,16},{4,20},{16,0},{20,4},{1,17},{5,21},{17,1},{21,5},{2,18},{6,... | collective-permute-start | bytes 811016 | tf_op jit(solution)/shard_map/ppermute | solution.py:231
  34.5 11.1 %all-to-all-start.1 = ((bf16[4,256,256]{2,1,0:T(8,128)(2,1)}), bf16[4,256,256]{2,1,0:T(8,128)(2,1)S(1)}, u32[]{:S(2)}, u32[]{:S(2)}) async-start(bf16[4,256,256]{2,1,0:T(8,128)(2,1)} %get-tuple-element.11), calls=%async_computation.1 | async-start | bytes 1048576 | tf_op jit(solution)/shard_map/all_to_all | solution.py:255
  38.7 5.1 %collective-permute-start = (bf16[528,256]{1,0:T(8,128)(2,1)S(1)}, bf16[528,256]{1,0:T(8,128)(2,1)S(1)}, u32[]{:S(2)}, u32[]{:S(2)}) collective-permute-start(bf16[528,256]{1,0:T(8,128)(2,1)S(1)} %get-tuple-element.10.qd0), channel_id=1, source_target_pairs={{0,4},{4,0},{16,20},{20,16},{1,5},{5,1},{17,21},{21,17},{2,6},{6,2... | collective-permute-start | bytes 811016 | tf_op jit(solution)/shard_map/ppermute | solution.py:231
  42.2 3.4 %collective-permute-start.2 = (bf16[528,256]{1,0:T(8,128)(2,1)S(1)}, bf16[528,256]{1,0:T(8,128)(2,1)S(1)}, u32[]{:S(2)}, u32[]{:S(2)}) collective-permute-start(bf16[528,256]{1,0:T(8,128)(2,1)S(1)} %collective-permute-done.1.qd2), channel_id=1, source_target_pairs={{0,4},{4,0},{16,20},{20,16},{1,5},{5,1},{17,21},{21,17},{2,6},{6,2... | collective-permute-start | bytes 811016 | tf_op jit(solution)/shard_map/ppermute | solution.py:231
  52.3 8.1 %collective-permute-start.3 = (bf16[2,512,128]{2,1,0:T(8,128)(2,1)S(1)}, bf16[2,512,128]{2,1,0:T(8,128)(2,1)S(1)}, u32[]{:S(2)}, u32[]{:S(2)}) collective-permute-start(bf16[2,512,128]{2,1,0:T(8,128)(2,1)S(1)} %get-tuple-element.14), channel_id=1, source_target_pairs={{0,4},{4,0},{16,20},{20,16},{1,5},{5,1},{17,21},{21,17},{2,6},{6,2... | collective-permute-start | bytes 786440 | tf_op jit(solution)/shard_map/ppermute | solution.py:231
  57.0 13.1 %all-to-all-start.2 = ((bf16[4,256,256]{2,1,0:T(8,128)(2,1)}), bf16[4,256,256]{2,1,0:T(8,128)(2,1)S(1)}, u32[]{:S(2)}, u32[]{:S(2)}) async-start(bf16[4,256,256]{2,1,0:T(8,128)(2,1)} %get-tuple-element.15), calls=%async_computation.2 | async-start | bytes 1048576 | tf_op jit(solution)/shard_map/all_to_all | solution.py:269
  60.5 9.6 %collective-permute-start.4 = (bf16[512,128]{1,0:T(8,128)(2,1)S(1)}, bf16[512,128]{1,0:T(8,128)(2,1)S(1)}, u32[]{:S(2)}, u32[]{:S(2)}) collective-permute-start(bf16[512,128]{1,0:T(8,128)(2,1)S(1)} %shard_map.106), channel_id=1, source_target_pairs={{0,16},{4,20},{16,0},{20,4},{1,17},{5,21},{17,1},{21,5},{2,18},{6,... | collective-permute-start | bytes 393224 | tf_op jit(solution)/shard_map/ppermute | solution.py:231
where the time goes:
time: 88.6 us; the launch traced here: 88.1 us
  blocking collectives  43.8 us (49%)
  starting transfers between devices  19.7 us (22%)
  Pallas kernels  12.4 us (14%)
  waiting for transfers between devices  10.8 us (12%)
    all_to_all x1, blocking collectives, per_device(): got = lax.all_to_all(packed, HEAD_AXES, 0, 0, tiled=True)  27.7 us
    all_to_all x1, blocking collectives, per_device(): back = lax.all_to_all(back, HEAD_AXES, 0, 0, tiled=True)  16.1 us
    pallas_call x6, Pallas kernels, call(): pl.pallas_call(body, out_shape=out_shape, in_specs=[SMEM if i in smem els...  12.4 us
    ppermute x5, starting transfers between devices, swap(): return lax.ppermute(x, QUERY_AXES, [(i, i ^ mask) for i in range(4)])  12 us
    all_to_all x1, waiting for transfers between devices, per_device(): dkvs = lax.all_to_all(dkv, 'y', 0, 0, tiled=True)  8.95 us
    all_to_all x1, starting transfers between devices, per_device(): kvs = lax.all_to_all(kv, 'y', 0, 0, tiled=True)  4.19 us
    all_to_all x1, starting transfers between devices, per_device(): dkvs = lax.all_to_all(dkv, 'y', 0, 0, tiled=True)  3.47 us
    all_to_all x1, waiting for transfers between devices, per_device(): kvs = lax.all_to_all(kv, 'y', 0, 0, tiled=True)  1.79 us
  transfers between devices with their start and end apart: 7, of which 2 were waited for; matrix products, arithmetic and copies ran while one was open for 1% of the time, Pallas kernels for 0%

commit v1 on v0

--- a/solution.py
+++ b/solution.py
@@ -127,7 +127,7 @@
 
 def attend_kernel(
     ids_ref, qd0, qd1, qd2, qd3, kv_ref, kvn_ref,
-    dq_keep, dq_send, dkv_ref, dkvn_ref,
+    dq_keep, dq_send, dkv0, dkv1, dkv2, dkv3, dkvn_ref,
     q_all, g_all, lse_all, delta_all, k_all, kt_all, v_all, dk_all, dv_all,
 ):
     y, xh = lax.axis_index("y"), lax.axis_index("xh")
@@ -188,22 +188,22 @@
         dq = contract(kt_all[:, first:last], dscores, 1, 0).T * SCALE
         dq_keep[other, 256 * zh : 256 * zh + 256, :] = dq[:256]
         dq_send[other, 256 * zh : 256 * zh + 256, :] = dq[256:].astype(BF16)
-    for first, ref in ((0, dkvn_ref.at[:128]), (1152, dkvn_ref.at[128:])) + tuple(
-        (128 + 256 * d, dkv_ref.at[d]) for d in range(4)
-    ):
-        size = ref.shape[0]
-        ref[:, :HD] = (dk_all[first : first + size, :] * SCALE).astype(BF16)
-        ref[:, HD:] = dv_all[first : first + size, :].astype(BF16)
+    pieces = [(0, dkvn_ref.at[:128]), (1152, dkvn_ref.at[128:])]
+    for m, ref in enumerate((dkv0, dkv1, dkv2, dkv3)):
+        pieces.append((pl.multiple_of(128 + 256 * (y ^ m), 128), ref))
+    for first, ref in pieces:
+        rows = pl.ds(first, ref.shape[0])
+        ref[:, :HD] = (dk_all[rows, :] * SCALE).astype(ref.dtype)
+        ref[:, HD:] = dv_all[rows, :].astype(ref.dtype)
 
 
 def add_kernel(keep_ref, got_ref, out_ref):
     out_ref[...] = (keep_ref[1] + got_ref[1].astype(F32)).astype(BF16)
 
 
-def unsort_kernel(keep_ref, got_core, got_chip, got_dkv, dkvn_ref, copy_ref, out_ref):
+def unsort_kernel(keep_ref, got_core, got_chip, dkv0, dkv1, dkv2, dkv3, dkvn_ref, copy_ref, out_ref):
     dq = (keep_ref[0] + got_core[0].astype(F32) + got_chip[...].astype(F32)).astype(BF16)
-    dkv = [got_dkv[y].astype(F32) for y in range(4)]
-    dkv = (dkv[0] + dkv[1] + dkv[2] + dkv[3]).astype(BF16)
+    dkv = (dkv0[...] + dkv1[...].astype(F32) + dkv2[...].astype(F32) + dkv3[...].astype(F32)).astype(BF16)
     for j in range(RUNS):
         zh, xl = divmod(j, 2)
         one_hot = placing(copy_ref, j).T.astype(BF16)
@@ -229,6 +229,10 @@
 
 def swap(x, mask):
     return lax.ppermute(x, QUERY_AXES, [(i, i ^ mask) for i in range(4)])
+
+
+def swap_y(x, mask):
+    return lax.ppermute(x, "y", [(i, i ^ mask) for i in range(4)])
 
 
 def shape(dims, dtype=BF16):
@@ -255,20 +259,23 @@
     kvs = lax.all_to_all(kv, "y", 0, 0, tiled=True)
     qd1 = swap(qd, 1)
     qd3 = swap(qd2, 1)
-    outs = (shape((2, 512, HD), F32), shape((2, 512, HD)), shape((4, 256, 256)), shape((256, 256)))
+    outs = (
+        (shape((2, 512, HD), F32), shape((2, 512, HD)), shape((256, 256), F32)) + (shape((256, 256)),) * 4
+    )
     scratch = (
         pltpu.VMEM((4, 512, HD), BF16), pltpu.VMEM((4, 512, HD), BF16),
         pltpu.VMEM((4, 1, 512), F32), pltpu.VMEM((4, 1, 512), F32),
         pltpu.VMEM((1280, HD), BF16), pltpu.VMEM((HD, 1280), BF16), pltpu.VMEM((1280, HD), BF16),
         pltpu.VMEM((1280, HD), F32), pltpu.VMEM((1280, HD), F32),
     )
-    dq_keep, dq_send, dkv, dkvn = call(
+    dq_keep, dq_send, *dkvs, dkvn = call(
         attend_kernel, outs, (ids, qd, qd1, qd2, qd3, kvs, kvn), smem=(0,), scratch=scratch
     )
     dq_core = swap(dq_send, 1)
-    dkvs = lax.all_to_all(dkv, "y", 0, 0, tiled=True)
+    for m in (2, 1, 3):
+        dkvs[m] = swap_y(dkvs[m], m)
     dq_chip = swap(call(add_kernel, shape((512, HD)), (dq_keep, dq_core)), 2)
-    back = call(unsort_kernel, shape((16, 3 * rows, HD)), (dq_keep, dq_core, dq_chip, dkvs, dkvn, copies))
+    back = call(unsort_kernel, shape((16, 3 * rows, HD)), (dq_keep, dq_core, dq_chip, *dkvs, dkvn, copies))
     back = lax.all_to_all(back, HEAD_AXES, 0, 0, tiled=True)
     return call(unpack_kernel, (shape((rows, 16 * HD)),) * 3, (back,))
 

time: 88.6 us -> 86.2 us (0.973)
  waiting for transfers between devices: 10.8 us -> 8.33 us
    all_to_all x1 -> x0, waiting for transfers between devices: 8.95 us -> none  [per_device(): dkvs = lax.all_to_all(dkv, 'y', 0, 0, tiled=True)]
    ppermute x0 -> x3, waiting for transfers between devices: none -> 6.53 us  [swap_y(): return lax.ppermute(x, 'y', [(i, i ^ mask) for i in range(4)])]
    ppermute x0 -> x3, starting transfers between devices: none -> 3.88 us  [swap_y(): return lax.ppermute(x, 'y', [(i, i ^ mask) for i in range(4)])]
    all_to_all x1 -> x0, starting transfers between devices: 3.47 us -> none  [per_device(): dkvs = lax.all_to_all(dkv, 'y', 0, 0, tiled=True)]
  transfers between devices with their start and end apart: 7 -> 9, of which waited for: 2 -> 4; matrix products, arithmetic and copies ran while one was open for 1% -> 1% of each run, Pallas kernels for 0% -> 0%
where the time goes in v1:
time: 86.2 us; the launch traced here: 85.8 us
  blocking collectives  43.8 us (51%)
  starting transfers between devices  20.1 us (23%)
  Pallas kernels  12 us (14%)
  waiting for transfers between devices  8.33 us (10%)
    all_to_all x1, blocking collectives, per_device(): got = lax.all_to_all(packed, HEAD_AXES, 0, 0, tiled=True)  27.7 us
    all_to_all x1, blocking collectives, per_device(): back = lax.all_to_all(back, HEAD_AXES, 0, 0, tiled=True)  16.1 us
    ppermute x5, starting transfers between devices, swap(): return lax.ppermute(x, QUERY_AXES, [(i, i ^ mask) for i in range(4)])  12.1 us
    pallas_call x6, Pallas kernels, call(): pl.pallas_call(body, out_shape=out_shape, in_specs=[SMEM if i in smem els...  12 us
    ppermute x3, waiting for transfers between devices, swap_y(): return lax.ppermute(x, 'y', [(i, i ^ mask) for i in range(4)])  6.53 us
    all_to_all x1, starting transfers between devices, per_device(): kvs = lax.all_to_all(kv, 'y', 0, 0, tiled=True)  4.19 us
    ppermute x3, starting transfers between devices, swap_y(): return lax.ppermute(x, 'y', [(i, i ^ mask) for i in range(4)])  3.88 us
    all_to_all x1, waiting for transfers between devices, per_device(): kvs = lax.all_to_all(kv, 'y', 0, 0, tiled=True)  1.79 us
  transfers between devices with their start and end apart: 9, of which 4 were waited for; matrix products, arithmetic and copies ran while one was open for 1% of the time, Pallas kernels for 0%

profile of v1, /device:TPU:1, one launch (start us, length us, event | category | flops | bytes accessed | tf_op | source)
XLA Modules:
  0.0 85.8 jit_solution(7765121300269488884)
XLA Ops:
  0.6 2.2 %shard_map.103 = bf16[16,144,128]{2,1,0:T(8,128)(2,1)} custom-call(bf16[32,2048]{1,0:T(8,128)(2,1)} %q_in.1, bf16[32,2048]{1,0:T(8,128)(2,1)} %k_in.1, bf16[32,2048]{1,0:T(8,128)(2,1)} %v_in.1, bf16[32,2048]{1,0:T(8,128)(2,1)} %o_in.1, bf16[32,2048]{1,0:T(8,128)(2,1)} %g_in.1, f32[4,128]{1,0:T(4,128)} %bitcast.4), custom_call_target="tpu_custom_call" | custom-call | tf_op jit(solution)/shard_map/pallas_call | solution.py:41
  2.8 0.0 copy-start
  2.8 27.7 %all_to_all.15.got_ref = bf16[16,144,128]{2,1,0:T(8,128)(2,1)S(1)} all-to-all(bf16[16,144,128]{2,1,0:T(8,128)(2,1)} %shard_map.103), channel_id=1, replica_groups=mesh['y'=4,'zh'=2,'xh'=2,'xl'=2,'c'=2,'zl'=4] {'zl','zh','xl'}, dimensions={0} | all-to-all | bytes 1179648 | tf_op jit(solution)/shard_map/all_to_all | solution.py:254
  30.5 0.0 copy-done
  30.5 1.6 %shard_map.104 = (bf16[528,256]{1,0:T(8,128)(2,1)S(1)}, bf16[4,256,256]{2,1,0:T(8,128)(2,1)}, bf16[256,256]{1,0:T(8,128)(2,1)S(1)}) custom-call(bf16[16,144,128]{2,1,0:T(8,128)(2,1)S(1)} %all_to_all.15.got_ref, s32[64,128]{1,0:T(8,128)S(1)} %bitcast.2), custom_call_target="tpu_custom_call" | custom-call | tf_op jit(solution)/shard_map/pallas_call | solution.py:41
  32.1 2.4 %collective-permute-start.1 = (bf16[528,256]{1,0:T(8,128)(2,1)S(1)}, bf16[528,256]{1,0:T(8,128)(2,1)S(1)}, u32[]{:S(2)}, u32[]{:S(2)}) collective-permute-start(bf16[528,256]{1,0:T(8,128)(2,1)S(1)} %get-tuple-element.13.qd0), channel_id=1, source_target_pairs={{0,16},{4,20},{16,0},{20,4},{1,17},{5,21},{17,1},{21,5},{2,18},{6,... | collective-permute-start | bytes 811016 | tf_op jit(solution)/shard_map/ppermute | solution.py:231
  34.5 4.2 %all-to-all-start.1 = ((bf16[4,256,256]{2,1,0:T(8,128)(2,1)}), bf16[4,256,256]{2,1,0:T(8,128)(2,1)S(1)}, u32[]{:S(2)}, u32[]{:S(2)}) async-start(bf16[4,256,256]{2,1,0:T(8,128)(2,1)} %get-tuple-element.14), calls=%async_computation.1 | async-start | bytes 1048576 | tf_op jit(solution)/shard_map/all_to_all | solution.py:259
  38.7 3.5 %collective-permute-start = (bf16[528,256]{1,0:T(8,128)(2,1)S(1)}, bf16[528,256]{1,0:T(8,128)(2,1)S(1)}, u32[]{:S(2)}, u32[]{:S(2)}) collective-permute-start(bf16[528,256]{1,0:T(8,128)(2,1)S(1)} %get-tuple-element.13.qd0), channel_id=1, source_target_pairs={{0,4},{4,0},{16,20},{20,16},{1,5},{5,1},{17,21},{21,17},{2,6},{6,2... | collective-permute-start | bytes 811016 | tf_op jit(solution)/shard_map/ppermute | solution.py:231
  42.2 0.0 collective-permute-done.1.qd2
  42.2 0.8 collective-permute-start.2
  43.0 0.8 slice.3.ids_ref
  43.9 0.0 collective-permute-done.qd1
  43.9 1.8 %all-to-all-done.1.kv_ref = bf16[4,256,256]{2,1,0:T(8,128)(2,1)S(1)} async-done(((bf16[4,256,256]{2,1,0:T(8,128)(2,1)}), bf16[4,256,256]{2,1,0:T(8,128)(2,1)S(1)}, u32[]{:S(2)}, u32[]{:S(2)}) %all-to-all-start.1) | async-done | bytes 524320 | tf_op jit(solution)/shard_map/all_to_all | solution.py:259
  45.7 0.0 collective-permute-done.2.qd3
  45.7 6.3 %shard_map.105 = (f32[2,512,128]{2,1,0:T(8,128)S(1)}, bf16[2,512,128]{2,1,0:T(8,128)(2,1)S(1)}, f32[256,256]{1,0:T(8,128)S(1)}, bf16[256,256]{1,0:T(8,128)(2,1)S...) custom-call(s32[16]{0:T(128)S(1)} %slice.3.ids_ref, ...), custom_call_target="tpu_custom_call" | custom-call | tf_op jit(solution)/shard_map/pallas_call | solution.py:41
  52.0 4.8 %collective-permute-start.3 = (bf16[2,512,128]{2,1,0:T(8,128)(2,1)S(1)}, bf16[2,512,128]{2,1,0:T(8,128)(2,1)S(1)}, u32[]{:S(2)}, u32[]{:S(2)}) collective-permute-start(bf16[2,512,128]{2,1,0:T(8,128)(2,1)S(1)} %get-tuple-element.17), channel_id=1, source_target_pairs={{0,4},{4,0},{16,20},{20,16},{1,5},{5,1},{17,21},{21,17},{2,6},{6,2... | collective-permute-start | bytes 786440 | tf_op jit(solution)/shard_map/ppermute | solution.py:231
  56.7 0.3 collective-permute-start.5
  57.0 1.8 %collective-permute-start.6 = (bf16[256,256]{1,0:T(8,128)(2,1)S(1)}, bf16[256,256]{1,0:T(8,128)(2,1)S(1)}, u32[]{:S(2)}, u32[]{:S(2)}) collective-permute-start(bf16[256,256]{1,0:T(8,128)(2,1)S(1)} %get-tuple-element.20), channel_id=1, source_target_pairs={{0,128},{64,192},{128,0},{192,64},{1,129},{65,193},{129,1},{193,65... | collective-permute-start | bytes 393224 | tf_op jit(solution)/shard_map/ppermute | solution.py:235
  58.8 1.8 %collective-permute-start.7 = (bf16[256,256]{1,0:T(8,128)(2,1)S(1)}, bf16[256,256]{1,0:T(8,128)(2,1)S(1)}, u32[]{:S(2)}, u32[]{:S(2)}) collective-permute-start(bf16[256,256]{1,0:T(8,128)(2,1)S(1)} %get-tuple-element.21), channel_id=1, source_target_pairs={{0,192},{64,128},{128,64},{192,0},{1,193},{65,129},{129,65},{193,1... | collective-permute-start | bytes 393224 | tf_op jit(solution)/shard_map/ppermute | solution.py:235
  60.6 0.0 collective-permute-done.3.got_ref.got_core
  60.6 0.6 collective-permute-start.4
  61.3 0.5 collective-permute-done.5.dkv1
  61.8 3.5 %collective-permute-done.6.dkv2 = bf16[256,256]{1,0:T(8,128)(2,1)S(1)} collective-permute-done((bf16[256,256]{1,0:T(8,128)(2,1)S(1)}, bf16[256,256]{1,0:T(8,128)(2,1)S(1)}, u32[]{:S(2)}, u32[]{:S(2)}) %collective-permute-start.6) | collective-permute-done | bytes 131104 | tf_op jit(solution)/shard_map/ppermute | solution.py:235
  65.3 2.5 %collective-permute-done.7.dkv3 = bf16[256,256]{1,0:T(8,128)(2,1)S(1)} collective-permute-done((bf16[256,256]{1,0:T(8,128)(2,1)S(1)}, bf16[256,256]{1,0:T(8,128)(2,1)S(1)}, u32[]{:S(2)}, u32[]{:S(2)}) %collective-permute-start.7) | collective-permute-done | bytes 131104 | tf_op jit(solution)/shard_map/ppermute | solution.py:235
  67.8 0.0 collective-permute-done.4.got_chip
  67.8 1.1 %shard_map.107 = bf16[16,96,128]{2,1,0:T(8,128)(2,1)S(1)} custom-call(f32[2,512,128]{2,1,0:T(8,128)S(1)} %get-tuple-element.16.keep_ref, bf16[2,512,128]{2,1,0:T(8,128)(2,1)S(1)} %collective-permute-done.3.got_ref.got_core, bf16[512,128]{1,0:T(8,128)(2,1)S(1)} %collective-permute-done.4.got_chip, f32[256,256]{1,0:T(8,128)S(1)} %get-tuple-element.18.dkv0, ...), custom_call_target="tpu_custom_call" | custom-call | tf_op jit(solution)/shard_map/pallas_call | solution.py:41
  68.9 16.1 %all_to_all.16.got_ref = bf16[16,96,128]{2,1,0:T(8,128)(2,1)S(1)} all-to-all(bf16[16,96,128]{2,1,0:T(8,128)(2,1)S(1)} %shard_map.107), channel_id=1, replica_groups=mesh['y'=4,'zh'=2,'xh'=2,'xl'=2,'c'=2,'zl'=4] {'zl','zh','xl'}, dimensions={0} | all-to-all | bytes 786432 | tf_op jit(solution)/shard_map/all_to_all | solution.py:279
  85.0 0.8 shard_map.108
  (1 shorter events, 0.0 us)
Async XLA Ops:
  2.8 27.7 %copy-start = (s32[8192]{0:T(1024)S(1)}, s32[8192]{0:T(1024)}, u32[]{:S(2)}) copy-start(s32[8192]{0:T(1024)} %param.15) | copy-start | bytes 98308
  32.1 10.2 %collective-permute-start.1 = (bf16[528,256]{1,0:T(8,128)(2,1)S(1)}, bf16[528,256]{1,0:T(8,128)(2,1)S(1)}, u32[]{:S(2)}, u32[]{:S(2)}) collective-permute-start(bf16[528,256]{1,0:T(8,128)(2,1)S(1)} %get-tuple-element.13.qd0), channel_id=1, source_target_pairs={{0,16},{4,20},{16,0},{20,4},{1,17},{5,21},{17,1},{21,5},{2,18},{6,... | collective-permute-start | bytes 811016 | tf_op jit(solution)/shard_map/ppermute | solution.py:231
  34.5 11.1 %all-to-all-start.1 = ((bf16[4,256,256]{2,1,0:T(8,128)(2,1)}), bf16[4,256,256]{2,1,0:T(8,128)(2,1)S(1)}, u32[]{:S(2)}, u32[]{:S(2)}) async-start(bf16[4,256,256]{2,1,0:T(8,128)(2,1)} %get-tuple-element.14), calls=%async_computation.1 | async-start | bytes 1048576 | tf_op jit(solution)/shard_map/all_to_all | solution.py:259
  38.7 5.1 %collective-permute-start = (bf16[528,256]{1,0:T(8,128)(2,1)S(1)}, bf16[528,256]{1,0:T(8,128)(2,1)S(1)}, u32[]{:S(2)}, u32[]{:S(2)}) collective-permute-start(bf16[528,256]{1,0:T(8,128)(2,1)S(1)} %get-tuple-element.13.qd0), channel_id=1, source_target_pairs={{0,4},{4,0},{16,20},{20,16},{1,5},{5,1},{17,21},{21,17},{2,6},{6,2... | collective-permute-start | bytes 811016 | tf_op jit(solution)/shard_map/ppermute | solution.py:231
  42.2 3.4 %collective-permute-start.2 = (bf16[528,256]{1,0:T(8,128)(2,1)S(1)}, bf16[528,256]{1,0:T(8,128)(2,1)S(1)}, u32[]{:S(2)}, u32[]{:S(2)}) collective-permute-start(bf16[528,256]{1,0:T(8,128)(2,1)S(1)} %collective-permute-done.1.qd2), channel_id=1, source_target_pairs={{0,4},{4,0},{16,20},{20,16},{1,5},{5,1},{17,21},{21,17},{2,6},{6,2... | collective-permute-start | bytes 811016 | tf_op jit(solution)/shard_map/ppermute | solution.py:231
  52.0 8.6 %collective-permute-start.3 = (bf16[2,512,128]{2,1,0:T(8,128)(2,1)S(1)}, bf16[2,512,128]{2,1,0:T(8,128)(2,1)S(1)}, u32[]{:S(2)}, u32[]{:S(2)}) collective-permute-start(bf16[2,512,128]{2,1,0:T(8,128)(2,1)S(1)} %get-tuple-element.17), channel_id=1, source_target_pairs={{0,4},{4,0},{16,20},{20,16},{1,5},{5,1},{17,21},{21,17},{2,6},{6,2... | collective-permute-start | bytes 786440 | tf_op jit(solution)/shard_map/ppermute | solution.py:231
  56.7 5.1 %collective-permute-start.5 = (bf16[256,256]{1,0:T(8,128)(2,1)S(1)}, bf16[256,256]{1,0:T(8,128)(2,1)S(1)}, u32[]{:S(2)}, u32[]{:S(2)}) collective-permute-start(bf16[256,256]{1,0:T(8,128)(2,1)S(1)} %get-tuple-element.19), channel_id=1, source_target_pairs={{0,64},{64,0},{128,192},{192,128},{1,65},{65,1},{129,193},{193,129... | collective-permute-start | bytes 393224 | tf_op jit(solution)/shard_map/ppermute | solution.py:235
  57.0 8.2 %collective-permute-start.6 = (bf16[256,256]{1,0:T(8,128)(2,1)S(1)}, bf16[256,256]{1,0:T(8,128)(2,1)S(1)}, u32[]{:S(2)}, u32[]{:S(2)}) collective-permute-start(bf16[256,256]{1,0:T(8,128)(2,1)S(1)} %get-tuple-element.20), channel_id=1, source_target_pairs={{0,128},{64,192},{128,0},{192,64},{1,129},{65,193},{129,1},{193,65... | collective-permute-start | bytes 393224 | tf_op jit(solution)/shard_map/ppermute | solution.py:235
  58.8 9.0 %collective-permute-start.7 = (bf16[256,256]{1,0:T(8,128)(2,1)S(1)}, bf16[256,256]{1,0:T(8,128)(2,1)S(1)}, u32[]{:S(2)}, u32[]{:S(2)}) collective-permute-start(bf16[256,256]{1,0:T(8,128)(2,1)S(1)} %get-tuple-element.21), channel_id=1, source_target_pairs={{0,192},{64,128},{128,64},{192,0},{1,193},{65,129},{129,65},{193,1... | collective-permute-start | bytes 393224 | tf_op jit(solution)/shard_map/ppermute | solution.py:235
  60.6 7.1 %collective-permute-start.4 = (bf16[512,128]{1,0:T(8,128)(2,1)S(1)}, bf16[512,128]{1,0:T(8,128)(2,1)S(1)}, u32[]{:S(2)}, u32[]{:S(2)}) collective-permute-start(bf16[512,128]{1,0:T(8,128)(2,1)S(1)} %shard_map.106), channel_id=1, source_target_pairs={{0,16},{4,20},{16,0},{20,4},{1,17},{5,21},{17,1},{21,5},{2,18},{6,... | collective-permute-start | bytes 393224 | tf_op jit(solution)/shard_map/ppermute | solution.py:231

commit v2 on v1

--- a/solution.py
+++ b/solution.py
@@ -12,6 +12,7 @@
 AXES = ("y", "zh", "xh", "xl", "c", "zl")
 SIZES = (4, 2, 2, 2, 2, 4)
 HEAD_AXES = ("zl", "zh", "xl")
+BACK_AXES = ("zh", "xl", "zl")
 QUERY_AXES = ("xh", "c")
 RUNS = 4
 SCALE = HD**-0.5
@@ -66,7 +67,7 @@
     delta = jnp.concatenate([delta, jnp.zeros((128 - rows, 128), F32)], axis=0).T
     delta_high, delta_low = split_two(delta)
     lse_high, lse_low = split_two(lse_ref[...])
-    row = iota((16, 128), 0)
+    row = iota((8, 128), 0)
     for copy in copies[3:]:
         copy.wait()
     for h in range(16):
@@ -78,7 +79,7 @@
         stats = jnp.where(row == 1, lse_low[j : j + 1], stats)
         stats = jnp.where(row == 2, delta_high[h : h + 1], stats)
         stats = jnp.where(row == 3, delta_low[h : h + 1], stats)
-        out_ref[h, 4 * rows : 4 * rows + 16, :] = stats.astype(BF16)
+        out_ref[h, 4 * rows : 4 * rows + 8, :] = stats.astype(BF16)
 
 
 def placing(copy_ref, j):
@@ -95,7 +96,7 @@
 
 def sort_kernel(got_ref, copy_ref, qd_ref, kv_ref, kvn_ref):
     zl = lax.axis_index("zl")
-    row = iota((16, RUN), 0)
+    row = iota((8, RUN), 0)
     stats = []
     for j in range(RUNS):
         zh, xl = divmod(j, 2)
@@ -110,11 +111,12 @@
         kvn_ref[128 * zh + 64 * xl : 128 * zh + 64 * xl + 64, :] = moved[:HALF, 256:]
         for y in range(4):
             kv_ref[y, 128 * zh + 64 * xl : 128 * zh + 64 * xl + 64, :] = moved[HALF:, 256:]
-        lse = got_ref[4 * zl + j, 128:144, :].astype(F32)
+        lse = got_ref[4 * zl + j, 128:136, :].astype(F32)
         delta = jnp.concatenate(
-            [got_ref[4 * z + j, 128:144, :].astype(F32)[:, :32] for z in range(4)], axis=1
-        )
-        both = jnp.where(row < 2, lse, delta).astype(BF16)
+            [got_ref[4 * z + j, 128:136, :].astype(F32)[:, :32] for z in range(4)], axis=1
+        )
+        both = jnp.where(row < 2, lse, delta)
+        both = jnp.concatenate([both, jnp.zeros_like(both)], axis=0).astype(BF16)
         stats.append(contract(both, one_hot, 1, 1))
     halves = []
     for zh in range(2):
@@ -217,14 +219,14 @@
         moved = contract(one_hot, jnp.concatenate([queries, keys], axis=1), 1, 0).astype(BF16)
         for z in range(4):
             for i in range(3):
-                out_ref[4 * z + j, 32 * i : 32 * i + 32, :] = moved[32 * z : 32 * z + 32, HD * i : HD * (i + 1)]
+                out_ref[4 * j + z, 32 * i : 32 * i + 32, :] = moved[32 * z : 32 * z + 32, HD * i : HD * (i + 1)]
 
 
 def unpack_kernel(got_ref, dq_ref, dk_ref, dv_ref):
     rows = dq_ref.shape[0]
     for h in range(16):
         for i, ref in enumerate((dq_ref, dk_ref, dv_ref)):
-            ref[:, h * HD : (h + 1) * HD] = got_ref[h, i * rows : (i + 1) * rows, :]
+            ref[:, h * HD : (h + 1) * HD] = got_ref[4 * (h % 4) + h // 4, i * rows : (i + 1) * rows, :]
 
 
 def swap(x, mask):
@@ -245,7 +247,7 @@
     rows = query_in.shape[0]
     packed = call(
         pack_kernel,
-        shape((16, 4 * rows + 16, HD)),
+        shape((16, 4 * rows + 8, HD)),
         (query_in, key_in, value_in, saved_out, grad_out, saved_lse.T),
         hbm=range(6),
         limit=62 << 20,
@@ -276,7 +278,7 @@
         dkvs[m] = swap_y(dkvs[m], m)
     dq_chip = swap(call(add_kernel, shape((512, HD)), (dq_keep, dq_core)), 2)
     back = call(unsort_kernel, shape((16, 3 * rows, HD)), (dq_keep, dq_core, dq_chip, *dkvs, dkvn, copies))
-    back = lax.all_to_all(back, HEAD_AXES, 0, 0, tiled=True)
+    back = lax.all_to_all(back, BACK_AXES, 0, 0, tiled=True)
     return call(unpack_kernel, (shape((rows, 16 * HD)),) * 3, (back,))
 
 

time: 86.2 us -> 84.4 us (0.979); the launches traced: 85.8 us -> 83.1 us
  blocking collectives: 43.8 us -> 41 us
    all_to_all x1, blocking collectives: 16.1 us -> 14.1 us  [per_device(): back = lax.all_to_all(back, BACK_AXES, 0, 0, tiled=True)]
where the time goes in v2:
time: 84.4 us; the launch traced here: 83.1 us
  blocking collectives  41 us (49%)
  starting transfers between devices  20.3 us (24%)
  Pallas kernels  12 us (14%)
  waiting for transfers between devices  8.25 us (10%)
  local copies, waits for them, and re-layouts  0.85 us (1%)
    all_to_all x1, blocking collectives, per_device(): got = lax.all_to_all(packed, HEAD_AXES, 0, 0, tiled=True)  26.9 us
    all_to_all x1, blocking collectives, per_device(): back = lax.all_to_all(back, BACK_AXES, 0, 0, tiled=True)  14.1 us
    ppermute x5, starting transfers between devices, swap(): return lax.ppermute(x, QUERY_AXES, [(i, i ^ mask) for i in range(4)])  12.3 us
    pallas_call x6, Pallas kernels, call(): pl.pallas_call(body, out_shape=out_shape, in_specs=[SMEM if i in smem els...  12 us
    ppermute x3, waiting for transfers between devices, swap_y(): return lax.ppermute(x, 'y', [(i, i ^ mask) for i in range(4)])  6.53 us
    all_to_all x1, starting transfers between devices, per_device(): kvs = lax.all_to_all(kv, 'y', 0, 0, tiled=True)  4.19 us
    ppermute x3, starting transfers between devices, swap_y(): return lax.ppermute(x, 'y', [(i, i ^ mask) for i in range(4)])  3.88 us
    all_to_all x1, waiting for transfers between devices, per_device(): kvs = lax.all_to_all(kv, 'y', 0, 0, tiled=True)  1.7 us
  transfers between devices with their start and end apart: 9, of which 4 were waited for; matrix products, arithmetic and copies ran while one was open for 1% of the time, Pallas kernels for 0%

profile of v2, /device:TPU:1, one launch (start us, length us, event | category | flops | bytes accessed | tf_op | source)
XLA Modules:
  0.0 83.1 jit_solution(6087159422652618452)
XLA Ops:
  0.6 2.1 %shard_map.103 = bf16[16,136,128]{2,1,0:T(8,128)(2,1)} custom-call(bf16[32,2048]{1,0:T(8,128)(2,1)} %q_in.1, bf16[32,2048]{1,0:T(8,128)(2,1)} %k_in.1, bf16[32,2048]{1,0:T(8,128)(2,1)} %v_in.1, bf16[32,2048]{1,0:T(8,128)(2,1)} %o_in.1, bf16[32,2048]{1,0:T(8,128)(2,1)} %g_in.1, f32[4,128]{1,0:T(4,128)} %bitcast.4), custom_call_target="tpu_custom_call" | custom-call | tf_op jit(solution)/shard_map/pallas_call | solution.py:42
  2.8 0.0 copy-start
  2.8 26.9 %all_to_all.15.got_ref = bf16[16,136,128]{2,1,0:T(8,128)(2,1)S(1)} all-to-all(bf16[16,136,128]{2,1,0:T(8,128)(2,1)} %shard_map.103), channel_id=1, replica_groups=mesh['y'=4,'zh'=2,'xh'=2,'xl'=2,'c'=2,'zl'=4] {'zl','zh','xl'}, dimensions={0} | all-to-all | bytes 1114112 | tf_op jit(solution)/shard_map/all_to_all | solution.py:256
  29.7 0.0 copy-done
  29.7 1.6 %shard_map.104 = (bf16[528,256]{1,0:T(8,128)(2,1)S(1)}, bf16[4,256,256]{2,1,0:T(8,128)(2,1)}, bf16[256,256]{1,0:T(8,128)(2,1)S(1)}) custom-call(bf16[16,136,128]{2,1,0:T(8,128)(2,1)S(1)} %all_to_all.15.got_ref, s32[64,128]{1,0:T(8,128)S(1)} %bitcast.2), custom_call_target="tpu_custom_call" | custom-call | tf_op jit(solution)/shard_map/pallas_call | solution.py:42
  31.3 2.5 %collective-permute-start.1 = (bf16[528,256]{1,0:T(8,128)(2,1)S(1)}, bf16[528,256]{1,0:T(8,128)(2,1)S(1)}, u32[]{:S(2)}, u32[]{:S(2)}) collective-permute-start(bf16[528,256]{1,0:T(8,128)(2,1)S(1)} %get-tuple-element.13.qd0), channel_id=1, source_target_pairs={{0,16},{4,20},{16,0},{20,4},{1,17},{5,21},{17,1},{21,5},{2,18},{6,... | collective-permute-start | bytes 811016 | tf_op jit(solution)/shard_map/ppermute | solution.py:233
  33.8 4.2 %all-to-all-start.1 = ((bf16[4,256,256]{2,1,0:T(8,128)(2,1)}), bf16[4,256,256]{2,1,0:T(8,128)(2,1)S(1)}, u32[]{:S(2)}, u32[]{:S(2)}) async-start(bf16[4,256,256]{2,1,0:T(8,128)(2,1)} %get-tuple-element.14), calls=%async_computation.1 | async-start | bytes 1048576 | tf_op jit(solution)/shard_map/all_to_all | solution.py:261
  38.0 3.6 %collective-permute-start = (bf16[528,256]{1,0:T(8,128)(2,1)S(1)}, bf16[528,256]{1,0:T(8,128)(2,1)S(1)}, u32[]{:S(2)}, u32[]{:S(2)}) collective-permute-start(bf16[528,256]{1,0:T(8,128)(2,1)S(1)} %get-tuple-element.13.qd0), channel_id=1, source_target_pairs={{0,4},{4,0},{16,20},{20,16},{1,5},{5,1},{17,21},{21,17},{2,6},{6,2... | collective-permute-start | bytes 811016 | tf_op jit(solution)/shard_map/ppermute | solution.py:233
  41.6 0.0 collective-permute-done.1.qd2
  41.6 0.8 collective-permute-start.2
  42.3 0.8 %slice.3.ids_ref = s32[16]{0:T(128)S(1)} slice(s32[8192]{0:T(1024)} %param.14), slice={[0:8192:512]} | slice | bytes 128 | tf_op jit(solution)/shard_map/slice | solution.py:246
  43.2 0.0 collective-permute-done.qd1
  43.2 1.7 %all-to-all-done.1.kv_ref = bf16[4,256,256]{2,1,0:T(8,128)(2,1)S(1)} async-done(((bf16[4,256,256]{2,1,0:T(8,128)(2,1)}), bf16[4,256,256]{2,1,0:T(8,128)(2,1)S(1)}, u32[]{:S(2)}, u32[]{:S(2)}) %all-to-all-start.1) | async-done | bytes 524320 | tf_op jit(solution)/shard_map/all_to_all | solution.py:261
  44.9 0.0 collective-permute-done.2.qd3
  44.9 6.3 %shard_map.105 = (f32[2,512,128]{2,1,0:T(8,128)S(1)}, bf16[2,512,128]{2,1,0:T(8,128)(2,1)S(1)}, f32[256,256]{1,0:T(8,128)S(1)}, bf16[256,256]{1,0:T(8,128)(2,1)S...) custom-call(s32[16]{0:T(128)S(1)} %slice.3.ids_ref, ...), custom_call_target="tpu_custom_call" | custom-call | tf_op jit(solution)/shard_map/pallas_call | solution.py:42
  51.2 4.8 %collective-permute-start.3 = (bf16[2,512,128]{2,1,0:T(8,128)(2,1)S(1)}, bf16[2,512,128]{2,1,0:T(8,128)(2,1)S(1)}, u32[]{:S(2)}, u32[]{:S(2)}) collective-permute-start(bf16[2,512,128]{2,1,0:T(8,128)(2,1)S(1)} %get-tuple-element.17), channel_id=1, source_target_pairs={{0,4},{4,0},{16,20},{20,16},{1,5},{5,1},{17,21},{21,17},{2,6},{6,2... | collective-permute-start | bytes 786440 | tf_op jit(solution)/shard_map/ppermute | solution.py:233
  56.1 0.3 collective-permute-start.5
  56.4 1.8 %collective-permute-start.6 = (bf16[256,256]{1,0:T(8,128)(2,1)S(1)}, bf16[256,256]{1,0:T(8,128)(2,1)S(1)}, u32[]{:S(2)}, u32[]{:S(2)}) collective-permute-start(bf16[256,256]{1,0:T(8,128)(2,1)S(1)} %get-tuple-element.20), channel_id=1, source_target_pairs={{0,128},{64,192},{128,0},{192,64},{1,129},{65,193},{129,1},{193,65... | collective-permute-start | bytes 393224 | tf_op jit(solution)/shard_map/ppermute | solution.py:237
  58.2 1.8 %collective-permute-start.7 = (bf16[256,256]{1,0:T(8,128)(2,1)S(1)}, bf16[256,256]{1,0:T(8,128)(2,1)S(1)}, u32[]{:S(2)}, u32[]{:S(2)}) collective-permute-start(bf16[256,256]{1,0:T(8,128)(2,1)S(1)} %get-tuple-element.21), channel_id=1, source_target_pairs={{0,192},{64,128},{128,64},{192,0},{1,193},{65,129},{129,65},{193,1... | collective-permute-start | bytes 393224 | tf_op jit(solution)/shard_map/ppermute | solution.py:237
  59.9 0.0 collective-permute-done.3.got_ref.got_core
  60.0 0.6 collective-permute-start.4
  60.6 0.5 collective-permute-done.5.dkv1
  61.1 3.5 %collective-permute-done.6.dkv2 = bf16[256,256]{1,0:T(8,128)(2,1)S(1)} collective-permute-done((bf16[256,256]{1,0:T(8,128)(2,1)S(1)}, bf16[256,256]{1,0:T(8,128)(2,1)S(1)}, u32[]{:S(2)}, u32[]{:S(2)}) %collective-permute-start.6) | collective-permute-done | bytes 131104 | tf_op jit(solution)/shard_map/ppermute | solution.py:237
  64.6 2.5 %collective-permute-done.7.dkv3 = bf16[256,256]{1,0:T(8,128)(2,1)S(1)} collective-permute-done((bf16[256,256]{1,0:T(8,128)(2,1)S(1)}, bf16[256,256]{1,0:T(8,128)(2,1)S(1)}, u32[]{:S(2)}, u32[]{:S(2)}) %collective-permute-start.7) | collective-permute-done | bytes 131104 | tf_op jit(solution)/shard_map/ppermute | solution.py:237
  67.1 0.0 collective-permute-done.4.got_chip
  67.1 1.1 %shard_map.107 = bf16[16,96,128]{2,1,0:T(8,128)(2,1)S(1)} custom-call(f32[2,512,128]{2,1,0:T(8,128)S(1)} %get-tuple-element.16.keep_ref, bf16[2,512,128]{2,1,0:T(8,128)(2,1)S(1)} %collective-permute-done.3.got_ref.got_core, bf16[512,128]{1,0:T(8,128)(2,1)S(1)} %collective-permute-done.4.got_chip, f32[256,256]{1,0:T(8,128)S(1)} %get-tuple-element.18.dkv0, ...), custom_call_target="tpu_custom_call" | custom-call | tf_op jit(solution)/shard_map/pallas_call | solution.py:42
  68.2 14.1 %all_to_all.16.got_ref = bf16[16,96,128]{2,1,0:T(8,128)(2,1)S(1)} all-to-all(bf16[16,96,128]{2,1,0:T(8,128)(2,1)S(1)} %shard_map.107), channel_id=1, replica_groups=mesh['y'=4,'zh'=2,'xh'=2,'xl'=2,'c'=2,'zl'=4] {'zh','xl','zl'}, dimensions={0} | all-to-all | bytes 786432 | tf_op jit(solution)/shard_map/all_to_all | solution.py:281
  82.2 0.8 shard_map.108
  (1 shorter events, 0.0 us)
Async XLA Ops:
  2.8 26.9 %copy-start = (s32[8192]{0:T(1024)S(1)}, s32[8192]{0:T(1024)}, u32[]{:S(2)}) copy-start(s32[8192]{0:T(1024)} %param.15) | copy-start | bytes 98308
  31.3 10.3 %collective-permute-start.1 = (bf16[528,256]{1,0:T(8,128)(2,1)S(1)}, bf16[528,256]{1,0:T(8,128)(2,1)S(1)}, u32[]{:S(2)}, u32[]{:S(2)}) collective-permute-start(bf16[528,256]{1,0:T(8,128)(2,1)S(1)} %get-tuple-element.13.qd0), channel_id=1, source_target_pairs={{0,16},{4,20},{16,0},{20,4},{1,17},{5,21},{17,1},{21,5},{2,18},{6,... | collective-permute-start | bytes 811016 | tf_op jit(solution)/shard_map/ppermute | solution.py:233
  33.8 11.1 %all-to-all-start.1 = ((bf16[4,256,256]{2,1,0:T(8,128)(2,1)}), bf16[4,256,256]{2,1,0:T(8,128)(2,1)S(1)}, u32[]{:S(2)}, u32[]{:S(2)}) async-start(bf16[4,256,256]{2,1,0:T(8,128)(2,1)} %get-tuple-element.14), calls=%async_computation.1 | async-start | bytes 1048576 | tf_op jit(solution)/shard_map/all_to_all | solution.py:261
  38.0 5.2 %collective-permute-start = (bf16[528,256]{1,0:T(8,128)(2,1)S(1)}, bf16[528,256]{1,0:T(8,128)(2,1)S(1)}, u32[]{:S(2)}, u32[]{:S(2)}) collective-permute-start(bf16[528,256]{1,0:T(8,128)(2,1)S(1)} %get-tuple-element.13.qd0), channel_id=1, source_target_pairs={{0,4},{4,0},{16,20},{20,16},{1,5},{5,1},{17,21},{21,17},{2,6},{6,2... | collective-permute-start | bytes 811016 | tf_op jit(solution)/shard_map/ppermute | solution.py:233
  41.6 3.3 %collective-permute-start.2 = (bf16[528,256]{1,0:T(8,128)(2,1)S(1)}, bf16[528,256]{1,0:T(8,128)(2,1)S(1)}, u32[]{:S(2)}, u32[]{:S(2)}) collective-permute-start(bf16[528,256]{1,0:T(8,128)(2,1)S(1)} %collective-permute-done.1.qd2), channel_id=1, source_target_pairs={{0,4},{4,0},{16,20},{20,16},{1,5},{5,1},{17,21},{21,17},{2,6},{6,2... | collective-permute-start | bytes 811016 | tf_op jit(solution)/shard_map/ppermute | solution.py:233
  51.2 8.7 %collective-permute-start.3 = (bf16[2,512,128]{2,1,0:T(8,128)(2,1)S(1)}, bf16[2,512,128]{2,1,0:T(8,128)(2,1)S(1)}, u32[]{:S(2)}, u32[]{:S(2)}) collective-permute-start(bf16[2,512,128]{2,1,0:T(8,128)(2,1)S(1)} %get-tuple-element.17), channel_id=1, source_target_pairs={{0,4},{4,0},{16,20},{20,16},{1,5},{5,1},{17,21},{21,17},{2,6},{6,2... | collective-permute-start | bytes 786440 | tf_op jit(solution)/shard_map/ppermute | solution.py:233
  56.1 5.1 %collective-permute-start.5 = (bf16[256,256]{1,0:T(8,128)(2,1)S(1)}, bf16[256,256]{1,0:T(8,128)(2,1)S(1)}, u32[]{:S(2)}, u32[]{:S(2)}) collective-permute-start(bf16[256,256]{1,0:T(8,128)(2,1)S(1)} %get-tuple-element.19), channel_id=1, source_target_pairs={{0,64},{64,0},{128,192},{192,128},{1,65},{65,1},{129,193},{193,129... | collective-permute-start | bytes 393224 | tf_op jit(solution)/shard_map/ppermute | solution.py:237
  56.4 8.2 %collective-permute-start.6 = (bf16[256,256]{1,0:T(8,128)(2,1)S(1)}, bf16[256,256]{1,0:T(8,128)(2,1)S(1)}, u32[]{:S(2)}, u32[]{:S(2)}) collective-permute-start(bf16[256,256]{1,0:T(8,128)(2,1)S(1)} %get-tuple-element.20), channel_id=1, source_target_pairs={{0,128},{64,192},{128,0},{192,64},{1,129},{65,193},{129,1},{193,65... | collective-permute-start | bytes 393224 | tf_op jit(solution)/shard_map/ppermute | solution.py:237
  58.2 9.0 %collective-permute-start.7 = (bf16[256,256]{1,0:T(8,128)(2,1)S(1)}, bf16[256,256]{1,0:T(8,128)(2,1)S(1)}, u32[]{:S(2)}, u32[]{:S(2)}) collective-permute-start(bf16[256,256]{1,0:T(8,128)(2,1)S(1)} %get-tuple-element.21), channel_id=1, source_target_pairs={{0,192},{64,128},{128,64},{192,0},{1,193},{65,129},{129,65},{193,1... | collective-permute-start | bytes 393224 | tf_op jit(solution)/shard_map/ppermute | solution.py:237
  60.0 7.1 %collective-permute-start.4 = (bf16[512,128]{1,0:T(8,128)(2,1)S(1)}, bf16[512,128]{1,0:T(8,128)(2,1)S(1)}, u32[]{:S(2)}, u32[]{:S(2)}) collective-permute-start(bf16[512,128]{1,0:T(8,128)(2,1)S(1)} %shard_map.106), channel_id=1, source_target_pairs={{0,16},{4,20},{16,0},{20,4},{1,17},{5,21},{17,1},{21,5},{2,18},{6,... | collective-permute-start | bytes 393224 | tf_op jit(solution)/shard_map/ppermute | solution.py:233

commit v3 on v2

--- a/solution.py
+++ b/solution.py
@@ -245,12 +245,12 @@
     copies = row_copy.reshape(-1, RUN)
     ids = row_block[:: 4 * RUN]
     rows = query_in.shape[0]
+    arrays = (query_in, key_in, value_in, saved_out, grad_out, saved_lse.T)
     packed = call(
         pack_kernel,
         shape((16, 4 * rows + 8, HD)),
-        (query_in, key_in, value_in, saved_out, grad_out, saved_lse.T),
+        tuple(pltpu.with_memory_space_constraint(x, pltpu.HBM) for x in arrays),
         hbm=range(6),
-        limit=62 << 20,
         scratch=[pltpu.VMEM(query_in.shape, BF16)] * 5 + [pltpu.VMEM((4, 128), F32), pltpu.SemaphoreType.DMA((6,))],
     )
     got = lax.all_to_all(packed, HEAD_AXES, 0, 0, tiled=True)
@@ -277,7 +277,7 @@
     for m in (2, 1, 3):
         dkvs[m] = swap_y(dkvs[m], m)
     dq_chip = swap(call(add_kernel, shape((512, HD)), (dq_keep, dq_core)), 2)
-    back = call(unsort_kernel, shape((16, 3 * rows, HD)), (dq_keep, dq_core, dq_chip, *dkvs, dkvn, copies))
+    back = call(unsort_kernel, shape((16, 3 * rows, HD)), (dq_keep, dq_core, dq_chip, dkvs[0], dkvs[3], dkvs[2], dkvs[1], dkvn, copies))
     back = lax.all_to_all(back, BACK_AXES, 0, 0, tiled=True)
     return call(unpack_kernel, (shape((rows, 16 * HD)),) * 3, (back,))
 

time: 84.4 us -> 81.7 us (0.968)
  waiting for transfers between devices: 8.25 us -> 7.16 us
    ppermute x3, waiting for transfers between devices: 6.53 us -> 5.45 us  [swap_y(): return lax.ppermute(x, 'y', [(i, i ^ mask) for i in range(4)])]
  transfers between devices with their start and end apart: 9 -> 9, of which waited for: 4 -> 3; matrix products, arithmetic and copies ran while one was open for 1% -> 1% of each run, Pallas kernels for 0% -> 0%
where the time goes in v3:
time: 81.7 us; the launch traced here: 80.5 us
  blocking collectives  40.9 us (50%)
  starting transfers between devices  19.7 us (24%)
  Pallas kernels  11.2 us (14%)
  waiting for transfers between devices  7.16 us (9%)
  local copies, waits for them, and re-layouts  0.85 us (1%)
    all_to_all x1, blocking collectives, per_device(): got = lax.all_to_all(packed, HEAD_AXES, 0, 0, tiled=True)  26.7 us
    all_to_all x1, blocking collectives, per_device(): back = lax.all_to_all(back, BACK_AXES, 0, 0, tiled=True)  14.2 us
    ppermute x5, starting transfers between devices, swap(): return lax.ppermute(x, QUERY_AXES, [(i, i ^ mask) for i in range(4)])  12.3 us
    pallas_call x6, Pallas kernels, call(): pl.pallas_call(body, out_shape=out_shape, in_specs=[SMEM if i in smem els...  11.2 us
    ppermute x3, waiting for transfers between devices, swap_y(): return lax.ppermute(x, 'y', [(i, i ^ mask) for i in range(4)])  5.45 us
    all_to_all x1, starting transfers between devices, per_device(): kvs = lax.all_to_all(kv, 'y', 0, 0, tiled=True)  4.19 us
    ppermute x3, starting transfers between devices, swap_y(): return lax.ppermute(x, 'y', [(i, i ^ mask) for i in range(4)])  3.27 us
    all_to_all x1, waiting for transfers between devices, per_device(): kvs = lax.all_to_all(kv, 'y', 0, 0, tiled=True)  1.7 us
  transfers between devices with their start and end apart: 9, of which 3 were waited for; matrix products, arithmetic and copies ran while one was open for 1% of the time, Pallas kernels for 0%

profile of v3, /device:TPU:1, one launch (start us, length us, event | category | flops | bytes accessed | tf_op | source)
XLA Modules:
  0.0 80.5 jit_solution(3857364035112303473)
XLA Ops:
  0.6 1.3 %shard_map.103 = bf16[16,136,128]{2,1,0:T(8,128)(2,1)S(1)} custom-call(bf16[32,2048]{1,0:T(8,128)(2,1)} %q_in.1, bf16[32,2048]{1,0:T(8,128)(2,1)} %k_in.1, bf16[32,2048]{1,0:T(8,128)(2,1)} %v_in.1, bf16[32,2048]{1,0:T(8,128)(2,1)} %o_in.1, bf16[32,2048]{1,0:T(8,128)(2,1)} %g_in.1, f32[4,128]{1,0:T(4,128)} %bitcast.4), custom_call_target="tpu_custom_call" | custom-call | tf_op jit(solution)/shard_map/pallas_call | solution.py:42
  2.0 0.0 copy-start
  2.0 26.7 %all_to_all.15.got_ref = bf16[16,136,128]{2,1,0:T(8,128)(2,1)S(1)} all-to-all(bf16[16,136,128]{2,1,0:T(8,128)(2,1)S(1)} %shard_map.103), channel_id=1, replica_groups=mesh['y'=4,'zh'=2,'xh'=2,'xl'=2,'c'=2,'zl'=4] {'zl','zh','xl'}, dimensions={0} | all-to-all | bytes 1114112 | tf_op jit(solution)/shard_map/all_to_all | solution.py:256
  28.7 0.0 copy-done
  28.7 1.6 %shard_map.104 = (bf16[528,256]{1,0:T(8,128)(2,1)S(1)}, bf16[4,256,256]{2,1,0:T(8,128)(2,1)}, bf16[256,256]{1,0:T(8,128)(2,1)S(1)}) custom-call(bf16[16,136,128]{2,1,0:T(8,128)(2,1)S(1)} %all_to_all.15.got_ref, s32[64,128]{1,0:T(8,128)S(1)} %bitcast.2), custom_call_target="tpu_custom_call" | custom-call | tf_op jit(solution)/shard_map/pallas_call | solution.py:42
  30.3 2.4 %collective-permute-start.1 = (bf16[528,256]{1,0:T(8,128)(2,1)S(1)}, bf16[528,256]{1,0:T(8,128)(2,1)S(1)}, u32[]{:S(2)}, u32[]{:S(2)}) collective-permute-start(bf16[528,256]{1,0:T(8,128)(2,1)S(1)} %get-tuple-element.13.qd0), channel_id=1, source_target_pairs={{0,16},{4,20},{16,0},{20,4},{1,17},{5,21},{17,1},{21,5},{2,18},{6,... | collective-permute-start | bytes 811016 | tf_op jit(solution)/shard_map/ppermute | solution.py:233
  32.8 4.2 %all-to-all-start.1 = ((bf16[4,256,256]{2,1,0:T(8,128)(2,1)}), bf16[4,256,256]{2,1,0:T(8,128)(2,1)S(1)}, u32[]{:S(2)}, u32[]{:S(2)}) async-start(bf16[4,256,256]{2,1,0:T(8,128)(2,1)} %get-tuple-element.14), calls=%async_computation.1 | async-start | bytes 1048576 | tf_op jit(solution)/shard_map/all_to_all | solution.py:261
  36.9 3.6 %collective-permute-start = (bf16[528,256]{1,0:T(8,128)(2,1)S(1)}, bf16[528,256]{1,0:T(8,128)(2,1)S(1)}, u32[]{:S(2)}, u32[]{:S(2)}) collective-permute-start(bf16[528,256]{1,0:T(8,128)(2,1)S(1)} %get-tuple-element.13.qd0), channel_id=1, source_target_pairs={{0,4},{4,0},{16,20},{20,16},{1,5},{5,1},{17,21},{21,17},{2,6},{6,2... | collective-permute-start | bytes 811016 | tf_op jit(solution)/shard_map/ppermute | solution.py:233
  40.5 0.0 collective-permute-done.1.qd2
  40.6 0.8 collective-permute-start.2
  41.3 0.8 %slice.3.ids_ref = s32[16]{0:T(128)S(1)} slice(s32[8192]{0:T(1024)} %param.14), slice={[0:8192:512]} | slice | bytes 128 | tf_op jit(solution)/shard_map/slice | solution.py:246
  42.2 0.0 collective-permute-done.qd1
  42.2 1.7 %all-to-all-done.1.kv_ref = bf16[4,256,256]{2,1,0:T(8,128)(2,1)S(1)} async-done(((bf16[4,256,256]{2,1,0:T(8,128)(2,1)}), bf16[4,256,256]{2,1,0:T(8,128)(2,1)S(1)}, u32[]{:S(2)}, u32[]{:S(2)}) %all-to-all-start.1) | async-done | bytes 524320 | tf_op jit(solution)/shard_map/all_to_all | solution.py:261
  43.9 0.0 collective-permute-done.2.qd3
  43.9 6.3 %shard_map.105 = (f32[2,512,128]{2,1,0:T(8,128)S(1)}, bf16[2,512,128]{2,1,0:T(8,128)(2,1)S(1)}, f32[256,256]{1,0:T(8,128)S(1)}, bf16[256,256]{1,0:T(8,128)(2,1)S...) custom-call(s32[16]{0:T(128)S(1)} %slice.3.ids_ref, ...), custom_call_target="tpu_custom_call" | custom-call | tf_op jit(solution)/shard_map/pallas_call | solution.py:42
  50.2 4.8 %collective-permute-start.3 = (bf16[2,512,128]{2,1,0:T(8,128)(2,1)S(1)}, bf16[2,512,128]{2,1,0:T(8,128)(2,1)S(1)}, u32[]{:S(2)}, u32[]{:S(2)}) collective-permute-start(bf16[2,512,128]{2,1,0:T(8,128)(2,1)S(1)} %get-tuple-element.17), channel_id=1, source_target_pairs={{0,4},{4,0},{16,20},{20,16},{1,5},{5,1},{17,21},{21,17},{2,6},{6,2... | collective-permute-start | bytes 786440 | tf_op jit(solution)/shard_map/ppermute | solution.py:233
  55.0 0.9 %collective-permute-start.5 = (bf16[256,256]{1,0:T(8,128)(2,1)S(1)}, bf16[256,256]{1,0:T(8,128)(2,1)S(1)}, u32[]{:S(2)}, u32[]{:S(2)}) collective-permute-start(bf16[256,256]{1,0:T(8,128)(2,1)S(1)} %get-tuple-element.19), channel_id=1, source_target_pairs={{0,192},{64,128},{128,64},{192,0},{1,193},{65,129},{129,65},{193,1... | collective-permute-start | bytes 393224 | tf_op jit(solution)/shard_map/ppermute | solution.py:237
  55.9 1.2 %collective-permute-start.6 = (bf16[256,256]{1,0:T(8,128)(2,1)S(1)}, bf16[256,256]{1,0:T(8,128)(2,1)S(1)}, u32[]{:S(2)}, u32[]{:S(2)}) collective-permute-start(bf16[256,256]{1,0:T(8,128)(2,1)S(1)} %get-tuple-element.20), channel_id=1, source_target_pairs={{0,128},{64,192},{128,0},{192,64},{1,129},{65,193},{129,1},{193,65... | collective-permute-start | bytes 393224 | tf_op jit(solution)/shard_map/ppermute | solution.py:237
  57.1 1.2 %collective-permute-start.7 = (bf16[256,256]{1,0:T(8,128)(2,1)S(1)}, bf16[256,256]{1,0:T(8,128)(2,1)S(1)}, u32[]{:S(2)}, u32[]{:S(2)}) collective-permute-start(bf16[256,256]{1,0:T(8,128)(2,1)S(1)} %get-tuple-element.21), channel_id=1, source_target_pairs={{0,64},{64,0},{128,192},{192,128},{1,65},{65,1},{129,193},{193,129... | collective-permute-start | bytes 393224 | tf_op jit(solution)/shard_map/ppermute | solution.py:237
  58.3 0.0 collective-permute-done.3.got_ref.got_core
  58.3 0.6 collective-permute-start.4
  59.0 5.2 %collective-permute-done.5.dkv1 = bf16[256,256]{1,0:T(8,128)(2,1)S(1)} collective-permute-done((bf16[256,256]{1,0:T(8,128)(2,1)S(1)}, bf16[256,256]{1,0:T(8,128)(2,1)S(1)}, u32[]{:S(2)}, u32[]{:S(2)}) %collective-permute-start.5) | collective-permute-done | bytes 131104 | tf_op jit(solution)/shard_map/ppermute | solution.py:237
  64.1 0.0 collective-permute-done.6.dkv2
  64.1 0.3 collective-permute-done.7.dkv3
  64.4 0.0 collective-permute-done.4.got_chip
  64.4 1.1 %shard_map.107 = bf16[16,96,128]{2,1,0:T(8,128)(2,1)S(1)} custom-call(f32[2,512,128]{2,1,0:T(8,128)S(1)} %get-tuple-element.16.keep_ref, bf16[2,512,128]{2,1,0:T(8,128)(2,1)S(1)} %collective-permute-done.3.got_ref.got_core, bf16[512,128]{1,0:T(8,128)(2,1)S(1)} %collective-permute-done.4.got_chip, f32[256,256]{1,0:T(8,128)S(1)} %get-tuple-element.18.dkv0, ...), custom_call_target="tpu_custom_call" | custom-call | tf_op jit(solution)/shard_map/pallas_call | solution.py:42
  65.5 14.2 %all_to_all.16.got_ref = bf16[16,96,128]{2,1,0:T(8,128)(2,1)S(1)} all-to-all(bf16[16,96,128]{2,1,0:T(8,128)(2,1)S(1)} %shard_map.107), channel_id=1, replica_groups=mesh['y'=4,'zh'=2,'xh'=2,'xl'=2,'c'=2,'zl'=4] {'zh','xl','zl'}, dimensions={0} | all-to-all | bytes 786432 | tf_op jit(solution)/shard_map/all_to_all | solution.py:281
  79.7 0.8 %shard_map.108 = (bf16[32,2048]{1,0:T(8,128)(2,1)}, bf16[32,2048]{1,0:T(8,128)(2,1)}, bf16[32,2048]{1,0:T(8,128)(2,1)}) custom-call(bf16[16,96,128]{2,1,0:T(8,128)(2,1)S(1)} %all_to_all.16.got_ref), custom_call_target="tpu_custom_call" | custom-call | tf_op jit(solution)/shard_map/pallas_call | solution.py:42
  (1 shorter events, 0.0 us)
Async XLA Ops:
  2.0 26.7 %copy-start = (s32[8192]{0:T(1024)S(1)}, s32[8192]{0:T(1024)}, u32[]{:S(2)}) copy-start(s32[8192]{0:T(1024)} %param.15) | copy-start | bytes 98308
  30.3 10.2 %collective-permute-start.1 = (bf16[528,256]{1,0:T(8,128)(2,1)S(1)}, bf16[528,256]{1,0:T(8,128)(2,1)S(1)}, u32[]{:S(2)}, u32[]{:S(2)}) collective-permute-start(bf16[528,256]{1,0:T(8,128)(2,1)S(1)} %get-tuple-element.13.qd0), channel_id=1, source_target_pairs={{0,16},{4,20},{16,0},{20,4},{1,17},{5,21},{17,1},{21,5},{2,18},{6,... | collective-permute-start | bytes 811016 | tf_op jit(solution)/shard_map/ppermute | solution.py:233
  32.8 11.1 %all-to-all-start.1 = ((bf16[4,256,256]{2,1,0:T(8,128)(2,1)}), bf16[4,256,256]{2,1,0:T(8,128)(2,1)S(1)}, u32[]{:S(2)}, u32[]{:S(2)}) async-start(bf16[4,256,256]{2,1,0:T(8,128)(2,1)} %get-tuple-element.14), calls=%async_computation.1 | async-start | bytes 1048576 | tf_op jit(solution)/shard_map/all_to_all | solution.py:261
  36.9 5.2 %collective-permute-start = (bf16[528,256]{1,0:T(8,128)(2,1)S(1)}, bf16[528,256]{1,0:T(8,128)(2,1)S(1)}, u32[]{:S(2)}, u32[]{:S(2)}) collective-permute-start(bf16[528,256]{1,0:T(8,128)(2,1)S(1)} %get-tuple-element.13.qd0), channel_id=1, source_target_pairs={{0,4},{4,0},{16,20},{20,16},{1,5},{5,1},{17,21},{21,17},{2,6},{6,2... | collective-permute-start | bytes 811016 | tf_op jit(solution)/shard_map/ppermute | solution.py:233
  40.6 3.3 %collective-permute-start.2 = (bf16[528,256]{1,0:T(8,128)(2,1)S(1)}, bf16[528,256]{1,0:T(8,128)(2,1)S(1)}, u32[]{:S(2)}, u32[]{:S(2)}) collective-permute-start(bf16[528,256]{1,0:T(8,128)(2,1)S(1)} %collective-permute-done.1.qd2), channel_id=1, source_target_pairs={{0,4},{4,0},{16,20},{20,16},{1,5},{5,1},{17,21},{21,17},{2,6},{6,2... | collective-permute-start | bytes 811016 | tf_op jit(solution)/shard_map/ppermute | solution.py:233
  50.2 8.1 %collective-permute-start.3 = (bf16[2,512,128]{2,1,0:T(8,128)(2,1)S(1)}, bf16[2,512,128]{2,1,0:T(8,128)(2,1)S(1)}, u32[]{:S(2)}, u32[]{:S(2)}) collective-permute-start(bf16[2,512,128]{2,1,0:T(8,128)(2,1)S(1)} %get-tuple-element.17), channel_id=1, source_target_pairs={{0,4},{4,0},{16,20},{20,16},{1,5},{5,1},{17,21},{21,17},{2,6},{6,2... | collective-permute-start | bytes 786440 | tf_op jit(solution)/shard_map/ppermute | solution.py:233
  55.0 9.1 %collective-permute-start.5 = (bf16[256,256]{1,0:T(8,128)(2,1)S(1)}, bf16[256,256]{1,0:T(8,128)(2,1)S(1)}, u32[]{:S(2)}, u32[]{:S(2)}) collective-permute-start(bf16[256,256]{1,0:T(8,128)(2,1)S(1)} %get-tuple-element.19), channel_id=1, source_target_pairs={{0,192},{64,128},{128,64},{192,0},{1,193},{65,129},{129,65},{193,1... | collective-permute-start | bytes 393224 | tf_op jit(solution)/shard_map/ppermute | solution.py:237
  55.9 8.2 %collective-permute-start.6 = (bf16[256,256]{1,0:T(8,128)(2,1)S(1)}, bf16[256,256]{1,0:T(8,128)(2,1)S(1)}, u32[]{:S(2)}, u32[]{:S(2)}) collective-permute-start(bf16[256,256]{1,0:T(8,128)(2,1)S(1)} %get-tuple-element.20), channel_id=1, source_target_pairs={{0,128},{64,192},{128,0},{192,64},{1,129},{65,193},{129,1},{193,65... | collective-permute-start | bytes 393224 | tf_op jit(solution)/shard_map/ppermute | solution.py:237
  57.1 7.3 %collective-permute-start.7 = (bf16[256,256]{1,0:T(8,128)(2,1)S(1)}, bf16[256,256]{1,0:T(8,128)(2,1)S(1)}, u32[]{:S(2)}, u32[]{:S(2)}) collective-permute-start(bf16[256,256]{1,0:T(8,128)(2,1)S(1)} %get-tuple-element.21), channel_id=1, source_target_pairs={{0,64},{64,0},{128,192},{192,128},{1,65},{65,1},{129,193},{193,129... | collective-permute-start | bytes 393224 | tf_op jit(solution)/shard_map/ppermute | solution.py:237
  58.3 6.1 %collective-permute-start.4 = (bf16[512,128]{1,0:T(8,128)(2,1)S(1)}, bf16[512,128]{1,0:T(8,128)(2,1)S(1)}, u32[]{:S(2)}, u32[]{:S(2)}) collective-permute-start(bf16[512,128]{1,0:T(8,128)(2,1)S(1)} %shard_map.106), channel_id=1, source_target_pairs={{0,16},{4,20},{16,0},{20,4},{1,17},{5,21},{17,1},{21,5},{2,18},{6,... | collective-permute-start | bytes 393224 | tf_op jit(solution)/shard_map/ppermute | solution.py:233

commit v4 on v3

--- a/solution.py
+++ b/solution.py
@@ -109,8 +109,7 @@
         qd_ref[256 * zh + 64 * xl : 256 * zh + 64 * xl + 64, :] = moved[:HALF, :256]
         qd_ref[256 * zh + 128 + 64 * xl : 256 * zh + 192 + 64 * xl, :] = moved[HALF:, :256]
         kvn_ref[128 * zh + 64 * xl : 128 * zh + 64 * xl + 64, :] = moved[:HALF, 256:]
-        for y in range(4):
-            kv_ref[y, 128 * zh + 64 * xl : 128 * zh + 64 * xl + 64, :] = moved[HALF:, 256:]
+        kv_ref[128 * zh + 64 * xl : 128 * zh + 64 * xl + 64, :] = moved[HALF:, 256:]
         lse = got_ref[4 * zl + j, 128:136, :].astype(F32)
         delta = jnp.concatenate(
             [got_ref[4 * z + j, 128:136, :].astype(F32)[:, :32] for z in range(4)], axis=1
@@ -127,76 +126,71 @@
     qd_ref[512:528, :] = jnp.concatenate(halves, axis=0).astype(BF16)
 
 
-def attend_kernel(
-    ids_ref, qd0, qd1, qd2, qd3, kv_ref, kvn_ref,
-    dq_keep, dq_send, dkv0, dkv1, dkv2, dkv3, dkvn_ref,
-    q_all, g_all, lse_all, delta_all, k_all, kt_all, v_all, dk_all, dv_all,
+def load_keys(clean, noisy_ref, k_all, kt_all, v_all):
+    for m, ref in enumerate((*clean, noisy_ref)):
+        rows = slice(256 * m, 256 * m + 256)
+        k = ref[:, :HD]
+        k_all[rows, :] = k
+        v_all[rows, :] = ref[:, HD:]
+        kt_all[:, rows] = k.astype(F32).T.astype(BF16)
+
+
+def attend(ids_ref, qd_ref, other, k_all, kt_all, v_all):
+    y, xh = lax.axis_index("y"), lax.axis_index("xh")
+    stats = qd_ref[512:528, :].astype(F32)
+    lse = jnp.concatenate([stats[0:1] + stats[1:2], stats[8:9] + stats[9:10]], axis=1) * LOG2E
+    delta = jnp.concatenate([stats[2:3] + stats[3:4], stats[10:11] + stats[11:12]], axis=1)
+    lane = iota((1, 512), 1)
+    clean, second = lane // 128 % 2 == 1, lane >= 256
+    own_ids = [ids_ref[(y * 2 + zh) * 2 + (xh ^ other)] for zh in range(2)]
+    limits = []
+    for n in range(8):
+        key_id = ids_ref[((y ^ (n // 2)) * 2 + n % 2) * 2 + xh]
+        noisy_off, clean_off = (
+            jnp.where(second, *(jnp.where(hit, 0.0, OFF) for hit in hits))
+            for hits in ([key_id < i for i in own_ids[::-1]], [key_id <= i for i in own_ids[::-1]])
+        )
+        limits.append(lse + jnp.where(clean, clean_off, noisy_off))
+    if not other:
+        limits.append(lse + jnp.where(clean | second, OFF, 0.0))
+        limits.append(lse + jnp.where(clean | ~second, OFF, 0.0))
+    last = 128 * len(limits)
+    q, g = qd_ref[:512, :HD], qd_ref[:512, HD:]
+    scores = contract(k_all[:last, :], q, 1, 1)
+    weights = jnp.concatenate(
+        [jnp.exp2(scores[128 * i : 128 * i + 128] * (SCALE * LOG2E) - row) for i, row in enumerate(limits)], axis=0
+    )
+    dweights = contract(v_all[:last, :], g, 1, 1)
+    dscores = (weights * (dweights - delta)).astype(BF16)
+    dv = contract(weights.astype(BF16), g, 1, 0)
+    dk = contract(dscores, q, 1, 0)
+    return dk, dv, contract(kt_all[:, :last], dscores, 1, 0).T * SCALE
+
+
+def first_kernel(ids_ref, qd0, qd2, kv0, kv1, kv2, kv3, kvn_ref, dq_ref, dk_ref, dv_ref, k_all, kt_all, v_all):
+    load_keys((kv0, kv1, kv2, kv3), kvn_ref, k_all, kt_all, v_all)
+    dk_ref[...], dv_ref[...], dq_ref[0] = attend(ids_ref, qd0, 0, k_all, kt_all, v_all)
+    dk, dv, dq_ref[1] = attend(ids_ref, qd2, 1, k_all, kt_all, v_all)
+    dk_ref[:1024, :] += dk
+    dv_ref[:1024, :] += dv
+
+
+def second_kernel(
+    ids_ref, qd1, qd3, kv0, kv1, kv2, kv3, kvn_ref, dk_ref, dv_ref,
+    dq_ref, dkv0, dkv1, dkv2, dkv3, dkvn, k_all, kt_all, v_all,
 ):
-    y, xh = lax.axis_index("y"), lax.axis_index("xh")
-    for m, ref in enumerate((qd0, qd1, qd2, qd3)):
-        stats = ref[512:528, :].astype(F32)
-        for zh in range(2):
-            block, at = zh * 2 + m // 2, 256 * (m % 2)
-            q_all[block, at : at + 256, :] = ref[256 * zh : 256 * zh + 256, :HD]
-            g_all[block, at : at + 256, :] = ref[256 * zh : 256 * zh + 256, HD:]
-            s = 8 * zh
-            lse_all[block, :, at : at + 256] = (stats[s : s + 1] + stats[s + 1 : s + 2]) * LOG2E
-            delta_all[block, :, at : at + 256] = stats[s + 2 : s + 3] + stats[s + 3 : s + 4]
-    for first, ref in ((0, kvn_ref.at[:128]), (1152, kvn_ref.at[128:])) + tuple(
-        (128 + 256 * d, kv_ref.at[d]) for d in range(4)
-    ):
-        size = ref.shape[0]
-        k = ref[:, :HD]
-        k_all[first : first + size, :] = k
-        v_all[first : first + size, :] = ref[:, HD:]
-        kt_all[:, first : first + size] = k.astype(F32).T.astype(BF16)
-
-    clean = iota((1, 512), 1) // 128 % 2 == 1
-    for block in (1, 3, 0, 2):
-        zh, other = divmod(block, 2)
-        own_id = ids_ref[(y * 2 + zh) * 2 + (xh ^ other)]
-        lse, delta = lse_all[block], delta_all[block]
-        limits = []
-        for n in range(8):
-            key_id = ids_ref[2 * n + xh]
-            noisy_off = jnp.where(key_id < own_id, 0.0, OFF)
-            clean_off = jnp.where(key_id <= own_id, 0.0, OFF)
-            limits.append(lse + jnp.where(clean, clean_off, noisy_off))
-        first, last = 128, 1152
-        if not other:
-            own_noisy = lse + jnp.where(clean, OFF, 0.0)
-            limits = limits + [own_noisy] if zh else [own_noisy] + limits
-            first, last = (128, 1280) if zh else (0, 1152)
-        q, g = q_all[block], g_all[block]
-        scores = contract(k_all[first:last, :], q, 1, 1)
-        weights = jnp.concatenate(
-            [jnp.exp2(scores[128 * i : 128 * i + 128] * (SCALE * LOG2E) - row) for i, row in enumerate(limits)],
-            axis=0,
-        )
-        dweights = contract(v_all[first:last, :], g, 1, 1)
-        dscores = (weights * (dweights - delta)).astype(BF16)
-        dv = contract(weights.astype(BF16), g, 1, 0)
-        dk = contract(dscores, q, 1, 0)
-        if block == 1:
-            dk_all[first:last, :] = dk
-            dv_all[first:last, :] = dv
-            zeros = jnp.zeros((128, HD), F32)
-            for ref in (dk_all, dv_all):
-                ref[:128, :] = zeros
-                ref[1152:, :] = zeros
-        else:
-            dk_all[first:last, :] += dk
-            dv_all[first:last, :] += dv
-        dq = contract(kt_all[:, first:last], dscores, 1, 0).T * SCALE
-        dq_keep[other, 256 * zh : 256 * zh + 256, :] = dq[:256]
-        dq_send[other, 256 * zh : 256 * zh + 256, :] = dq[256:].astype(BF16)
-    pieces = [(0, dkvn_ref.at[:128]), (1152, dkvn_ref.at[128:])]
-    for m, ref in enumerate((dkv0, dkv1, dkv2, dkv3)):
-        pieces.append((pl.multiple_of(128 + 256 * (y ^ m), 128), ref))
-    for first, ref in pieces:
-        rows = pl.ds(first, ref.shape[0])
-        ref[:, :HD] = (dk_all[rows, :] * SCALE).astype(ref.dtype)
-        ref[:, HD:] = dv_all[rows, :].astype(ref.dtype)
+    load_keys((kv0, kv1, kv2, kv3), kvn_ref, k_all, kt_all, v_all)
+    near_dk, near_dv, dq = attend(ids_ref, qd1, 0, k_all, kt_all, v_all)
+    dq_ref[0] = dq.astype(BF16)
+    far_dk, far_dv, dq = attend(ids_ref, qd3, 1, k_all, kt_all, v_all)
+    dq_ref[1] = dq.astype(BF16)
+    for m, ref in enumerate((dkv0, dkv1, dkv2, dkv3, dkvn)):
+        rows = slice(256 * m, 256 * m + 256)
+        dk, dv = dk_ref[rows, :] + near_dk[rows], dv_ref[rows, :] + near_dv[rows]
+        if m < 4:
+            dk, dv = dk + far_dk[rows], dv + far_dv[rows]
+        ref[:, :HD] = (dk * SCALE).astype(ref.dtype)
+        ref[:, HD:] = dv.astype(ref.dtype)
 
 
 def add_kernel(keep_ref, got_ref, out_ref):
@@ -255,23 +249,29 @@
     )
     got = lax.all_to_all(packed, HEAD_AXES, 0, 0, tiled=True)
     qd, kv, kvn = call(
-        sort_kernel, (shape((528, 256)), shape((4, 256, 256)), shape((256, 256))), (got, copies)
+        sort_kernel, (shape((528, 256)), shape((256, 256)), shape((256, 256))), (got, copies)
     )
     qd2 = swap(qd, 2)
-    kvs = lax.all_to_all(kv, "y", 0, 0, tiled=True)
+    kv1, kv2, kv3 = (swap_y(kv, m) for m in (1, 2, 3))
+    qd2, kv1, kv2, kv3, ids, qd = lax.optimization_barrier((qd2, kv1, kv2, kv3, ids, qd))
     qd1 = swap(qd, 1)
     qd3 = swap(qd2, 1)
-    outs = (
-        (shape((2, 512, HD), F32), shape((2, 512, HD)), shape((256, 256), F32)) + (shape((256, 256)),) * 4
-    )
-    scratch = (
-        pltpu.VMEM((4, 512, HD), BF16), pltpu.VMEM((4, 512, HD), BF16),
-        pltpu.VMEM((4, 1, 512), F32), pltpu.VMEM((4, 1, 512), F32),
-        pltpu.VMEM((1280, HD), BF16), pltpu.VMEM((HD, 1280), BF16), pltpu.VMEM((1280, HD), BF16),
-        pltpu.VMEM((1280, HD), F32), pltpu.VMEM((1280, HD), F32),
-    )
-    dq_keep, dq_send, *dkvs, dkvn = call(
-        attend_kernel, outs, (ids, qd, qd1, qd2, qd3, kvs, kvn), smem=(0,), scratch=scratch
+    keys = (kv, kv1, kv2, kv3, kvn)
+    scratch = (pltpu.VMEM((1280, HD), BF16), pltpu.VMEM((HD, 1280), BF16), pltpu.VMEM((1280, HD), BF16))
+    total = shape((1280, HD), F32)
+    dq_keep, dk, dv = call(
+        first_kernel,
+        (shape((2, 512, HD), F32), total, total),
+        (ids, qd, qd2, *keys),
+        smem=(0,),
+        scratch=scratch,
+    )
+    dq_send, *dkvs, dkvn = call(
+        second_kernel,
+        (shape((2, 512, HD)), shape((256, 256), F32)) + (shape((256, 256)),) * 4,
+        (ids, qd1, qd3, *keys, dk, dv),
+        smem=(0,),
+        scratch=scratch,
     )
     dq_core = swap(dq_send, 1)
     for m in (2, 1, 3):

time: 81.7 us -> 79.3 us (0.971)
  starting transfers between devices: 19.7 us -> 14.9 us
  waiting for transfers between devices: 7.16 us -> 9.48 us
    all_to_all x1 -> x0, starting transfers between devices: 4.19 us -> none  [per_device(): kvs = lax.all_to_all(kv, 'y', 0, 0, tiled=True)]
    ppermute x3 -> x6, waiting for transfers between devices: 5.45 us -> 9.47 us  [swap_y(): return lax.ppermute(x, 'y', [(i, i ^ mask) for i in range(4)])]
    ppermute x5, starting transfers between devices: 12.3 us -> 8.32 us  [swap(): return lax.ppermute(x, QUERY_AXES, [(i, i ^ mask) for i in range(4)])]
    ppermute x3 -> x6, starting transfers between devices: 3.27 us -> 6.59 us  [swap_y(): return lax.ppermute(x, 'y', [(i, i ^ mask) for i in range(4)])]
    all_to_all x1 -> x0, waiting for transfers between devices: 1.7 us -> none  [per_device(): kvs = lax.all_to_all(kv, 'y', 0, 0, tiled=True)]
    pallas_call x6 -> x7, Pallas kernels: 11.2 us -> 11.4 us  [call(): pl.pallas_call(body, out_shape=out_shape, in_specs=[SMEM if i in smem els...]
  transfers between devices with their start and end apart: 9 -> 11, of which waited for: 3 -> 4; matrix products, arithmetic and copies ran while one was open for 1% -> 1% of each run, Pallas kernels for 0% -> 5%
where the time goes in v4:
time: 79.3 us; the launch traced here: 78.2 us
  blocking collectives  40.9 us (52%)
  starting transfers between devices  14.9 us (19%)
  Pallas kernels  11.4 us (14%)
  waiting for transfers between devices  9.48 us (12%)
  local copies, waits for them, and re-layouts  0.85 us (1%)
    all_to_all x1, blocking collectives, per_device(): got = lax.all_to_all(packed, HEAD_AXES, 0, 0, tiled=True)  26.7 us
    all_to_all x1, blocking collectives, per_device(): back = lax.all_to_all(back, BACK_AXES, 0, 0, tiled=True)  14.2 us
    pallas_call x7, Pallas kernels, call(): pl.pallas_call(body, out_shape=out_shape, in_specs=[SMEM if i in smem els...  11.4 us
    ppermute x6, waiting for transfers between devices, swap_y(): return lax.ppermute(x, 'y', [(i, i ^ mask) for i in range(4)])  9.47 us
    ppermute x5, starting transfers between devices, swap(): return lax.ppermute(x, QUERY_AXES, [(i, i ^ mask) for i in range(4)])  8.32 us
    ppermute x6, starting transfers between devices, swap_y(): return lax.ppermute(x, 'y', [(i, i ^ mask) for i in range(4)])  6.59 us
  transfers between devices with their start and end apart: 11, of which 4 were waited for; matrix products, arithmetic and copies ran while one was open for 1% of the time, Pallas kernels for 5%

profile of v4, /device:TPU:1, one launch (start us, length us, event | category | flops | bytes accessed | tf_op | source)
XLA Modules:
  0.0 78.2 jit_solution(15411291991172506167)
XLA Ops:
  0.6 1.3 %shard_map.103 = bf16[16,136,128]{2,1,0:T(8,128)(2,1)S(1)} custom-call(bf16[32,2048]{1,0:T(8,128)(2,1)} %q_in.1, bf16[32,2048]{1,0:T(8,128)(2,1)} %k_in.1, bf16[32,2048]{1,0:T(8,128)(2,1)} %v_in.1, bf16[32,2048]{1,0:T(8,128)(2,1)} %o_in.1, bf16[32,2048]{1,0:T(8,128)(2,1)} %g_in.1, f32[4,128]{1,0:T(4,128)} %bitcast.4), custom_call_target="tpu_custom_call" | custom-call | tf_op jit(solution)/shard_map/pallas_call | solution.py:42
  2.0 0.0 copy-start
  2.0 26.7 %all_to_all.10.got_ref = bf16[16,136,128]{2,1,0:T(8,128)(2,1)S(1)} all-to-all(bf16[16,136,128]{2,1,0:T(8,128)(2,1)S(1)} %shard_map.103), channel_id=1, replica_groups=mesh['y'=4,'zh'=2,'xh'=2,'xl'=2,'c'=2,'zl'=4] {'zl','zh','xl'}, dimensions={0} | all-to-all | bytes 1114112 | tf_op jit(solution)/shard_map/all_to_all | solution.py:250
  28.7 0.0 copy-done
  28.7 0.9 %shard_map.104 = (bf16[528,256]{1,0:T(8,128)(2,1)S(1)}, bf16[256,256]{1,0:T(8,128)(2,1)S(1)}, bf16[256,256]{1,0:T(8,128)(2,1)S(1)}) custom-call(bf16[16,136,128]{2,1,0:T(8,128)(2,1)S(1)} %all_to_all.10.got_ref, s32[64,128]{1,0:T(8,128)S(1)} %bitcast.2), custom_call_target="tpu_custom_call" | custom-call | tf_op jit(solution)/shard_map/pallas_call | solution.py:42
  29.6 2.5 %collective-permute-start = (bf16[528,256]{1,0:T(8,128)(2,1)S(1)}, bf16[528,256]{1,0:T(8,128)(2,1)S(1)}, u32[]{:S(2)}, u32[]{:S(2)}) collective-permute-start(bf16[528,256]{1,0:T(8,128)(2,1)S(1)} %get-tuple-element.24.qd0), channel_id=1, source_target_pairs={{0,16},{4,20},{16,0},{20,4},{1,17},{5,21},{17,1},{21,5},{2,18},{6,... | collective-permute-start | bytes 811016 | tf_op jit(solution)/shard_map/ppermute | solution.py:227
  32.0 2.7 %collective-permute-start.3 = (bf16[256,256]{1,0:T(8,128)(2,1)S(1)}, bf16[256,256]{1,0:T(8,128)(2,1)S(1)}, u32[]{:S(2)}, u32[]{:S(2)}) collective-permute-start(bf16[256,256]{1,0:T(8,128)(2,1)S(1)} %get-tuple-element.22.kv0), channel_id=1, source_target_pairs={{0,192},{64,128},{128,64},{192,0},{1,193},{65,129},{129,65},{193,1... | collective-permute-start | bytes 393224 | tf_op jit(solution)/shard_map/ppermute | solution.py:231
  34.8 0.3 collective-permute-start.2
  35.1 0.2 collective-permute-start.1
  35.4 0.8 %slice.3.ids_ref = s32[16]{0:T(128)S(1)} slice(s32[8192]{0:T(1024)} %param.14), slice={[0:8192:512]} | slice | bytes 128 | tf_op jit(solution)/shard_map/slice | solution.py:240
  36.2 1.9 %collective-permute-done.3.kv3 = bf16[256,256]{1,0:T(8,128)(2,1)S(1)} collective-permute-done((bf16[256,256]{1,0:T(8,128)(2,1)S(1)}, bf16[256,256]{1,0:T(8,128)(2,1)S(1)}, u32[]{:S(2)}, u32[]{:S(2)}) %collective-permute-start.3) | collective-permute-done | bytes 131104 | tf_op jit(solution)/shard_map/ppermute | solution.py:231
  38.1 2.1 %collective-permute-done.2.kv2 = bf16[256,256]{1,0:T(8,128)(2,1)S(1)} collective-permute-done((bf16[256,256]{1,0:T(8,128)(2,1)S(1)}, bf16[256,256]{1,0:T(8,128)(2,1)S(1)}, u32[]{:S(2)}, u32[]{:S(2)}) %collective-permute-start.2) | collective-permute-done | bytes 131104 | tf_op jit(solution)/shard_map/ppermute | solution.py:231
  40.2 0.0 collective-permute-done.1.kv1
  40.2 0.0 collective-permute-done.qd2
  40.2 4.6 %collective-permute-start.4 = (bf16[528,256]{1,0:T(8,128)(2,1)S(1)}, bf16[528,256]{1,0:T(8,128)(2,1)S(1)}, u32[]{:S(2)}, u32[]{:S(2)}) collective-permute-start(bf16[528,256]{1,0:T(8,128)(2,1)S(1)} %get-tuple-element.24.qd0), channel_id=1, source_target_pairs={{0,4},{4,0},{16,20},{20,16},{1,5},{5,1},{17,21},{21,17},{2,6},{6,2... | collective-permute-start | bytes 811016 | tf_op jit(solution)/shard_map/ppermute | solution.py:227
  44.9 0.1 collective-permute-start.5
  45.0 3.6 %shard_map.105 = (f32[2,512,128]{2,1,0:T(8,128)S(1)}, f32[1280,128]{1,0:T(8,128)S(1)}, f32[1280,128]{1,0:T(8,128)S(1)}) custom-call(s32[16]{0:T(128)S(1)} %slice.3.ids_ref, bf16[528,256]{1,0:T(8,128)(2,1)S(1)} %get-tuple-element.24.qd0, bf16[528,256]{1,0:T(8,128)(2,1)S(1)} %collective-permute-done.qd2, bf16[256,256]{1,0:T(8,128)(2,1)S(1)} %get-tuple-element.22.kv0, ...), custom_call_target="tpu_custom_call" | custom-call | tf_op jit(solution)/shard_map/pallas_call | solution.py:42
  48.6 0.0 collective-permute-done.4.qd1
  48.6 0.0 collective-permute-done.5.qd3
  48.6 3.6 %shard_map.106 = (bf16[2,512,128]{2,1,0:T(8,128)(2,1)S(1)}, f32[256,256]{1,0:T(8,128)S(1)}, bf16[256,256]{1,0:T(8,128)(2,1)S(1)}, bf16[256,256]{1,0:T(8,128)(2,1...) custom-call(s32[16]{0:T(128)S(1)} %slice.3.ids_ref, bf16[528,256]{1,0:T(8,128)(2,1)S(1)} %collective-permute-done.4.qd1, ...), custom_call_target="tpu_custom_call" | custom-call | tf_op jit(solution)/shard_map/pallas_call | solution.py:42
  52.2 0.5 collective-permute-start.6
  52.7 1.7 %collective-permute-start.8 = (bf16[256,256]{1,0:T(8,128)(2,1)S(1)}, bf16[256,256]{1,0:T(8,128)(2,1)S(1)}, u32[]{:S(2)}, u32[]{:S(2)}) collective-permute-start(bf16[256,256]{1,0:T(8,128)(2,1)S(1)} %get-tuple-element.35), channel_id=1, source_target_pairs={{0,192},{64,128},{128,64},{192,0},{1,193},{65,129},{129,65},{193,1... | collective-permute-start | bytes 393224 | tf_op jit(solution)/shard_map/ppermute | solution.py:231
  54.4 0.3 collective-permute-start.9
  54.8 1.2 %collective-permute-start.10 = (bf16[256,256]{1,0:T(8,128)(2,1)S(1)}, bf16[256,256]{1,0:T(8,128)(2,1)S(1)}, u32[]{:S(2)}, u32[]{:S(2)}) collective-permute-start(bf16[256,256]{1,0:T(8,128)(2,1)S(1)} %get-tuple-element.37), channel_id=1, source_target_pairs={{0,64},{64,0},{128,192},{192,128},{1,65},{65,1},{129,193},{193,129... | collective-permute-start | bytes 393224 | tf_op jit(solution)/shard_map/ppermute | solution.py:231
  56.0 0.0 collective-permute-done.6.got_ref.got_core
  56.0 0.6 collective-permute-start.7
  56.7 4.7 %collective-permute-done.8.dkv1 = bf16[256,256]{1,0:T(8,128)(2,1)S(1)} collective-permute-done((bf16[256,256]{1,0:T(8,128)(2,1)S(1)}, bf16[256,256]{1,0:T(8,128)(2,1)S(1)}, u32[]{:S(2)}, u32[]{:S(2)}) %collective-permute-start.8) | collective-permute-done | bytes 131104 | tf_op jit(solution)/shard_map/ppermute | solution.py:231
  61.3 0.0 collective-permute-done.9.dkv2
  61.3 0.8 %collective-permute-done.10.dkv3 = bf16[256,256]{1,0:T(8,128)(2,1)S(1)} collective-permute-done((bf16[256,256]{1,0:T(8,128)(2,1)S(1)}, bf16[256,256]{1,0:T(8,128)(2,1)S(1)}, u32[]{:S(2)}, u32[]{:S(2)}) %collective-permute-start.10) | collective-permute-done | bytes 131104 | tf_op jit(solution)/shard_map/ppermute | solution.py:231
  62.1 0.0 collective-permute-done.7.got_chip
  62.1 1.1 %shard_map.108 = bf16[16,96,128]{2,1,0:T(8,128)(2,1)S(1)} custom-call(f32[2,512,128]{2,1,0:T(8,128)S(1)} %get-tuple-element.30.keep_ref, bf16[2,512,128]{2,1,0:T(8,128)(2,1)S(1)} %collective-permute-done.6.got_ref.got_core, bf16[512,128]{1,0:T(8,128)(2,1)S(1)} %collective-permute-done.7.got_chip, f32[256,256]{1,0:T(8,128)S(1)} %get-tuple-element.34.dkv0, ...), custom_call_target="tpu_custom_call" | custom-call | tf_op jit(solution)/shard_map/pallas_call | solution.py:42
  63.2 14.2 %all_to_all.11.got_ref = bf16[16,96,128]{2,1,0:T(8,128)(2,1)S(1)} all-to-all(bf16[16,96,128]{2,1,0:T(8,128)(2,1)S(1)} %shard_map.108), channel_id=1, replica_groups=mesh['y'=4,'zh'=2,'xh'=2,'xl'=2,'c'=2,'zl'=4] {'zh','xl','zl'}, dimensions={0} | all-to-all | bytes 786432 | tf_op jit(solution)/shard_map/all_to_all | solution.py:281
  77.4 0.8 %shard_map.109 = (bf16[32,2048]{1,0:T(8,128)(2,1)}, bf16[32,2048]{1,0:T(8,128)(2,1)}, bf16[32,2048]{1,0:T(8,128)(2,1)}) custom-call(bf16[16,96,128]{2,1,0:T(8,128)(2,1)S(1)} %all_to_all.11.got_ref), custom_call_target="tpu_custom_call" | custom-call | tf_op jit(solution)/shard_map/pallas_call | solution.py:42
  (1 shorter events, 0.0 us)
Async XLA Ops:
  2.0 26.7 %copy-start = (s32[8192]{0:T(1024)S(1)}, s32[8192]{0:T(1024)}, u32[]{:S(2)}) copy-start(s32[8192]{0:T(1024)} %param.15) | copy-start | bytes 98308
  29.6 10.7 %collective-permute-start = (bf16[528,256]{1,0:T(8,128)(2,1)S(1)}, bf16[528,256]{1,0:T(8,128)(2,1)S(1)}, u32[]{:S(2)}, u32[]{:S(2)}) collective-permute-start(bf16[528,256]{1,0:T(8,128)(2,1)S(1)} %get-tuple-element.24.qd0), channel_id=1, source_target_pairs={{0,16},{4,20},{16,0},{20,4},{1,17},{5,21},{17,1},{21,5},{2,18},{6,... | collective-permute-start | bytes 811016 | tf_op jit(solution)/shard_map/ppermute | solution.py:227
  32.0 6.1 %collective-permute-start.3 = (bf16[256,256]{1,0:T(8,128)(2,1)S(1)}, bf16[256,256]{1,0:T(8,128)(2,1)S(1)}, u32[]{:S(2)}, u32[]{:S(2)}) collective-permute-start(bf16[256,256]{1,0:T(8,128)(2,1)S(1)} %get-tuple-element.22.kv0), channel_id=1, source_target_pairs={{0,192},{64,128},{128,64},{192,0},{1,193},{65,129},{129,65},{193,1... | collective-permute-start | bytes 393224 | tf_op jit(solution)/shard_map/ppermute | solution.py:231
  34.8 5.4 %collective-permute-start.2 = (bf16[256,256]{1,0:T(8,128)(2,1)S(1)}, bf16[256,256]{1,0:T(8,128)(2,1)S(1)}, u32[]{:S(2)}, u32[]{:S(2)}) collective-permute-start(bf16[256,256]{1,0:T(8,128)(2,1)S(1)} %get-tuple-element.22.kv0), channel_id=1, source_target_pairs={{0,128},{64,192},{128,0},{192,64},{1,129},{65,193},{129,1},{193,65... | collective-permute-start | bytes 393224 | tf_op jit(solution)/shard_map/ppermute | solution.py:231
  35.1 5.1 %collective-permute-start.1 = (bf16[256,256]{1,0:T(8,128)(2,1)S(1)}, bf16[256,256]{1,0:T(8,128)(2,1)S(1)}, u32[]{:S(2)}, u32[]{:S(2)}) collective-permute-start(bf16[256,256]{1,0:T(8,128)(2,1)S(1)} %get-tuple-element.22.kv0), channel_id=1, source_target_pairs={{0,64},{64,0},{128,192},{192,128},{1,65},{65,1},{129,193},{193,129... | collective-permute-start | bytes 393224 | tf_op jit(solution)/shard_map/ppermute | solution.py:231
  40.2 8.4 %collective-permute-start.4 = (bf16[528,256]{1,0:T(8,128)(2,1)S(1)}, bf16[528,256]{1,0:T(8,128)(2,1)S(1)}, u32[]{:S(2)}, u32[]{:S(2)}) collective-permute-start(bf16[528,256]{1,0:T(8,128)(2,1)S(1)} %get-tuple-element.24.qd0), channel_id=1, source_target_pairs={{0,4},{4,0},{16,20},{20,16},{1,5},{5,1},{17,21},{21,17},{2,6},{6,2... | collective-permute-start | bytes 811016 | tf_op jit(solution)/shard_map/ppermute | solution.py:227
  44.9 3.7 %collective-permute-start.5 = (bf16[528,256]{1,0:T(8,128)(2,1)S(1)}, bf16[528,256]{1,0:T(8,128)(2,1)S(1)}, u32[]{:S(2)}, u32[]{:S(2)}) collective-permute-start(bf16[528,256]{1,0:T(8,128)(2,1)S(1)} %collective-permute-done.qd2), channel_id=1, source_target_pairs={{0,4},{4,0},{16,20},{20,16},{1,5},{5,1},{17,21},{21,17},{2,6},{6,2... | collective-permute-start | bytes 811016 | tf_op jit(solution)/shard_map/ppermute | solution.py:227
  52.2 3.8 %collective-permute-start.6 = (bf16[2,512,128]{2,1,0:T(8,128)(2,1)S(1)}, bf16[2,512,128]{2,1,0:T(8,128)(2,1)S(1)}, u32[]{:S(2)}, u32[]{:S(2)}) collective-permute-start(bf16[2,512,128]{2,1,0:T(8,128)(2,1)S(1)} %get-tuple-element.33), channel_id=1, source_target_pairs={{0,4},{4,0},{16,20},{20,16},{1,5},{5,1},{17,21},{21,17},{2,6},{6,2... | collective-permute-start | bytes 786440 | tf_op jit(solution)/shard_map/ppermute | solution.py:227
  52.7 8.6 %collective-permute-start.8 = (bf16[256,256]{1,0:T(8,128)(2,1)S(1)}, bf16[256,256]{1,0:T(8,128)(2,1)S(1)}, u32[]{:S(2)}, u32[]{:S(2)}) collective-permute-start(bf16[256,256]{1,0:T(8,128)(2,1)S(1)} %get-tuple-element.35), channel_id=1, source_target_pairs={{0,192},{64,128},{128,64},{192,0},{1,193},{65,129},{129,65},{193,1... | collective-permute-start | bytes 393224 | tf_op jit(solution)/shard_map/ppermute | solution.py:231
  54.4 6.9 %collective-permute-start.9 = (bf16[256,256]{1,0:T(8,128)(2,1)S(1)}, bf16[256,256]{1,0:T(8,128)(2,1)S(1)}, u32[]{:S(2)}, u32[]{:S(2)}) collective-permute-start(bf16[256,256]{1,0:T(8,128)(2,1)S(1)} %get-tuple-element.36), channel_id=1, source_target_pairs={{0,128},{64,192},{128,0},{192,64},{1,129},{65,193},{129,1},{193,65... | collective-permute-start | bytes 393224 | tf_op jit(solution)/shard_map/ppermute | solution.py:231
  54.8 7.3 %collective-permute-start.10 = (bf16[256,256]{1,0:T(8,128)(2,1)S(1)}, bf16[256,256]{1,0:T(8,128)(2,1)S(1)}, u32[]{:S(2)}, u32[]{:S(2)}) collective-permute-start(bf16[256,256]{1,0:T(8,128)(2,1)S(1)} %get-tuple-element.37), channel_id=1, source_target_pairs={{0,64},{64,0},{128,192},{192,128},{1,65},{65,1},{129,193},{193,129... | collective-permute-start | bytes 393224 | tf_op jit(solution)/shard_map/ppermute | solution.py:231
  56.0 6.1 %collective-permute-start.7 = (bf16[512,128]{1,0:T(8,128)(2,1)S(1)}, bf16[512,128]{1,0:T(8,128)(2,1)S(1)}, u32[]{:S(2)}, u32[]{:S(2)}) collective-permute-start(bf16[512,128]{1,0:T(8,128)(2,1)S(1)} %shard_map.107), channel_id=1, source_target_pairs={{0,16},{4,20},{16,0},{20,4},{1,17},{5,21},{17,1},{21,5},{2,18},{6,... | collective-permute-start | bytes 393224 | tf_op jit(solution)/shard_map/ppermute | solution.py:227

commit v5 on v4

--- a/solution.py
+++ b/solution.py
@@ -126,8 +126,8 @@
     qd_ref[512:528, :] = jnp.concatenate(halves, axis=0).astype(BF16)
 
 
-def load_keys(clean, noisy_ref, k_all, kt_all, v_all):
-    for m, ref in enumerate((*clean, noisy_ref)):
+def load_keys(pieces, k_all, kt_all, v_all):
+    for m, ref in enumerate(pieces):
         rows = slice(256 * m, 256 * m + 256)
         k = ref[:, :HD]
         k_all[rows, :] = k
@@ -135,7 +135,7 @@
         kt_all[:, rows] = k.astype(F32).T.astype(BF16)
 
 
-def attend(ids_ref, qd_ref, other, k_all, kt_all, v_all):
+def attend(ids_ref, qd_ref, other, masks, noisy, k_all, kt_all, v_all):
     y, xh = lax.axis_index("y"), lax.axis_index("xh")
     stats = qd_ref[512:528, :].astype(F32)
     lse = jnp.concatenate([stats[0:1] + stats[1:2], stats[8:9] + stats[9:10]], axis=1) * LOG2E
@@ -144,45 +144,61 @@
     clean, second = lane // 128 % 2 == 1, lane >= 256
     own_ids = [ids_ref[(y * 2 + zh) * 2 + (xh ^ other)] for zh in range(2)]
     limits = []
-    for n in range(8):
-        key_id = ids_ref[((y ^ (n // 2)) * 2 + n % 2) * 2 + xh]
-        noisy_off, clean_off = (
-            jnp.where(second, *(jnp.where(hit, 0.0, OFF) for hit in hits))
-            for hits in ([key_id < i for i in own_ids[::-1]], [key_id <= i for i in own_ids[::-1]])
-        )
-        limits.append(lse + jnp.where(clean, clean_off, noisy_off))
-    if not other:
+    for mask in masks:
+        for zh in range(2):
+            key_id = ids_ref[((y ^ mask) * 2 + zh) * 2 + xh]
+            noisy_off, clean_off = (
+                jnp.where(second, *(jnp.where(hit, 0.0, OFF) for hit in hits))
+                for hits in ([key_id < i for i in own_ids[::-1]], [key_id <= i for i in own_ids[::-1]])
+            )
+            limits.append(lse + jnp.where(clean, clean_off, noisy_off))
+    if noisy:
         limits.append(lse + jnp.where(clean | second, OFF, 0.0))
         limits.append(lse + jnp.where(clean | ~second, OFF, 0.0))
-    last = 128 * len(limits)
     q, g = qd_ref[:512, :HD], qd_ref[:512, HD:]
-    scores = contract(k_all[:last, :], q, 1, 1)
+    scores = contract(k_all, q, 1, 1)
     weights = jnp.concatenate(
         [jnp.exp2(scores[128 * i : 128 * i + 128] * (SCALE * LOG2E) - row) for i, row in enumerate(limits)], axis=0
     )
-    dweights = contract(v_all[:last, :], g, 1, 1)
+    dweights = contract(v_all, g, 1, 1)
     dscores = (weights * (dweights - delta)).astype(BF16)
     dv = contract(weights.astype(BF16), g, 1, 0)
     dk = contract(dscores, q, 1, 0)
-    return dk, dv, contract(kt_all[:, :last], dscores, 1, 0).T * SCALE
-
-
-def first_kernel(ids_ref, qd0, qd2, kv0, kv1, kv2, kv3, kvn_ref, dq_ref, dk_ref, dv_ref, k_all, kt_all, v_all):
-    load_keys((kv0, kv1, kv2, kv3), kvn_ref, k_all, kt_all, v_all)
-    dk_ref[...], dv_ref[...], dq_ref[0] = attend(ids_ref, qd0, 0, k_all, kt_all, v_all)
-    dk, dv, dq_ref[1] = attend(ids_ref, qd2, 1, k_all, kt_all, v_all)
-    dk_ref[:1024, :] += dk
-    dv_ref[:1024, :] += dv
+    return dk, dv, contract(kt_all, dscores, 1, 0).T * SCALE
+
+
+def own_kernel(ids_ref, qd0, kv0, kvn_ref, dq_ref, dk_ref, dv_ref, k_all, kt_all, v_all):
+    load_keys((kv0, kvn_ref), k_all, kt_all, v_all)
+    dk_ref[...], dv_ref[...], dq_ref[...] = attend(
+        ids_ref, qd0, 0, (0,), True, k_all[...], kt_all[...], v_all[...]
+    )
+
+
+def first_kernel(
+    ids_ref, qd0, qd2, kv0, kv1, kv2, kv3, own_dq, own_dk, own_dv, dq_ref, dk_ref, dv_ref, k_all, kt_all, v_all
+):
+    load_keys((kv0, kv1, kv2, kv3), k_all, kt_all, v_all)
+    far_dk, far_dv, dq_ref[1] = attend(ids_ref, qd2, 1, range(4), False, k_all[...], kt_all[...], v_all[...])
+    dk, dv, dq = attend(
+        ids_ref, qd0, 0, (1, 2, 3), False, k_all[256:, :], kt_all[:, 256:], v_all[256:, :]
+    )
+    dq_ref[0] = own_dq[...] + dq
+    for total, own, near, far in ((dk_ref, own_dk, dk, far_dk), (dv_ref, own_dv, dv, far_dv)):
+        total[:256, :] = own[:256, :] + far[:256]
+        total[256:1024, :] = near + far[256:]
+        total[1024:, :] = own[256:, :]
 
 
 def second_kernel(
     ids_ref, qd1, qd3, kv0, kv1, kv2, kv3, kvn_ref, dk_ref, dv_ref,
     dq_ref, dkv0, dkv1, dkv2, dkv3, dkvn, k_all, kt_all, v_all,
 ):
-    load_keys((kv0, kv1, kv2, kv3), kvn_ref, k_all, kt_all, v_all)
-    near_dk, near_dv, dq = attend(ids_ref, qd1, 0, k_all, kt_all, v_all)
+    load_keys((kv0, kv1, kv2, kv3, kvn_ref), k_all, kt_all, v_all)
+    near_dk, near_dv, dq = attend(ids_ref, qd1, 0, range(4), True, k_all[...], kt_all[...], v_all[...])
     dq_ref[0] = dq.astype(BF16)
-    far_dk, far_dv, dq = attend(ids_ref, qd3, 1, k_all, kt_all, v_all)
+    far_dk, far_dv, dq = attend(
+        ids_ref, qd3, 1, range(4), False, k_all[:1024, :], kt_all[:, :1024], v_all[:1024, :]
+    )
     dq_ref[1] = dq.astype(BF16)
     for m, ref in enumerate((dkv0, dkv1, dkv2, dkv3, dkvn)):
         rows = slice(256 * m, 256 * m + 256)
@@ -252,26 +268,30 @@
         sort_kernel, (shape((528, 256)), shape((256, 256)), shape((256, 256))), (got, copies)
     )
     qd2 = swap(qd, 2)
-    kv1, kv2, kv3 = (swap_y(kv, m) for m in (1, 2, 3))
-    qd2, kv1, kv2, kv3, ids, qd = lax.optimization_barrier((qd2, kv1, kv2, kv3, ids, qd))
+    kv3, kv2, kv1 = (swap_y(kv, m) for m in (3, 2, 1))
+    def scratch(count):
+        return pltpu.VMEM((count, HD), BF16), pltpu.VMEM((HD, count), BF16), pltpu.VMEM((count, HD), BF16)
+
+    part = shape((512, HD), F32)
+    own = call(own_kernel, (part,) * 3, (ids, qd, kv, kvn), smem=(0,), scratch=scratch(512))
+    qd2, kv3, kv2, kv1, ids, qd, *own = lax.optimization_barrier((qd2, kv3, kv2, kv1, ids, qd, *own))
     qd1 = swap(qd, 1)
     qd3 = swap(qd2, 1)
-    keys = (kv, kv1, kv2, kv3, kvn)
-    scratch = (pltpu.VMEM((1280, HD), BF16), pltpu.VMEM((HD, 1280), BF16), pltpu.VMEM((1280, HD), BF16))
+    keys = (kv, kv1, kv2, kv3)
     total = shape((1280, HD), F32)
     dq_keep, dk, dv = call(
         first_kernel,
         (shape((2, 512, HD), F32), total, total),
-        (ids, qd, qd2, *keys),
+        (ids, qd, qd2, *keys, *own),
         smem=(0,),
-        scratch=scratch,
+        scratch=scratch(1024),
     )
     dq_send, *dkvs, dkvn = call(
         second_kernel,
         (shape((2, 512, HD)), shape((256, 256), F32)) + (shape((256, 256)),) * 4,
-        (ids, qd1, qd3, *keys, dk, dv),
+        (ids, qd1, qd3, *keys, kvn, dk, dv),
         smem=(0,),
-        scratch=scratch,
+        scratch=scratch(1280),
     )
     dq_core = swap(dq_send, 1)
     for m in (2, 1, 3):

time: 79.3 us -> 78.7 us (level)
  waiting for transfers between devices: 9.48 us -> 8.03 us
  Pallas kernels: 11.4 us -> 12.2 us
    ppermute x6, waiting for transfers between devices: 9.47 us -> 8.02 us  [swap_y(): return lax.ppermute(x, 'y', [(i, i ^ mask) for i in range(4)])]
    pallas_call x7 -> x8, Pallas kernels: 11.4 us -> 12.2 us  [call(): pl.pallas_call(body, out_shape=out_shape, in_specs=[SMEM if i in smem els...]
  transfers between devices with their start and end apart: 11 -> 11, of which waited for: 4 -> 4; matrix products, arithmetic and copies ran while one was open for 1% -> 1% of each run, Pallas kernels for 5% -> 6%
where the time goes in v5:
time: 78.7 us; the launch traced here: 77.6 us
  blocking collectives  40.9 us (52%)
  starting transfers between devices  14.9 us (19%)
  Pallas kernels  12.2 us (16%)
  waiting for transfers between devices  8.03 us (10%)
  local copies, waits for them, and re-layouts  0.85 us (1%)
    all_to_all x1, blocking collectives, per_device(): got = lax.all_to_all(packed, HEAD_AXES, 0, 0, tiled=True)  26.7 us
    all_to_all x1, blocking collectives, per_device(): back = lax.all_to_all(back, BACK_AXES, 0, 0, tiled=True)  14.2 us
    pallas_call x8, Pallas kernels, call(): pl.pallas_call(body, out_shape=out_shape, in_specs=[SMEM if i in smem els...  12.2 us
    ppermute x5, starting transfers between devices, swap(): return lax.ppermute(x, QUERY_AXES, [(i, i ^ mask) for i in range(4)])  8.33 us
    ppermute x6, waiting for transfers between devices, swap_y(): return lax.ppermute(x, 'y', [(i, i ^ mask) for i in range(4)])  8.02 us
    ppermute x6, starting transfers between devices, swap_y(): return lax.ppermute(x, 'y', [(i, i ^ mask) for i in range(4)])  6.59 us
  transfers between devices with their start and end apart: 11, of which 4 were waited for; matrix products, arithmetic and copies ran while one was open for 1% of the time, Pallas kernels for 6%

profile of v5, /device:TPU:1, one launch (start us, length us, event | category | flops | bytes accessed | tf_op | source)
XLA Modules:
  0.0 77.6 jit_solution(9306498309030310111)
XLA Ops:
  0.6 1.3 %shard_map.103 = bf16[16,136,128]{2,1,0:T(8,128)(2,1)S(1)} custom-call(bf16[32,2048]{1,0:T(8,128)(2,1)} %q_in.1, bf16[32,2048]{1,0:T(8,128)(2,1)} %k_in.1, bf16[32,2048]{1,0:T(8,128)(2,1)} %v_in.1, bf16[32,2048]{1,0:T(8,128)(2,1)} %o_in.1, bf16[32,2048]{1,0:T(8,128)(2,1)} %g_in.1, f32[4,128]{1,0:T(4,128)} %bitcast.4), custom_call_target="tpu_custom_call" | custom-call | tf_op jit(solution)/shard_map/pallas_call | solution.py:42
  2.0 0.0 copy-start
  2.0 26.7 %all_to_all.10.got_ref = bf16[16,136,128]{2,1,0:T(8,128)(2,1)S(1)} all-to-all(bf16[16,136,128]{2,1,0:T(8,128)(2,1)S(1)} %shard_map.103), channel_id=1, replica_groups=mesh['y'=4,'zh'=2,'xh'=2,'xl'=2,'c'=2,'zl'=4] {'zl','zh','xl'}, dimensions={0} | all-to-all | bytes 1114112 | tf_op jit(solution)/shard_map/all_to_all | solution.py:266
  28.7 0.0 copy-done
  28.7 0.9 %shard_map.104 = (bf16[528,256]{1,0:T(8,128)(2,1)S(1)}, bf16[256,256]{1,0:T(8,128)(2,1)S(1)}, bf16[256,256]{1,0:T(8,128)(2,1)S(1)}) custom-call(bf16[16,136,128]{2,1,0:T(8,128)(2,1)S(1)} %all_to_all.10.got_ref, s32[64,128]{1,0:T(8,128)S(1)} %bitcast.2), custom_call_target="tpu_custom_call" | custom-call | tf_op jit(solution)/shard_map/pallas_call | solution.py:42
  29.6 2.5 %collective-permute-start = (bf16[528,256]{1,0:T(8,128)(2,1)S(1)}, bf16[528,256]{1,0:T(8,128)(2,1)S(1)}, u32[]{:S(2)}, u32[]{:S(2)}) collective-permute-start(bf16[528,256]{1,0:T(8,128)(2,1)S(1)} %get-tuple-element.34.qd0), channel_id=1, source_target_pairs={{0,16},{4,20},{16,0},{20,4},{1,17},{5,21},{17,1},{21,5},{2,18},{6,... | collective-permute-start | bytes 811016 | tf_op jit(solution)/shard_map/ppermute | solution.py:243
  32.0 2.7 %collective-permute-start.1 = (bf16[256,256]{1,0:T(8,128)(2,1)S(1)}, bf16[256,256]{1,0:T(8,128)(2,1)S(1)}, u32[]{:S(2)}, u32[]{:S(2)}) collective-permute-start(bf16[256,256]{1,0:T(8,128)(2,1)S(1)} %get-tuple-element.28.kv0), channel_id=1, source_target_pairs={{0,192},{64,128},{128,64},{192,0},{1,193},{65,129},{129,65},{193,1... | collective-permute-start | bytes 393224 | tf_op jit(solution)/shard_map/ppermute | solution.py:247
  34.8 0.3 collective-permute-start.2
  35.1 0.2 collective-permute-start.3
  35.4 0.8 %slice.3.ids_ref = s32[16]{0:T(128)S(1)} slice(s32[8192]{0:T(1024)} %param.14), slice={[0:8192:512]} | slice | bytes 128 | tf_op jit(solution)/shard_map/slice | solution.py:256
  36.2 1.4 %shard_map.105 = (f32[512,128]{1,0:T(8,128)S(1)}, f32[512,128]{1,0:T(8,128)S(1)}, f32[512,128]{1,0:T(8,128)S(1)}) custom-call(s32[16]{0:T(128)S(1)} %slice.3.ids_ref, bf16[528,256]{1,0:T(8,128)(2,1)S(1)} %get-tuple-element.34.qd0, bf16[256,256]{1,0:T(8,128)(2,1)S(1)} %get-tuple-element.28.kv0, bf16[256,256]{1,0:T(8,128)(2,1)S(1)} %get-tuple-element.29.kvn_ref), custom_call_target="tpu_custom_call" | custom-call | tf_op jit(solution)/shard_map/pallas_call | solution.py:42
  37.6 0.5 collective-permute-done.1.kv3
  38.1 2.1 %collective-permute-done.2.kv2 = bf16[256,256]{1,0:T(8,128)(2,1)S(1)} collective-permute-done((bf16[256,256]{1,0:T(8,128)(2,1)S(1)}, bf16[256,256]{1,0:T(8,128)(2,1)S(1)}, u32[]{:S(2)}, u32[]{:S(2)}) %collective-permute-start.2) | collective-permute-done | bytes 131104 | tf_op jit(solution)/shard_map/ppermute | solution.py:247
  40.2 0.0 collective-permute-done.3.kv1
  40.2 0.0 collective-permute-done.qd2
  40.2 4.6 %collective-permute-start.4 = (bf16[528,256]{1,0:T(8,128)(2,1)S(1)}, bf16[528,256]{1,0:T(8,128)(2,1)S(1)}, u32[]{:S(2)}, u32[]{:S(2)}) collective-permute-start(bf16[528,256]{1,0:T(8,128)(2,1)S(1)} %get-tuple-element.34.qd0), channel_id=1, source_target_pairs={{0,4},{4,0},{16,20},{20,16},{1,5},{5,1},{17,21},{21,17},{2,6},{6,2... | collective-permute-start | bytes 811016 | tf_op jit(solution)/shard_map/ppermute | solution.py:243
  44.9 0.1 collective-permute-start.5
  45.0 3.0 %shard_map.106 = (f32[2,512,128]{2,1,0:T(8,128)S(1)}, f32[1280,128]{1,0:T(8,128)S(1)}, f32[1280,128]{1,0:T(8,128)S(1)}) custom-call(s32[16]{0:T(128)S(1)} %slice.3.ids_ref, bf16[528,256]{1,0:T(8,128)(2,1)S(1)} %get-tuple-element.34.qd0, bf16[528,256]{1,0:T(8,128)(2,1)S(1)} %collective-permute-done.qd2, bf16[256,256]{1,0:T(8,128)(2,1)S(1)} %get-tuple-element.28.kv0, ...), custom_call_target="tpu_custom_call" | custom-call | tf_op jit(solution)/shard_map/pallas_call | solution.py:42
  48.0 0.0 collective-permute-done.4.qd1
  48.0 0.0 collective-permute-done.5.qd3
  48.0 3.6 %shard_map.107 = (bf16[2,512,128]{2,1,0:T(8,128)(2,1)S(1)}, f32[256,256]{1,0:T(8,128)S(1)}, bf16[256,256]{1,0:T(8,128)(2,1)S(1)}, bf16[256,256]{1,0:T(8,128)(2,1...) custom-call(s32[16]{0:T(128)S(1)} %slice.3.ids_ref, bf16[528,256]{1,0:T(8,128)(2,1)S(1)} %collective-permute-done.4.qd1, ...), custom_call_target="tpu_custom_call" | custom-call | tf_op jit(solution)/shard_map/pallas_call | solution.py:42
  51.6 0.5 collective-permute-start.6
  52.1 1.7 %collective-permute-start.8 = (bf16[256,256]{1,0:T(8,128)(2,1)S(1)}, bf16[256,256]{1,0:T(8,128)(2,1)S(1)}, u32[]{:S(2)}, u32[]{:S(2)}) collective-permute-start(bf16[256,256]{1,0:T(8,128)(2,1)S(1)} %get-tuple-element.47), channel_id=1, source_target_pairs={{0,192},{64,128},{128,64},{192,0},{1,193},{65,129},{129,65},{193,1... | collective-permute-start | bytes 393224 | tf_op jit(solution)/shard_map/ppermute | solution.py:247
  53.8 0.3 collective-permute-start.9
  54.2 1.2 %collective-permute-start.10 = (bf16[256,256]{1,0:T(8,128)(2,1)S(1)}, bf16[256,256]{1,0:T(8,128)(2,1)S(1)}, u32[]{:S(2)}, u32[]{:S(2)}) collective-permute-start(bf16[256,256]{1,0:T(8,128)(2,1)S(1)} %get-tuple-element.49), channel_id=1, source_target_pairs={{0,64},{64,0},{128,192},{192,128},{1,65},{65,1},{129,193},{193,129... | collective-permute-start | bytes 393224 | tf_op jit(solution)/shard_map/ppermute | solution.py:247
  55.4 0.0 collective-permute-done.6.got_ref.got_core
  55.5 0.6 collective-permute-start.7
  56.1 4.7 %collective-permute-done.8.dkv1 = bf16[256,256]{1,0:T(8,128)(2,1)S(1)} collective-permute-done((bf16[256,256]{1,0:T(8,128)(2,1)S(1)}, bf16[256,256]{1,0:T(8,128)(2,1)S(1)}, u32[]{:S(2)}, u32[]{:S(2)}) %collective-permute-start.8) | collective-permute-done | bytes 131104 | tf_op jit(solution)/shard_map/ppermute | solution.py:247
  60.7 0.0 collective-permute-done.9.dkv2
  60.7 0.8 %collective-permute-done.10.dkv3 = bf16[256,256]{1,0:T(8,128)(2,1)S(1)} collective-permute-done((bf16[256,256]{1,0:T(8,128)(2,1)S(1)}, bf16[256,256]{1,0:T(8,128)(2,1)S(1)}, u32[]{:S(2)}, u32[]{:S(2)}) %collective-permute-start.10) | collective-permute-done | bytes 131104 | tf_op jit(solution)/shard_map/ppermute | solution.py:247
  61.5 0.0 collective-permute-done.7.got_chip
  61.5 1.1 %shard_map.109 = bf16[16,96,128]{2,1,0:T(8,128)(2,1)S(1)} custom-call(f32[2,512,128]{2,1,0:T(8,128)S(1)} %get-tuple-element.42.keep_ref, bf16[2,512,128]{2,1,0:T(8,128)(2,1)S(1)} %collective-permute-done.6.got_ref.got_core, bf16[512,128]{1,0:T(8,128)(2,1)S(1)} %collective-permute-done.7.got_chip, f32[256,256]{1,0:T(8,128)S(1)} %get-tuple-element.46.dkv0, ...), custom_call_target="tpu_custom_call" | custom-call | tf_op jit(solution)/shard_map/pallas_call | solution.py:42
  62.6 14.2 %all_to_all.11.got_ref = bf16[16,96,128]{2,1,0:T(8,128)(2,1)S(1)} all-to-all(bf16[16,96,128]{2,1,0:T(8,128)(2,1)S(1)} %shard_map.109), channel_id=1, replica_groups=mesh['y'=4,'zh'=2,'xh'=2,'xl'=2,'c'=2,'zl'=4] {'zh','xl','zl'}, dimensions={0} | all-to-all | bytes 786432 | tf_op jit(solution)/shard_map/all_to_all | solution.py:301
  76.8 0.8 %shard_map.110 = (bf16[32,2048]{1,0:T(8,128)(2,1)}, bf16[32,2048]{1,0:T(8,128)(2,1)}, bf16[32,2048]{1,0:T(8,128)(2,1)}) custom-call(bf16[16,96,128]{2,1,0:T(8,128)(2,1)S(1)} %all_to_all.11.got_ref), custom_call_target="tpu_custom_call" | custom-call | tf_op jit(solution)/shard_map/pallas_call | solution.py:42
  (1 shorter events, 0.0 us)
Async XLA Ops:
  2.0 26.7 %copy-start = (s32[8192]{0:T(1024)S(1)}, s32[8192]{0:T(1024)}, u32[]{:S(2)}) copy-start(s32[8192]{0:T(1024)} %param.15) | copy-start | bytes 98308
  29.6 10.7 %collective-permute-start = (bf16[528,256]{1,0:T(8,128)(2,1)S(1)}, bf16[528,256]{1,0:T(8,128)(2,1)S(1)}, u32[]{:S(2)}, u32[]{:S(2)}) collective-permute-start(bf16[528,256]{1,0:T(8,128)(2,1)S(1)} %get-tuple-element.34.qd0), channel_id=1, source_target_pairs={{0,16},{4,20},{16,0},{20,4},{1,17},{5,21},{17,1},{21,5},{2,18},{6,... | collective-permute-start | bytes 811016 | tf_op jit(solution)/shard_map/ppermute | solution.py:243
  32.0 6.1 %collective-permute-start.1 = (bf16[256,256]{1,0:T(8,128)(2,1)S(1)}, bf16[256,256]{1,0:T(8,128)(2,1)S(1)}, u32[]{:S(2)}, u32[]{:S(2)}) collective-permute-start(bf16[256,256]{1,0:T(8,128)(2,1)S(1)} %get-tuple-element.28.kv0), channel_id=1, source_target_pairs={{0,192},{64,128},{128,64},{192,0},{1,193},{65,129},{129,65},{193,1... | collective-permute-start | bytes 393224 | tf_op jit(solution)/shard_map/ppermute | solution.py:247
  34.8 5.4 %collective-permute-start.2 = (bf16[256,256]{1,0:T(8,128)(2,1)S(1)}, bf16[256,256]{1,0:T(8,128)(2,1)S(1)}, u32[]{:S(2)}, u32[]{:S(2)}) collective-permute-start(bf16[256,256]{1,0:T(8,128)(2,1)S(1)} %get-tuple-element.28.kv0), channel_id=1, source_target_pairs={{0,128},{64,192},{128,0},{192,64},{1,129},{65,193},{129,1},{193,65... | collective-permute-start | bytes 393224 | tf_op jit(solution)/shard_map/ppermute | solution.py:247
  35.1 5.1 %collective-permute-start.3 = (bf16[256,256]{1,0:T(8,128)(2,1)S(1)}, bf16[256,256]{1,0:T(8,128)(2,1)S(1)}, u32[]{:S(2)}, u32[]{:S(2)}) collective-permute-start(bf16[256,256]{1,0:T(8,128)(2,1)S(1)} %get-tuple-element.28.kv0), channel_id=1, source_target_pairs={{0,64},{64,0},{128,192},{192,128},{1,65},{65,1},{129,193},{193,129... | collective-permute-start | bytes 393224 | tf_op jit(solution)/shard_map/ppermute | solution.py:247
  40.2 7.8 %collective-permute-start.4 = (bf16[528,256]{1,0:T(8,128)(2,1)S(1)}, bf16[528,256]{1,0:T(8,128)(2,1)S(1)}, u32[]{:S(2)}, u32[]{:S(2)}) collective-permute-start(bf16[528,256]{1,0:T(8,128)(2,1)S(1)} %get-tuple-element.34.qd0), channel_id=1, source_target_pairs={{0,4},{4,0},{16,20},{20,16},{1,5},{5,1},{17,21},{21,17},{2,6},{6,2... | collective-permute-start | bytes 811016 | tf_op jit(solution)/shard_map/ppermute | solution.py:243
  44.9 3.1 %collective-permute-start.5 = (bf16[528,256]{1,0:T(8,128)(2,1)S(1)}, bf16[528,256]{1,0:T(8,128)(2,1)S(1)}, u32[]{:S(2)}, u32[]{:S(2)}) collective-permute-start(bf16[528,256]{1,0:T(8,128)(2,1)S(1)} %collective-permute-done.qd2), channel_id=1, source_target_pairs={{0,4},{4,0},{16,20},{20,16},{1,5},{5,1},{17,21},{21,17},{2,6},{6,2... | collective-permute-start | bytes 811016 | tf_op jit(solution)/shard_map/ppermute | solution.py:243
  51.6 3.8 %collective-permute-start.6 = (bf16[2,512,128]{2,1,0:T(8,128)(2,1)S(1)}, bf16[2,512,128]{2,1,0:T(8,128)(2,1)S(1)}, u32[]{:S(2)}, u32[]{:S(2)}) collective-permute-start(bf16[2,512,128]{2,1,0:T(8,128)(2,1)S(1)} %get-tuple-element.45), channel_id=1, source_target_pairs={{0,4},{4,0},{16,20},{20,16},{1,5},{5,1},{17,21},{21,17},{2,6},{6,2... | collective-permute-start | bytes 786440 | tf_op jit(solution)/shard_map/ppermute | solution.py:243
  52.1 8.6 %collective-permute-start.8 = (bf16[256,256]{1,0:T(8,128)(2,1)S(1)}, bf16[256,256]{1,0:T(8,128)(2,1)S(1)}, u32[]{:S(2)}, u32[]{:S(2)}) collective-permute-start(bf16[256,256]{1,0:T(8,128)(2,1)S(1)} %get-tuple-element.47), channel_id=1, source_target_pairs={{0,192},{64,128},{128,64},{192,0},{1,193},{65,129},{129,65},{193,1... | collective-permute-start | bytes 393224 | tf_op jit(solution)/shard_map/ppermute | solution.py:247
  53.8 6.9 %collective-permute-start.9 = (bf16[256,256]{1,0:T(8,128)(2,1)S(1)}, bf16[256,256]{1,0:T(8,128)(2,1)S(1)}, u32[]{:S(2)}, u32[]{:S(2)}) collective-permute-start(bf16[256,256]{1,0:T(8,128)(2,1)S(1)} %get-tuple-element.48), channel_id=1, source_target_pairs={{0,128},{64,192},{128,0},{192,64},{1,129},{65,193},{129,1},{193,65... | collective-permute-start | bytes 393224 | tf_op jit(solution)/shard_map/ppermute | solution.py:247
  54.2 7.3 %collective-permute-start.10 = (bf16[256,256]{1,0:T(8,128)(2,1)S(1)}, bf16[256,256]{1,0:T(8,128)(2,1)S(1)}, u32[]{:S(2)}, u32[]{:S(2)}) collective-permute-start(bf16[256,256]{1,0:T(8,128)(2,1)S(1)} %get-tuple-element.49), channel_id=1, source_target_pairs={{0,64},{64,0},{128,192},{192,128},{1,65},{65,1},{129,193},{193,129... | collective-permute-start | bytes 393224 | tf_op jit(solution)/shard_map/ppermute | solution.py:247
  55.5 6.1 %collective-permute-start.7 = (bf16[512,128]{1,0:T(8,128)(2,1)S(1)}, bf16[512,128]{1,0:T(8,128)(2,1)S(1)}, u32[]{:S(2)}, u32[]{:S(2)}) collective-permute-start(bf16[512,128]{1,0:T(8,128)(2,1)S(1)} %shard_map.108), channel_id=1, source_target_pairs={{0,16},{4,20},{16,0},{20,4},{1,17},{5,21},{17,1},{21,5},{2,18},{6,... | collective-permute-start | bytes 393224 | tf_op jit(solution)/shard_map/ppermute | solution.py:243

commit v6 on v5

--- a/solution.py
+++ b/solution.py
@@ -209,24 +209,33 @@
         ref[:, HD:] = dv.astype(ref.dtype)
 
 
-def add_kernel(keep_ref, got_ref, out_ref):
-    out_ref[...] = (keep_ref[1] + got_ref[1].astype(F32)).astype(BF16)
-
-
-def unsort_kernel(keep_ref, got_core, got_chip, dkv0, dkv1, dkv2, dkv3, dkvn_ref, copy_ref, out_ref):
-    dq = (keep_ref[0] + got_core[0].astype(F32) + got_chip[...].astype(F32)).astype(BF16)
+def add_kernel(keep_ref, got_ref, send_ref, sum_ref):
+    send_ref[...] = (keep_ref[1] + got_ref[1].astype(F32)).astype(BF16)
+    sum_ref[...] = keep_ref[0] + got_ref[0].astype(F32)
+
+
+def prepare_kernel(dkvn_ref, copy_ref, one_hot_ref, noisy_ref):
+    for j in range(RUNS):
+        one_hot = placing(copy_ref, j).T.astype(BF16)
+        one_hot_ref[j] = one_hot
+        rows = dkvn_ref[64 * j : 64 * j + 64, :]
+        noisy_ref[j] = contract(one_hot, jnp.concatenate([rows, jnp.zeros_like(rows)], axis=0), 1, 0).astype(BF16)
+
+
+def unsort_kernel(sum_ref, got_chip, dkv0, dkv1, dkv2, dkv3, one_hot_ref, noisy_ref, out_ref):
+    dq = (sum_ref[...] + got_chip[...].astype(F32)).astype(BF16)
     dkv = (dkv0[...] + dkv1[...].astype(F32) + dkv2[...].astype(F32) + dkv3[...].astype(F32)).astype(BF16)
     for j in range(RUNS):
         zh, xl = divmod(j, 2)
-        one_hot = placing(copy_ref, j).T.astype(BF16)
         at = 64 * xl
         queries = jnp.concatenate(
             [dq[256 * zh + at : 256 * zh + at + 64], dq[256 * zh + 128 + at : 256 * zh + 192 + at]], axis=0
         )
-        keys = jnp.concatenate(
-            [dkvn_ref[128 * zh + at : 128 * zh + at + 64, :], dkv[128 * zh + at : 128 * zh + at + 64]], axis=0
-        )
-        moved = contract(one_hot, jnp.concatenate([queries, keys], axis=1), 1, 0).astype(BF16)
+        rows = dkv[64 * j : 64 * j + 64]
+        keys = jnp.concatenate([jnp.zeros_like(rows), rows], axis=0)
+        moved = contract(one_hot_ref[j], jnp.concatenate([queries, keys], axis=1), 1, 0)
+        moved_keys = (moved[:, HD:] + noisy_ref[j].astype(F32)).astype(BF16)
+        moved = jnp.concatenate([moved[:, :HD].astype(BF16), moved_keys], axis=1)
         for z in range(4):
             for i in range(3):
                 out_ref[4 * j + z, 32 * i : 32 * i + 32, :] = moved[32 * z : 32 * z + 32, HD * i : HD * (i + 1)]
@@ -296,8 +305,15 @@
     dq_core = swap(dq_send, 1)
     for m in (2, 1, 3):
         dkvs[m] = swap_y(dkvs[m], m)
-    dq_chip = swap(call(add_kernel, shape((512, HD)), (dq_keep, dq_core)), 2)
-    back = call(unsort_kernel, shape((16, 3 * rows, HD)), (dq_keep, dq_core, dq_chip, dkvs[0], dkvs[3], dkvs[2], dkvs[1], dkvn, copies))
+    half, dq_sum = call(add_kernel, (shape((512, HD)), shape((512, HD), F32)), (dq_keep, dq_core))
+    one_hot, noisy = call(
+        prepare_kernel, (shape((RUNS, RUN, RUN)), shape((RUNS, RUN, 256))), (dkvn, copies)
+    )
+    back = call(
+        unsort_kernel,
+        shape((16, 3 * rows, HD)),
+        (dq_sum, swap(half, 2), dkvs[0], dkvs[3], dkvs[2], dkvs[1], one_hot, noisy),
+    )
     back = lax.all_to_all(back, BACK_AXES, 0, 0, tiled=True)
     return call(unpack_kernel, (shape((rows, 16 * HD)),) * 3, (back,))
 

time: 78.7 us -> 77.9 us (0.990)
    pallas_call x8 -> x9, Pallas kernels: 12.2 us -> 12 us  [call(): pl.pallas_call(body, out_shape=out_shape, in_specs=[SMEM if i in smem els...]
  transfers between devices with their start and end apart: 11 -> 11, of which waited for: 4 -> 4; matrix products, arithmetic and copies ran while one was open for 1% -> 1% of each run, Pallas kernels for 6% -> 7%
where the time goes in v6:
time: 77.9 us; the launch traced here: 76.8 us
  blocking collectives  40.9 us (53%)
  starting transfers between devices  14.9 us (19%)
  Pallas kernels  12 us (15%)
  waiting for transfers between devices  7.4 us (9%)
  local copies, waits for them, and re-layouts  0.85 us (1%)
    all_to_all x1, blocking collectives, per_device(): got = lax.all_to_all(packed, HEAD_AXES, 0, 0, tiled=True)  26.7 us
    all_to_all x1, blocking collectives, per_device(): back = lax.all_to_all(back, BACK_AXES, 0, 0, tiled=True)  14.1 us
    pallas_call x9, Pallas kernels, call(): pl.pallas_call(body, out_shape=out_shape, in_specs=[SMEM if i in smem els...  12 us
    ppermute x5, starting transfers between devices, swap(): return lax.ppermute(x, QUERY_AXES, [(i, i ^ mask) for i in range(4)])  8.33 us
    ppermute x6, waiting for transfers between devices, swap_y(): return lax.ppermute(x, 'y', [(i, i ^ mask) for i in range(4)])  7.38 us
    ppermute x6, starting transfers between devices, swap_y(): return lax.ppermute(x, 'y', [(i, i ^ mask) for i in range(4)])  6.59 us
  transfers between devices with their start and end apart: 11, of which 4 were waited for; matrix products, arithmetic and copies ran while one was open for 1% of the time, Pallas kernels for 7%

profile of v6, /device:TPU:1, one launch (start us, length us, event | category | flops | bytes accessed | tf_op | source)
XLA Modules:
  0.0 76.8 jit_solution(9641139371237682170)
XLA Ops:
  0.6 1.3 %shard_map.103 = bf16[16,136,128]{2,1,0:T(8,128)(2,1)S(1)} custom-call(bf16[32,2048]{1,0:T(8,128)(2,1)} %q_in.1, bf16[32,2048]{1,0:T(8,128)(2,1)} %k_in.1, bf16[32,2048]{1,0:T(8,128)(2,1)} %v_in.1, bf16[32,2048]{1,0:T(8,128)(2,1)} %o_in.1, bf16[32,2048]{1,0:T(8,128)(2,1)} %g_in.1, f32[4,128]{1,0:T(4,128)} %bitcast.4), custom_call_target="tpu_custom_call" | custom-call | tf_op jit(solution)/shard_map/pallas_call | solution.py:42
  2.0 0.0 copy-start
  2.0 26.7 %all_to_all.10.got_ref = bf16[16,136,128]{2,1,0:T(8,128)(2,1)S(1)} all-to-all(bf16[16,136,128]{2,1,0:T(8,128)(2,1)S(1)} %shard_map.103), channel_id=1, replica_groups=mesh['y'=4,'zh'=2,'xh'=2,'xl'=2,'c'=2,'zl'=4] {'zl','zh','xl'}, dimensions={0} | all-to-all | bytes 1114112 | tf_op jit(solution)/shard_map/all_to_all | solution.py:275
  28.7 0.0 copy-done
  28.7 0.9 %shard_map.104 = (bf16[528,256]{1,0:T(8,128)(2,1)S(1)}, bf16[256,256]{1,0:T(8,128)(2,1)S(1)}, bf16[256,256]{1,0:T(8,128)(2,1)S(1)}) custom-call(bf16[16,136,128]{2,1,0:T(8,128)(2,1)S(1)} %all_to_all.10.got_ref, s32[64,128]{1,0:T(8,128)S(1)} %bitcast.2), custom_call_target="tpu_custom_call" | custom-call | tf_op jit(solution)/shard_map/pallas_call | solution.py:42
  29.6 2.5 %collective-permute-start = (bf16[528,256]{1,0:T(8,128)(2,1)S(1)}, bf16[528,256]{1,0:T(8,128)(2,1)S(1)}, u32[]{:S(2)}, u32[]{:S(2)}) collective-permute-start(bf16[528,256]{1,0:T(8,128)(2,1)S(1)} %get-tuple-element.38.qd0), channel_id=1, source_target_pairs={{0,16},{4,20},{16,0},{20,4},{1,17},{5,21},{17,1},{21,5},{2,18},{6,... | collective-permute-start | bytes 811016 | tf_op jit(solution)/shard_map/ppermute | solution.py:252
  32.0 2.7 %collective-permute-start.1 = (bf16[256,256]{1,0:T(8,128)(2,1)S(1)}, bf16[256,256]{1,0:T(8,128)(2,1)S(1)}, u32[]{:S(2)}, u32[]{:S(2)}) collective-permute-start(bf16[256,256]{1,0:T(8,128)(2,1)S(1)} %get-tuple-element.32.kv0), channel_id=1, source_target_pairs={{0,192},{64,128},{128,64},{192,0},{1,193},{65,129},{129,65},{193,1... | collective-permute-start | bytes 393224 | tf_op jit(solution)/shard_map/ppermute | solution.py:256
  34.8 0.3 collective-permute-start.2
  35.1 0.2 collective-permute-start.3
  35.4 0.8 %slice.3.ids_ref = s32[16]{0:T(128)S(1)} slice(s32[8192]{0:T(1024)} %param.14), slice={[0:8192:512]} | slice | bytes 128 | tf_op jit(solution)/shard_map/slice | solution.py:265
  36.2 1.4 %shard_map.105 = (f32[512,128]{1,0:T(8,128)S(1)}, f32[512,128]{1,0:T(8,128)S(1)}, f32[512,128]{1,0:T(8,128)S(1)}) custom-call(s32[16]{0:T(128)S(1)} %slice.3.ids_ref, bf16[528,256]{1,0:T(8,128)(2,1)S(1)} %get-tuple-element.38.qd0, bf16[256,256]{1,0:T(8,128)(2,1)S(1)} %get-tuple-element.32.kv0, bf16[256,256]{1,0:T(8,128)(2,1)S(1)} %get-tuple-element.33.kvn_ref), custom_call_target="tpu_custom_call" | custom-call | tf_op jit(solution)/shard_map/pallas_call | solution.py:42
  37.6 0.5 collective-permute-done.1.kv3
  38.1 2.1 %collective-permute-done.2.kv2 = bf16[256,256]{1,0:T(8,128)(2,1)S(1)} collective-permute-done((bf16[256,256]{1,0:T(8,128)(2,1)S(1)}, bf16[256,256]{1,0:T(8,128)(2,1)S(1)}, u32[]{:S(2)}, u32[]{:S(2)}) %collective-permute-start.2) | collective-permute-done | bytes 131104 | tf_op jit(solution)/shard_map/ppermute | solution.py:256
  40.2 0.0 collective-permute-done.3.kv1
  40.2 0.0 collective-permute-done.qd2
  40.2 4.6 %collective-permute-start.4 = (bf16[528,256]{1,0:T(8,128)(2,1)S(1)}, bf16[528,256]{1,0:T(8,128)(2,1)S(1)}, u32[]{:S(2)}, u32[]{:S(2)}) collective-permute-start(bf16[528,256]{1,0:T(8,128)(2,1)S(1)} %get-tuple-element.38.qd0), channel_id=1, source_target_pairs={{0,4},{4,0},{16,20},{20,16},{1,5},{5,1},{17,21},{21,17},{2,6},{6,2... | collective-permute-start | bytes 811016 | tf_op jit(solution)/shard_map/ppermute | solution.py:252
  44.9 0.1 collective-permute-start.5
  45.0 3.0 %shard_map.106 = (f32[2,512,128]{2,1,0:T(8,128)S(1)}, f32[1280,128]{1,0:T(8,128)S(1)}, f32[1280,128]{1,0:T(8,128)S(1)}) custom-call(s32[16]{0:T(128)S(1)} %slice.3.ids_ref, bf16[528,256]{1,0:T(8,128)(2,1)S(1)} %get-tuple-element.38.qd0, bf16[528,256]{1,0:T(8,128)(2,1)S(1)} %collective-permute-done.qd2, bf16[256,256]{1,0:T(8,128)(2,1)S(1)} %get-tuple-element.32.kv0, ...), custom_call_target="tpu_custom_call" | custom-call | tf_op jit(solution)/shard_map/pallas_call | solution.py:42
  48.0 0.0 collective-permute-done.4.qd1
  48.0 0.0 collective-permute-done.5.qd3
  48.0 3.6 %shard_map.107 = (bf16[2,512,128]{2,1,0:T(8,128)(2,1)S(1)}, f32[256,256]{1,0:T(8,128)S(1)}, bf16[256,256]{1,0:T(8,128)(2,1)S(1)}, bf16[256,256]{1,0:T(8,128)(2,1...) custom-call(s32[16]{0:T(128)S(1)} %slice.3.ids_ref, bf16[528,256]{1,0:T(8,128)(2,1)S(1)} %collective-permute-done.4.qd1, ...), custom_call_target="tpu_custom_call" | custom-call | tf_op jit(solution)/shard_map/pallas_call | solution.py:42
  51.6 0.5 collective-permute-start.6
  52.1 1.7 %collective-permute-start.8 = (bf16[256,256]{1,0:T(8,128)(2,1)S(1)}, bf16[256,256]{1,0:T(8,128)(2,1)S(1)}, u32[]{:S(2)}, u32[]{:S(2)}) collective-permute-start(bf16[256,256]{1,0:T(8,128)(2,1)S(1)} %get-tuple-element.53), channel_id=1, source_target_pairs={{0,192},{64,128},{128,64},{192,0},{1,193},{65,129},{129,65},{193,1... | collective-permute-start | bytes 393224 | tf_op jit(solution)/shard_map/ppermute | solution.py:256
  53.8 0.3 collective-permute-start.9
  54.2 1.2 %collective-permute-start.10 = (bf16[256,256]{1,0:T(8,128)(2,1)S(1)}, bf16[256,256]{1,0:T(8,128)(2,1)S(1)}, u32[]{:S(2)}, u32[]{:S(2)}) collective-permute-start(bf16[256,256]{1,0:T(8,128)(2,1)S(1)} %get-tuple-element.55), channel_id=1, source_target_pairs={{0,64},{64,0},{128,192},{192,128},{1,65},{65,1},{129,193},{193,129... | collective-permute-start | bytes 393224 | tf_op jit(solution)/shard_map/ppermute | solution.py:256
  55.4 0.0 collective-permute-done.6.got_ref
  55.4 0.1 shard_map.108
  55.5 0.6 collective-permute-start.7
  56.1 0.6 shard_map.109
  56.7 4.0 %collective-permute-done.8.dkv1 = bf16[256,256]{1,0:T(8,128)(2,1)S(1)} collective-permute-done((bf16[256,256]{1,0:T(8,128)(2,1)S(1)}, bf16[256,256]{1,0:T(8,128)(2,1)S(1)}, u32[]{:S(2)}, u32[]{:S(2)}) %collective-permute-start.8) | collective-permute-done | bytes 131104 | tf_op jit(solution)/shard_map/ppermute | solution.py:256
  60.7 0.0 collective-permute-done.9.dkv2
  60.7 0.8 %collective-permute-done.10.dkv3 = bf16[256,256]{1,0:T(8,128)(2,1)S(1)} collective-permute-done((bf16[256,256]{1,0:T(8,128)(2,1)S(1)}, bf16[256,256]{1,0:T(8,128)(2,1)S(1)}, u32[]{:S(2)}, u32[]{:S(2)}) %collective-permute-start.10) | collective-permute-done | bytes 131104 | tf_op jit(solution)/shard_map/ppermute | solution.py:256
  61.5 0.0 collective-permute-done.7.got_chip
  61.5 0.3 shard_map.110
  61.8 14.1 %all_to_all.11.got_ref = bf16[16,96,128]{2,1,0:T(8,128)(2,1)S(1)} all-to-all(bf16[16,96,128]{2,1,0:T(8,128)(2,1)S(1)} %shard_map.110), channel_id=1, replica_groups=mesh['y'=4,'zh'=2,'xh'=2,'xl'=2,'c'=2,'zl'=4] {'zh','xl','zl'}, dimensions={0} | all-to-all | bytes 786432 | tf_op jit(solution)/shard_map/all_to_all | solution.py:317
  76.0 0.8 %shard_map.111 = (bf16[32,2048]{1,0:T(8,128)(2,1)}, bf16[32,2048]{1,0:T(8,128)(2,1)}, bf16[32,2048]{1,0:T(8,128)(2,1)}) custom-call(bf16[16,96,128]{2,1,0:T(8,128)(2,1)S(1)} %all_to_all.11.got_ref), custom_call_target="tpu_custom_call" | custom-call | tf_op jit(solution)/shard_map/pallas_call | solution.py:42
Async XLA Ops:
  2.0 26.7 %copy-start = (s32[8192]{0:T(1024)S(1)}, s32[8192]{0:T(1024)}, u32[]{:S(2)}) copy-start(s32[8192]{0:T(1024)} %param.15) | copy-start | bytes 98308
  29.6 10.7 %collective-permute-start = (bf16[528,256]{1,0:T(8,128)(2,1)S(1)}, bf16[528,256]{1,0:T(8,128)(2,1)S(1)}, u32[]{:S(2)}, u32[]{:S(2)}) collective-permute-start(bf16[528,256]{1,0:T(8,128)(2,1)S(1)} %get-tuple-element.38.qd0), channel_id=1, source_target_pairs={{0,16},{4,20},{16,0},{20,4},{1,17},{5,21},{17,1},{21,5},{2,18},{6,... | collective-permute-start | bytes 811016 | tf_op jit(solution)/shard_map/ppermute | solution.py:252
  32.0 6.1 %collective-permute-start.1 = (bf16[256,256]{1,0:T(8,128)(2,1)S(1)}, bf16[256,256]{1,0:T(8,128)(2,1)S(1)}, u32[]{:S(2)}, u32[]{:S(2)}) collective-permute-start(bf16[256,256]{1,0:T(8,128)(2,1)S(1)} %get-tuple-element.32.kv0), channel_id=1, source_target_pairs={{0,192},{64,128},{128,64},{192,0},{1,193},{65,129},{129,65},{193,1... | collective-permute-start | bytes 393224 | tf_op jit(solution)/shard_map/ppermute | solution.py:256
  34.8 5.4 %collective-permute-start.2 = (bf16[256,256]{1,0:T(8,128)(2,1)S(1)}, bf16[256,256]{1,0:T(8,128)(2,1)S(1)}, u32[]{:S(2)}, u32[]{:S(2)}) collective-permute-start(bf16[256,256]{1,0:T(8,128)(2,1)S(1)} %get-tuple-element.32.kv0), channel_id=1, source_target_pairs={{0,128},{64,192},{128,0},{192,64},{1,129},{65,193},{129,1},{193,65... | collective-permute-start | bytes 393224 | tf_op jit(solution)/shard_map/ppermute | solution.py:256
  35.1 5.1 %collective-permute-start.3 = (bf16[256,256]{1,0:T(8,128)(2,1)S(1)}, bf16[256,256]{1,0:T(8,128)(2,1)S(1)}, u32[]{:S(2)}, u32[]{:S(2)}) collective-permute-start(bf16[256,256]{1,0:T(8,128)(2,1)S(1)} %get-tuple-element.32.kv0), channel_id=1, source_target_pairs={{0,64},{64,0},{128,192},{192,128},{1,65},{65,1},{129,193},{193,129... | collective-permute-start | bytes 393224 | tf_op jit(solution)/shard_map/ppermute | solution.py:256
  40.2 7.8 %collective-permute-start.4 = (bf16[528,256]{1,0:T(8,128)(2,1)S(1)}, bf16[528,256]{1,0:T(8,128)(2,1)S(1)}, u32[]{:S(2)}, u32[]{:S(2)}) collective-permute-start(bf16[528,256]{1,0:T(8,128)(2,1)S(1)} %get-tuple-element.38.qd0), channel_id=1, source_target_pairs={{0,4},{4,0},{16,20},{20,16},{1,5},{5,1},{17,21},{21,17},{2,6},{6,2... | collective-permute-start | bytes 811016 | tf_op jit(solution)/shard_map/ppermute | solution.py:252
  44.9 3.1 %collective-permute-start.5 = (bf16[528,256]{1,0:T(8,128)(2,1)S(1)}, bf16[528,256]{1,0:T(8,128)(2,1)S(1)}, u32[]{:S(2)}, u32[]{:S(2)}) collective-permute-start(bf16[528,256]{1,0:T(8,128)(2,1)S(1)} %collective-permute-done.qd2), channel_id=1, source_target_pairs={{0,4},{4,0},{16,20},{20,16},{1,5},{5,1},{17,21},{21,17},{2,6},{6,2... | collective-permute-start | bytes 811016 | tf_op jit(solution)/shard_map/ppermute | solution.py:252
  51.6 3.8 %collective-permute-start.6 = (bf16[2,512,128]{2,1,0:T(8,128)(2,1)S(1)}, bf16[2,512,128]{2,1,0:T(8,128)(2,1)S(1)}, u32[]{:S(2)}, u32[]{:S(2)}) collective-permute-start(bf16[2,512,128]{2,1,0:T(8,128)(2,1)S(1)} %get-tuple-element.49), channel_id=1, source_target_pairs={{0,4},{4,0},{16,20},{20,16},{1,5},{5,1},{17,21},{21,17},{2,6},{6,2... | collective-permute-start | bytes 786440 | tf_op jit(solution)/shard_map/ppermute | solution.py:252
  52.1 8.6 %collective-permute-start.8 = (bf16[256,256]{1,0:T(8,128)(2,1)S(1)}, bf16[256,256]{1,0:T(8,128)(2,1)S(1)}, u32[]{:S(2)}, u32[]{:S(2)}) collective-permute-start(bf16[256,256]{1,0:T(8,128)(2,1)S(1)} %get-tuple-element.53), channel_id=1, source_target_pairs={{0,192},{64,128},{128,64},{192,0},{1,193},{65,129},{129,65},{193,1... | collective-permute-start | bytes 393224 | tf_op jit(solution)/shard_map/ppermute | solution.py:256
  53.8 6.9 %collective-permute-start.9 = (bf16[256,256]{1,0:T(8,128)(2,1)S(1)}, bf16[256,256]{1,0:T(8,128)(2,1)S(1)}, u32[]{:S(2)}, u32[]{:S(2)}) collective-permute-start(bf16[256,256]{1,0:T(8,128)(2,1)S(1)} %get-tuple-element.54), channel_id=1, source_target_pairs={{0,128},{64,192},{128,0},{192,64},{1,129},{65,193},{129,1},{193,65... | collective-permute-start | bytes 393224 | tf_op jit(solution)/shard_map/ppermute | solution.py:256
  54.2 7.3 %collective-permute-start.10 = (bf16[256,256]{1,0:T(8,128)(2,1)S(1)}, bf16[256,256]{1,0:T(8,128)(2,1)S(1)}, u32[]{:S(2)}, u32[]{:S(2)}) collective-permute-start(bf16[256,256]{1,0:T(8,128)(2,1)S(1)} %get-tuple-element.55), channel_id=1, source_target_pairs={{0,64},{64,0},{128,192},{192,128},{1,65},{65,1},{129,193},{193,129... | collective-permute-start | bytes 393224 | tf_op jit(solution)/shard_map/ppermute | solution.py:256
  55.5 6.0 %collective-permute-start.7 = (bf16[512,128]{1,0:T(8,128)(2,1)S(1)}, bf16[512,128]{1,0:T(8,128)(2,1)S(1)}, u32[]{:S(2)}, u32[]{:S(2)}) collective-permute-start(bf16[512,128]{1,0:T(8,128)(2,1)S(1)} %get-tuple-element.51), channel_id=1, source_target_pairs={{0,16},{4,20},{16,0},{20,4},{1,17},{5,21},{17,1},{21,5},{2,18},{6,... | collective-permute-start | bytes 393224 | tf_op jit(solution)/shard_map/ppermute | solution.py:252

commit v7 on v6

--- a/solution.py
+++ b/solution.py
@@ -67,7 +67,7 @@
     delta = jnp.concatenate([delta, jnp.zeros((128 - rows, 128), F32)], axis=0).T
     delta_high, delta_low = split_two(delta)
     lse_high, lse_low = split_two(lse_ref[...])
-    row = iota((8, 128), 0)
+    row = iota((16, 128), 0)
     for copy in copies[3:]:
         copy.wait()
     for h in range(16):
@@ -79,7 +79,7 @@
         stats = jnp.where(row == 1, lse_low[j : j + 1], stats)
         stats = jnp.where(row == 2, delta_high[h : h + 1], stats)
         stats = jnp.where(row == 3, delta_low[h : h + 1], stats)
-        out_ref[h, 4 * rows : 4 * rows + 8, :] = stats.astype(BF16)
+        out_ref[h, 4 * rows : 4 * rows + 16, :] = stats.astype(BF16)
 
 
 def placing(copy_ref, j):
@@ -96,7 +96,7 @@
 
 def sort_kernel(got_ref, copy_ref, qd_ref, kv_ref, kvn_ref):
     zl = lax.axis_index("zl")
-    row = iota((8, RUN), 0)
+    row = iota((16, RUN), 0)
     stats = []
     for j in range(RUNS):
         zh, xl = divmod(j, 2)
@@ -110,12 +110,11 @@
         qd_ref[256 * zh + 128 + 64 * xl : 256 * zh + 192 + 64 * xl, :] = moved[HALF:, :256]
         kvn_ref[128 * zh + 64 * xl : 128 * zh + 64 * xl + 64, :] = moved[:HALF, 256:]
         kv_ref[128 * zh + 64 * xl : 128 * zh + 64 * xl + 64, :] = moved[HALF:, 256:]
-        lse = got_ref[4 * zl + j, 128:136, :].astype(F32)
+        lse = got_ref[4 * zl + j, 128:144, :].astype(F32)
         delta = jnp.concatenate(
-            [got_ref[4 * z + j, 128:136, :].astype(F32)[:, :32] for z in range(4)], axis=1
+            [got_ref[4 * z + j, 128:144, :].astype(F32)[:, :32] for z in range(4)], axis=1
         )
-        both = jnp.where(row < 2, lse, delta)
-        both = jnp.concatenate([both, jnp.zeros_like(both)], axis=0).astype(BF16)
+        both = jnp.where(row < 2, lse, delta).astype(BF16)
         stats.append(contract(both, one_hot, 1, 1))
     halves = []
     for zh in range(2):
@@ -267,7 +266,7 @@
     arrays = (query_in, key_in, value_in, saved_out, grad_out, saved_lse.T)
     packed = call(
         pack_kernel,
-        shape((16, 4 * rows + 8, HD)),
+        shape((16, 4 * rows + 16, HD)),
         tuple(pltpu.with_memory_space_constraint(x, pltpu.HBM) for x in arrays),
         hbm=range(6),
         scratch=[pltpu.VMEM(query_in.shape, BF16)] * 5 + [pltpu.VMEM((4, 128), F32), pltpu.SemaphoreType.DMA((6,))],

time: 77.9 us -> 78.6 us (level)
  no operation moved by 1% of the time
where the time goes in v7:
time: 78.6 us; the launch traced here: 77.4 us
  blocking collectives  41.6 us (53%)
  starting transfers between devices  14.9 us (19%)
  Pallas kernels  12 us (15%)
  waiting for transfers between devices  7.37 us (9%)
  local copies, waits for them, and re-layouts  0.85 us (1%)
    all_to_all x1, blocking collectives, per_device(): got = lax.all_to_all(packed, HEAD_AXES, 0, 0, tiled=True)  27.5 us
    all_to_all x1, blocking collectives, per_device(): back = lax.all_to_all(back, BACK_AXES, 0, 0, tiled=True)  14.1 us
    pallas_call x9, Pallas kernels, call(): pl.pallas_call(body, out_shape=out_shape, in_specs=[SMEM if i in smem els...  12 us
    ppermute x5, starting transfers between devices, swap(): return lax.ppermute(x, QUERY_AXES, [(i, i ^ mask) for i in range(4)])  8.28 us
    ppermute x6, waiting for transfers between devices, swap_y(): return lax.ppermute(x, 'y', [(i, i ^ mask) for i in range(4)])  7.36 us
    ppermute x6, starting transfers between devices, swap_y(): return lax.ppermute(x, 'y', [(i, i ^ mask) for i in range(4)])  6.58 us
  transfers between devices with their start and end apart: 11, of which 4 were waited for; matrix products, arithmetic and copies ran while one was open for 1% of the time, Pallas kernels for 7%

profile of v7, /device:TPU:1, one launch (start us, length us, event | category | flops | bytes accessed | tf_op | source)
XLA Modules:
  0.0 77.4 jit_solution(1701265199747101764)
XLA Ops:
  0.6 1.3 %shard_map.103 = bf16[16,144,128]{2,1,0:T(8,128)(2,1)S(1)} custom-call(bf16[32,2048]{1,0:T(8,128)(2,1)} %q_in.1, bf16[32,2048]{1,0:T(8,128)(2,1)} %k_in.1, bf16[32,2048]{1,0:T(8,128)(2,1)} %v_in.1, bf16[32,2048]{1,0:T(8,128)(2,1)} %o_in.1, bf16[32,2048]{1,0:T(8,128)(2,1)} %g_in.1, f32[4,128]{1,0:T(4,128)} %bitcast.4), custom_call_target="tpu_custom_call" | custom-call | tf_op jit(solution)/shard_map/pallas_call | solution.py:42
  2.0 0.0 copy-start
  2.0 27.5 %all_to_all.10.got_ref = bf16[16,144,128]{2,1,0:T(8,128)(2,1)S(1)} all-to-all(bf16[16,144,128]{2,1,0:T(8,128)(2,1)S(1)} %shard_map.103), channel_id=1, replica_groups=mesh['y'=4,'zh'=2,'xh'=2,'xl'=2,'c'=2,'zl'=4] {'zl','zh','xl'}, dimensions={0} | all-to-all | bytes 1179648 | tf_op jit(solution)/shard_map/all_to_all | solution.py:274
  29.4 0.0 copy-done
  29.5 0.9 %shard_map.104 = (bf16[528,256]{1,0:T(8,128)(2,1)S(1)}, bf16[256,256]{1,0:T(8,128)(2,1)S(1)}, bf16[256,256]{1,0:T(8,128)(2,1)S(1)}) custom-call(bf16[16,144,128]{2,1,0:T(8,128)(2,1)S(1)} %all_to_all.10.got_ref, s32[64,128]{1,0:T(8,128)S(1)} %bitcast.2), custom_call_target="tpu_custom_call" | custom-call | tf_op jit(solution)/shard_map/pallas_call | solution.py:42
  30.3 2.5 %collective-permute-start = (bf16[528,256]{1,0:T(8,128)(2,1)S(1)}, bf16[528,256]{1,0:T(8,128)(2,1)S(1)}, u32[]{:S(2)}, u32[]{:S(2)}) collective-permute-start(bf16[528,256]{1,0:T(8,128)(2,1)S(1)} %get-tuple-element.38.qd0), channel_id=1, source_target_pairs={{0,16},{4,20},{16,0},{20,4},{1,17},{5,21},{17,1},{21,5},{2,18},{6,... | collective-permute-start | bytes 811016 | tf_op jit(solution)/shard_map/ppermute | solution.py:251
  32.8 2.7 %collective-permute-start.1 = (bf16[256,256]{1,0:T(8,128)(2,1)S(1)}, bf16[256,256]{1,0:T(8,128)(2,1)S(1)}, u32[]{:S(2)}, u32[]{:S(2)}) collective-permute-start(bf16[256,256]{1,0:T(8,128)(2,1)S(1)} %get-tuple-element.32.kv0), channel_id=1, source_target_pairs={{0,192},{64,128},{128,64},{192,0},{1,193},{65,129},{129,65},{193,1... | collective-permute-start | bytes 393224 | tf_op jit(solution)/shard_map/ppermute | solution.py:255
  35.5 0.4 collective-permute-start.2
  35.9 0.2 collective-permute-start.3
  36.1 0.8 %slice.3.ids_ref = s32[16]{0:T(128)S(1)} slice(s32[8192]{0:T(1024)} %param.14), slice={[0:8192:512]} | slice | bytes 128 | tf_op jit(solution)/shard_map/slice | solution.py:264
  37.0 1.4 %shard_map.105 = (f32[512,128]{1,0:T(8,128)S(1)}, f32[512,128]{1,0:T(8,128)S(1)}, f32[512,128]{1,0:T(8,128)S(1)}) custom-call(s32[16]{0:T(128)S(1)} %slice.3.ids_ref, bf16[528,256]{1,0:T(8,128)(2,1)S(1)} %get-tuple-element.38.qd0, bf16[256,256]{1,0:T(8,128)(2,1)S(1)} %get-tuple-element.32.kv0, bf16[256,256]{1,0:T(8,128)(2,1)S(1)} %get-tuple-element.33.kvn_ref), custom_call_target="tpu_custom_call" | custom-call | tf_op jit(solution)/shard_map/pallas_call | solution.py:42
  38.4 0.5 collective-permute-done.1.kv3
  38.9 2.1 %collective-permute-done.2.kv2 = bf16[256,256]{1,0:T(8,128)(2,1)S(1)} collective-permute-done((bf16[256,256]{1,0:T(8,128)(2,1)S(1)}, bf16[256,256]{1,0:T(8,128)(2,1)S(1)}, u32[]{:S(2)}, u32[]{:S(2)}) %collective-permute-start.2) | collective-permute-done | bytes 131104 | tf_op jit(solution)/shard_map/ppermute | solution.py:255
  40.9 0.0 collective-permute-done.3.kv1
  40.9 0.0 collective-permute-done.qd2
  40.9 4.6 %collective-permute-start.4 = (bf16[528,256]{1,0:T(8,128)(2,1)S(1)}, bf16[528,256]{1,0:T(8,128)(2,1)S(1)}, u32[]{:S(2)}, u32[]{:S(2)}) collective-permute-start(bf16[528,256]{1,0:T(8,128)(2,1)S(1)} %get-tuple-element.38.qd0), channel_id=1, source_target_pairs={{0,4},{4,0},{16,20},{20,16},{1,5},{5,1},{17,21},{21,17},{2,6},{6,2... | collective-permute-start | bytes 811016 | tf_op jit(solution)/shard_map/ppermute | solution.py:251
  45.5 0.1 collective-permute-start.5
  45.6 3.0 %shard_map.106 = (f32[2,512,128]{2,1,0:T(8,128)S(1)}, f32[1280,128]{1,0:T(8,128)S(1)}, f32[1280,128]{1,0:T(8,128)S(1)}) custom-call(s32[16]{0:T(128)S(1)} %slice.3.ids_ref, bf16[528,256]{1,0:T(8,128)(2,1)S(1)} %get-tuple-element.38.qd0, bf16[528,256]{1,0:T(8,128)(2,1)S(1)} %collective-permute-done.qd2, bf16[256,256]{1,0:T(8,128)(2,1)S(1)} %get-tuple-element.32.kv0, ...), custom_call_target="tpu_custom_call" | custom-call | tf_op jit(solution)/shard_map/pallas_call | solution.py:42
  48.6 0.0 collective-permute-done.4.qd1
  48.6 0.0 collective-permute-done.5.qd3
  48.7 3.6 %shard_map.107 = (bf16[2,512,128]{2,1,0:T(8,128)(2,1)S(1)}, f32[256,256]{1,0:T(8,128)S(1)}, bf16[256,256]{1,0:T(8,128)(2,1)S(1)}, bf16[256,256]{1,0:T(8,128)(2,1...) custom-call(s32[16]{0:T(128)S(1)} %slice.3.ids_ref, bf16[528,256]{1,0:T(8,128)(2,1)S(1)} %collective-permute-done.4.qd1, ...), custom_call_target="tpu_custom_call" | custom-call | tf_op jit(solution)/shard_map/pallas_call | solution.py:42
  52.3 0.5 collective-permute-start.6
  52.8 1.7 %collective-permute-start.8 = (bf16[256,256]{1,0:T(8,128)(2,1)S(1)}, bf16[256,256]{1,0:T(8,128)(2,1)S(1)}, u32[]{:S(2)}, u32[]{:S(2)}) collective-permute-start(bf16[256,256]{1,0:T(8,128)(2,1)S(1)} %get-tuple-element.53), channel_id=1, source_target_pairs={{0,192},{64,128},{128,64},{192,0},{1,193},{65,129},{129,65},{193,1... | collective-permute-start | bytes 393224 | tf_op jit(solution)/shard_map/ppermute | solution.py:255
  54.5 0.3 collective-permute-start.9
  54.9 1.2 %collective-permute-start.10 = (bf16[256,256]{1,0:T(8,128)(2,1)S(1)}, bf16[256,256]{1,0:T(8,128)(2,1)S(1)}, u32[]{:S(2)}, u32[]{:S(2)}) collective-permute-start(bf16[256,256]{1,0:T(8,128)(2,1)S(1)} %get-tuple-element.55), channel_id=1, source_target_pairs={{0,64},{64,0},{128,192},{192,128},{1,65},{65,1},{129,193},{193,129... | collective-permute-start | bytes 393224 | tf_op jit(solution)/shard_map/ppermute | solution.py:255
  56.1 0.0 collective-permute-done.6.got_ref
  56.1 0.1 shard_map.108
  56.1 0.6 collective-permute-start.7
  56.8 0.6 shard_map.109
  57.4 4.0 %collective-permute-done.8.dkv1 = bf16[256,256]{1,0:T(8,128)(2,1)S(1)} collective-permute-done((bf16[256,256]{1,0:T(8,128)(2,1)S(1)}, bf16[256,256]{1,0:T(8,128)(2,1)S(1)}, u32[]{:S(2)}, u32[]{:S(2)}) %collective-permute-start.8) | collective-permute-done | bytes 131104 | tf_op jit(solution)/shard_map/ppermute | solution.py:255
  61.4 0.0 collective-permute-done.9.dkv2
  61.4 0.8 %collective-permute-done.10.dkv3 = bf16[256,256]{1,0:T(8,128)(2,1)S(1)} collective-permute-done((bf16[256,256]{1,0:T(8,128)(2,1)S(1)}, bf16[256,256]{1,0:T(8,128)(2,1)S(1)}, u32[]{:S(2)}, u32[]{:S(2)}) %collective-permute-start.10) | collective-permute-done | bytes 131104 | tf_op jit(solution)/shard_map/ppermute | solution.py:255
  62.2 0.0 collective-permute-done.7.got_chip
  62.2 0.3 shard_map.110
  62.5 14.1 %all_to_all.11.got_ref = bf16[16,96,128]{2,1,0:T(8,128)(2,1)S(1)} all-to-all(bf16[16,96,128]{2,1,0:T(8,128)(2,1)S(1)} %shard_map.110), channel_id=1, replica_groups=mesh['y'=4,'zh'=2,'xh'=2,'xl'=2,'c'=2,'zl'=4] {'zh','xl','zl'}, dimensions={0} | all-to-all | bytes 786432 | tf_op jit(solution)/shard_map/all_to_all | solution.py:316
  76.6 0.8 %shard_map.111 = (bf16[32,2048]{1,0:T(8,128)(2,1)}, bf16[32,2048]{1,0:T(8,128)(2,1)}, bf16[32,2048]{1,0:T(8,128)(2,1)}) custom-call(bf16[16,96,128]{2,1,0:T(8,128)(2,1)S(1)} %all_to_all.11.got_ref), custom_call_target="tpu_custom_call" | custom-call | tf_op jit(solution)/shard_map/pallas_call | solution.py:42
Async XLA Ops:
  2.0 27.5 %copy-start = (s32[8192]{0:T(1024)S(1)}, s32[8192]{0:T(1024)}, u32[]{:S(2)}) copy-start(s32[8192]{0:T(1024)} %param.15) | copy-start | bytes 98308
  30.3 10.6 %collective-permute-start = (bf16[528,256]{1,0:T(8,128)(2,1)S(1)}, bf16[528,256]{1,0:T(8,128)(2,1)S(1)}, u32[]{:S(2)}, u32[]{:S(2)}) collective-permute-start(bf16[528,256]{1,0:T(8,128)(2,1)S(1)} %get-tuple-element.38.qd0), channel_id=1, source_target_pairs={{0,16},{4,20},{16,0},{20,4},{1,17},{5,21},{17,1},{21,5},{2,18},{6,... | collective-permute-start | bytes 811016 | tf_op jit(solution)/shard_map/ppermute | solution.py:251
  32.8 6.0 %collective-permute-start.1 = (bf16[256,256]{1,0:T(8,128)(2,1)S(1)}, bf16[256,256]{1,0:T(8,128)(2,1)S(1)}, u32[]{:S(2)}, u32[]{:S(2)}) collective-permute-start(bf16[256,256]{1,0:T(8,128)(2,1)S(1)} %get-tuple-element.32.kv0), channel_id=1, source_target_pairs={{0,192},{64,128},{128,64},{192,0},{1,193},{65,129},{129,65},{193,1... | collective-permute-start | bytes 393224 | tf_op jit(solution)/shard_map/ppermute | solution.py:255
  35.5 5.4 %collective-permute-start.2 = (bf16[256,256]{1,0:T(8,128)(2,1)S(1)}, bf16[256,256]{1,0:T(8,128)(2,1)S(1)}, u32[]{:S(2)}, u32[]{:S(2)}) collective-permute-start(bf16[256,256]{1,0:T(8,128)(2,1)S(1)} %get-tuple-element.32.kv0), channel_id=1, source_target_pairs={{0,128},{64,192},{128,0},{192,64},{1,129},{65,193},{129,1},{193,65... | collective-permute-start | bytes 393224 | tf_op jit(solution)/shard_map/ppermute | solution.py:255
  35.9 5.0 %collective-permute-start.3 = (bf16[256,256]{1,0:T(8,128)(2,1)S(1)}, bf16[256,256]{1,0:T(8,128)(2,1)S(1)}, u32[]{:S(2)}, u32[]{:S(2)}) collective-permute-start(bf16[256,256]{1,0:T(8,128)(2,1)S(1)} %get-tuple-element.32.kv0), channel_id=1, source_target_pairs={{0,64},{64,0},{128,192},{192,128},{1,65},{65,1},{129,193},{193,129... | collective-permute-start | bytes 393224 | tf_op jit(solution)/shard_map/ppermute | solution.py:255
  40.9 7.7 %collective-permute-start.4 = (bf16[528,256]{1,0:T(8,128)(2,1)S(1)}, bf16[528,256]{1,0:T(8,128)(2,1)S(1)}, u32[]{:S(2)}, u32[]{:S(2)}) collective-permute-start(bf16[528,256]{1,0:T(8,128)(2,1)S(1)} %get-tuple-element.38.qd0), channel_id=1, source_target_pairs={{0,4},{4,0},{16,20},{20,16},{1,5},{5,1},{17,21},{21,17},{2,6},{6,2... | collective-permute-start | bytes 811016 | tf_op jit(solution)/shard_map/ppermute | solution.py:251
  45.5 3.1 %collective-permute-start.5 = (bf16[528,256]{1,0:T(8,128)(2,1)S(1)}, bf16[528,256]{1,0:T(8,128)(2,1)S(1)}, u32[]{:S(2)}, u32[]{:S(2)}) collective-permute-start(bf16[528,256]{1,0:T(8,128)(2,1)S(1)} %collective-permute-done.qd2), channel_id=1, source_target_pairs={{0,4},{4,0},{16,20},{20,16},{1,5},{5,1},{17,21},{21,17},{2,6},{6,2... | collective-permute-start | bytes 811016 | tf_op jit(solution)/shard_map/ppermute | solution.py:251
  52.3 3.8 %collective-permute-start.6 = (bf16[2,512,128]{2,1,0:T(8,128)(2,1)S(1)}, bf16[2,512,128]{2,1,0:T(8,128)(2,1)S(1)}, u32[]{:S(2)}, u32[]{:S(2)}) collective-permute-start(bf16[2,512,128]{2,1,0:T(8,128)(2,1)S(1)} %get-tuple-element.49), channel_id=1, source_target_pairs={{0,4},{4,0},{16,20},{20,16},{1,5},{5,1},{17,21},{21,17},{2,6},{6,2... | collective-permute-start | bytes 786440 | tf_op jit(solution)/shard_map/ppermute | solution.py:251
  52.8 8.6 %collective-permute-start.8 = (bf16[256,256]{1,0:T(8,128)(2,1)S(1)}, bf16[256,256]{1,0:T(8,128)(2,1)S(1)}, u32[]{:S(2)}, u32[]{:S(2)}) collective-permute-start(bf16[256,256]{1,0:T(8,128)(2,1)S(1)} %get-tuple-element.53), channel_id=1, source_target_pairs={{0,192},{64,128},{128,64},{192,0},{1,193},{65,129},{129,65},{193,1... | collective-permute-start | bytes 393224 | tf_op jit(solution)/shard_map/ppermute | solution.py:255
  54.5 6.9 %collective-permute-start.9 = (bf16[256,256]{1,0:T(8,128)(2,1)S(1)}, bf16[256,256]{1,0:T(8,128)(2,1)S(1)}, u32[]{:S(2)}, u32[]{:S(2)}) collective-permute-start(bf16[256,256]{1,0:T(8,128)(2,1)S(1)} %get-tuple-element.54), channel_id=1, source_target_pairs={{0,128},{64,192},{128,0},{192,64},{1,129},{65,193},{129,1},{193,65... | collective-permute-start | bytes 393224 | tf_op jit(solution)/shard_map/ppermute | solution.py:255
  54.9 7.3 %collective-permute-start.10 = (bf16[256,256]{1,0:T(8,128)(2,1)S(1)}, bf16[256,256]{1,0:T(8,128)(2,1)S(1)}, u32[]{:S(2)}, u32[]{:S(2)}) collective-permute-start(bf16[256,256]{1,0:T(8,128)(2,1)S(1)} %get-tuple-element.55), channel_id=1, source_target_pairs={{0,64},{64,0},{128,192},{192,128},{1,65},{65,1},{129,193},{193,129... | collective-permute-start | bytes 393224 | tf_op jit(solution)/shard_map/ppermute | solution.py:255
  56.1 6.1 %collective-permute-start.7 = (bf16[512,128]{1,0:T(8,128)(2,1)S(1)}, bf16[512,128]{1,0:T(8,128)(2,1)S(1)}, u32[]{:S(2)}, u32[]{:S(2)}) collective-permute-start(bf16[512,128]{1,0:T(8,128)(2,1)S(1)} %get-tuple-element.51), channel_id=1, source_target_pairs={{0,16},{4,20},{16,0},{20,4},{1,17},{5,21},{17,1},{21,5},{2,18},{6,... | collective-permute-start | bytes 393224 | tf_op jit(solution)/shard_map/ppermute | solution.py:251

commit v8 on v7

--- a/solution.py
+++ b/solution.py
@@ -50,13 +50,21 @@
     )(*args)
 
 
-def pack_kernel(q_in, k_in, v_in, o_in, g_in, lse_in, out_ref, q_ref, k_ref, v_ref, o_ref, g_ref, lse_ref, sems):
-    pairs = ((g_in, g_ref), (o_in, o_ref), (lse_in, lse_ref), (q_in, q_ref), (k_in, k_ref), (v_in, v_ref))
+def pack_kernel(
+    q_in, k_in, v_in, o_in, g_in, lse_in, copy_in, out_ref, there_ref, back_ref,
+    q_ref, k_ref, v_ref, o_ref, g_ref, lse_ref, copy_ref, sems,
+):
+    pairs = ((copy_in, copy_ref), (g_in, g_ref), (o_in, o_ref), (lse_in, lse_ref), (q_in, q_ref), (k_in, k_ref), (v_in, v_ref))
     copies = [pltpu.make_async_copy(a, b, sems.at[i]) for i, (a, b) in enumerate(pairs)]
     for copy in copies:
         copy.start()
     rows = q_ref.shape[0]
-    for copy in copies[:3]:
+    copies[0].wait()
+    for j in range(RUNS):
+        one_hot = placing(copy_ref, j)
+        there_ref[j] = one_hot.astype(BF16)
+        back_ref[j] = one_hot.T.astype(BF16)
+    for copy in copies[1:4]:
         copy.wait()
     lane = iota((rows, 128), 1)
     delta = jnp.zeros((rows, 128), F32)
@@ -68,7 +76,7 @@
     delta_high, delta_low = split_two(delta)
     lse_high, lse_low = split_two(lse_ref[...])
     row = iota((16, 128), 0)
-    for copy in copies[3:]:
+    for copy in copies[4:]:
         copy.wait()
     for h in range(16):
         j = h % 4
@@ -94,13 +102,13 @@
     return (iota((RUN, RUN), 0) == place).astype(F32)
 
 
-def sort_kernel(got_ref, copy_ref, qd_ref, kv_ref, kvn_ref):
+def sort_kernel(got_ref, there_ref, qd_ref, kv_ref, kvn_ref):
     zl = lax.axis_index("zl")
     row = iota((16, RUN), 0)
     stats = []
     for j in range(RUNS):
         zh, xl = divmod(j, 2)
-        one_hot = placing(copy_ref, j).astype(BF16)
+        one_hot = there_ref[j]
         parts = [
             jnp.concatenate([got_ref[4 * z + j, 32 * i : 32 * i + 32, :] for z in range(4)], axis=0)
             for i in range(4)
@@ -213,10 +221,9 @@
     sum_ref[...] = keep_ref[0] + got_ref[0].astype(F32)
 
 
-def prepare_kernel(dkvn_ref, copy_ref, one_hot_ref, noisy_ref):
+def prepare_kernel(dkvn_ref, back_ref, noisy_ref):
     for j in range(RUNS):
-        one_hot = placing(copy_ref, j).T.astype(BF16)
-        one_hot_ref[j] = one_hot
+        one_hot = back_ref[j]
         rows = dkvn_ref[64 * j : 64 * j + 64, :]
         noisy_ref[j] = contract(one_hot, jnp.concatenate([rows, jnp.zeros_like(rows)], axis=0), 1, 0).astype(BF16)
 
@@ -263,17 +270,19 @@
     copies = row_copy.reshape(-1, RUN)
     ids = row_block[:: 4 * RUN]
     rows = query_in.shape[0]
-    arrays = (query_in, key_in, value_in, saved_out, grad_out, saved_lse.T)
-    packed = call(
+    arrays = (query_in, key_in, value_in, saved_out, grad_out, saved_lse.T, copies)
+    packed, there, back_places = call(
         pack_kernel,
-        shape((16, 4 * rows + 16, HD)),
+        (shape((16, 4 * rows + 16, HD)),) + (shape((RUNS, RUN, RUN)),) * 2,
         tuple(pltpu.with_memory_space_constraint(x, pltpu.HBM) for x in arrays),
-        hbm=range(6),
-        scratch=[pltpu.VMEM(query_in.shape, BF16)] * 5 + [pltpu.VMEM((4, 128), F32), pltpu.SemaphoreType.DMA((6,))],
+        hbm=range(7),
+        scratch=[pltpu.VMEM(query_in.shape, BF16)] * 5 + [
+            pltpu.VMEM((4, 128), F32), pltpu.VMEM(copies.shape, copies.dtype), pltpu.SemaphoreType.DMA((7,))
+        ],
     )
     got = lax.all_to_all(packed, HEAD_AXES, 0, 0, tiled=True)
     qd, kv, kvn = call(
-        sort_kernel, (shape((528, 256)), shape((256, 256)), shape((256, 256))), (got, copies)
+        sort_kernel, (shape((528, 256)), shape((256, 256)), shape((256, 256))), (got, there)
     )
     qd2 = swap(qd, 2)
     kv3, kv2, kv1 = (swap_y(kv, m) for m in (3, 2, 1))
@@ -305,13 +314,11 @@
     for m in (2, 1, 3):
         dkvs[m] = swap_y(dkvs[m], m)
     half, dq_sum = call(add_kernel, (shape((512, HD)), shape((512, HD), F32)), (dq_keep, dq_core))
-    one_hot, noisy = call(
-        prepare_kernel, (shape((RUNS, RUN, RUN)), shape((RUNS, RUN, 256))), (dkvn, copies)
-    )
+    noisy = call(prepare_kernel, shape((RUNS, RUN, 256)), (dkvn, back_places))
     back = call(
         unsort_kernel,
         shape((16, 3 * rows, HD)),
-        (dq_sum, swap(half, 2), dkvs[0], dkvs[3], dkvs[2], dkvs[1], one_hot, noisy),
+        (dq_sum, swap(half, 2), dkvs[0], dkvs[3], dkvs[2], dkvs[1], back_places, noisy),
     )
     back = lax.all_to_all(back, BACK_AXES, 0, 0, tiled=True)
     return call(unpack_kernel, (shape((rows, 16 * HD)),) * 3, (back,))

time: 78.6 us -> 78.1 us (level)
  Pallas kernels: 12 us -> 11.2 us
    pallas_call x9, Pallas kernels: 12 us -> 11.2 us  [call(): pl.pallas_call(body, out_shape=out_shape, in_specs=[SMEM if i in smem els...]
  transfers between devices with their start and end apart: 11 -> 11, of which waited for: 4 -> 4; matrix products, arithmetic and copies ran while one was open for 1% -> 1% of each run, Pallas kernels for 7% -> 6%
where the time goes in v8:
time: 78.1 us; the launch traced here: 77 us
  blocking collectives  41.6 us (53%)
  starting transfers between devices  14.9 us (19%)
  Pallas kernels  11.2 us (14%)
  waiting for transfers between devices  7.77 us (10%)
  local copies, waits for them, and re-layouts  0.85 us (1%)
    all_to_all x1, blocking collectives, per_device(): got = lax.all_to_all(packed, HEAD_AXES, 0, 0, tiled=True)  27.5 us
    all_to_all x1, blocking collectives, per_device(): back = lax.all_to_all(back, BACK_AXES, 0, 0, tiled=True)  14.1 us
    pallas_call x9, Pallas kernels, call(): pl.pallas_call(body, out_shape=out_shape, in_specs=[SMEM if i in smem els...  11.2 us
    ppermute x5, starting transfers between devices, swap(): return lax.ppermute(x, QUERY_AXES, [(i, i ^ mask) for i in range(4)])  8.31 us
    ppermute x6, waiting for transfers between devices, swap_y(): return lax.ppermute(x, 'y', [(i, i ^ mask) for i in range(4)])  7.76 us
    ppermute x6, starting transfers between devices, swap_y(): return lax.ppermute(x, 'y', [(i, i ^ mask) for i in range(4)])  6.59 us
  transfers between devices with their start and end apart: 11, of which 4 were waited for; matrix products, arithmetic and copies ran while one was open for 1% of the time, Pallas kernels for 6%

profile of v8, /device:TPU:1, one launch (start us, length us, event | category | flops | bytes accessed | tf_op | source)
XLA Modules:
  0.0 77.0 jit_solution(15477040242417199699)
XLA Ops:
  0.6 1.4 %shard_map.103 = (bf16[16,144,128]{2,1,0:T(8,128)(2,1)S(1)}, bf16[4,128,128]{2,1,0:T(8,128)(2,1)S(1)}, bf16[4,128,128]{2,1,0:T(8,128)(2,1)S(1)}) custom-call(bf16[32,2048]{1,0:T(8,128)(2,1)} %q_in.1, bf16[32,2048]{1,0:T(8,128)(2,1)} %k_in.1, bf16[32,2048]{1,0:T(8,128)(2,1)} %v_in.1, bf16[32,2048]{1,0:T(8,128)(2,1)} %o_in.1, bf16[32,2048]{1,0:T(8,128)(2,1)} %g_in.1, ...), custom_call_target="tpu_custom_call" | custom-call | tf_op jit(solution)/shard_map/pallas_call | solution.py:42
  2.0 27.5 %all_to_all.10.got_ref = bf16[16,144,128]{2,1,0:T(8,128)(2,1)S(1)} all-to-all(bf16[16,144,128]{2,1,0:T(8,128)(2,1)S(1)} %get-tuple-element.32), channel_id=1, replica_groups=mesh['y'=4,'zh'=2,'xh'=2,'xl'=2,'c'=2,'zl'=4] {'zl','zh','xl'}, dimensions={0} | all-to-all | bytes 1179648 | tf_op jit(solution)/shard_map/all_to_all | solution.py:283
  29.5 0.4 shard_map.104
  29.9 2.5 %collective-permute-start = (bf16[528,256]{1,0:T(8,128)(2,1)S(1)}, bf16[528,256]{1,0:T(8,128)(2,1)S(1)}, u32[]{:S(2)}, u32[]{:S(2)}) collective-permute-start(bf16[528,256]{1,0:T(8,128)(2,1)S(1)} %get-tuple-element.41.qd0), channel_id=1, source_target_pairs={{0,16},{4,20},{16,0},{20,4},{1,17},{5,21},{17,1},{21,5},{2,18},{6,... | collective-permute-start | bytes 811016 | tf_op jit(solution)/shard_map/ppermute | solution.py:258
  32.4 2.7 %collective-permute-start.1 = (bf16[256,256]{1,0:T(8,128)(2,1)S(1)}, bf16[256,256]{1,0:T(8,128)(2,1)S(1)}, u32[]{:S(2)}, u32[]{:S(2)}) collective-permute-start(bf16[256,256]{1,0:T(8,128)(2,1)S(1)} %get-tuple-element.35.kv0), channel_id=1, source_target_pairs={{0,192},{64,128},{128,64},{192,0},{1,193},{65,129},{129,65},{193,1... | collective-permute-start | bytes 393224 | tf_op jit(solution)/shard_map/ppermute | solution.py:262
  35.1 0.3 collective-permute-start.2
  35.5 0.2 collective-permute-start.3
  35.7 0.8 %slice.3.ids_ref = s32[16]{0:T(128)S(1)} slice(s32[8192]{0:T(1024)} %param.14), slice={[0:8192:512]} | slice | bytes 128 | tf_op jit(solution)/shard_map/slice | solution.py:271
  36.6 1.4 %shard_map.105 = (f32[512,128]{1,0:T(8,128)S(1)}, f32[512,128]{1,0:T(8,128)S(1)}, f32[512,128]{1,0:T(8,128)S(1)}) custom-call(s32[16]{0:T(128)S(1)} %slice.3.ids_ref, bf16[528,256]{1,0:T(8,128)(2,1)S(1)} %get-tuple-element.41.qd0, bf16[256,256]{1,0:T(8,128)(2,1)S(1)} %get-tuple-element.35.kv0, bf16[256,256]{1,0:T(8,128)(2,1)S(1)} %get-tuple-element.36.kvn_ref), custom_call_target="tpu_custom_call" | custom-call | tf_op jit(solution)/shard_map/pallas_call | solution.py:42
  38.0 0.5 collective-permute-done.1.kv3
  38.4 2.1 %collective-permute-done.2.kv2 = bf16[256,256]{1,0:T(8,128)(2,1)S(1)} collective-permute-done((bf16[256,256]{1,0:T(8,128)(2,1)S(1)}, bf16[256,256]{1,0:T(8,128)(2,1)S(1)}, u32[]{:S(2)}, u32[]{:S(2)}) %collective-permute-start.2) | collective-permute-done | bytes 131104 | tf_op jit(solution)/shard_map/ppermute | solution.py:262
  40.5 0.0 collective-permute-done.3.kv1
  40.5 0.0 collective-permute-done.qd2
  40.5 4.6 %collective-permute-start.4 = (bf16[528,256]{1,0:T(8,128)(2,1)S(1)}, bf16[528,256]{1,0:T(8,128)(2,1)S(1)}, u32[]{:S(2)}, u32[]{:S(2)}) collective-permute-start(bf16[528,256]{1,0:T(8,128)(2,1)S(1)} %get-tuple-element.41.qd0), channel_id=1, source_target_pairs={{0,4},{4,0},{16,20},{20,16},{1,5},{5,1},{17,21},{21,17},{2,6},{6,2... | collective-permute-start | bytes 811016 | tf_op jit(solution)/shard_map/ppermute | solution.py:258
  45.1 0.1 collective-permute-start.5
  45.2 3.0 %shard_map.106 = (f32[2,512,128]{2,1,0:T(8,128)S(1)}, f32[1280,128]{1,0:T(8,128)S(1)}, f32[1280,128]{1,0:T(8,128)S(1)}) custom-call(s32[16]{0:T(128)S(1)} %slice.3.ids_ref, bf16[528,256]{1,0:T(8,128)(2,1)S(1)} %get-tuple-element.41.qd0, bf16[528,256]{1,0:T(8,128)(2,1)S(1)} %collective-permute-done.qd2, bf16[256,256]{1,0:T(8,128)(2,1)S(1)} %get-tuple-element.35.kv0, ...), custom_call_target="tpu_custom_call" | custom-call | tf_op jit(solution)/shard_map/pallas_call | solution.py:42
  48.2 0.0 collective-permute-done.4.qd1
  48.2 0.0 collective-permute-done.5.qd3
  48.3 3.6 %shard_map.107 = (bf16[2,512,128]{2,1,0:T(8,128)(2,1)S(1)}, f32[256,256]{1,0:T(8,128)S(1)}, bf16[256,256]{1,0:T(8,128)(2,1)S(1)}, bf16[256,256]{1,0:T(8,128)(2,1...) custom-call(s32[16]{0:T(128)S(1)} %slice.3.ids_ref, bf16[528,256]{1,0:T(8,128)(2,1)S(1)} %collective-permute-done.4.qd1, ...), custom_call_target="tpu_custom_call" | custom-call | tf_op jit(solution)/shard_map/pallas_call | solution.py:42
  51.9 0.5 collective-permute-start.6
  52.4 1.7 %collective-permute-start.8 = (bf16[256,256]{1,0:T(8,128)(2,1)S(1)}, bf16[256,256]{1,0:T(8,128)(2,1)S(1)}, u32[]{:S(2)}, u32[]{:S(2)}) collective-permute-start(bf16[256,256]{1,0:T(8,128)(2,1)S(1)} %get-tuple-element.56), channel_id=1, source_target_pairs={{0,192},{64,128},{128,64},{192,0},{1,193},{65,129},{129,65},{193,1... | collective-permute-start | bytes 393224 | tf_op jit(solution)/shard_map/ppermute | solution.py:262
  54.1 0.3 collective-permute-start.9
  54.5 1.2 %collective-permute-start.10 = (bf16[256,256]{1,0:T(8,128)(2,1)S(1)}, bf16[256,256]{1,0:T(8,128)(2,1)S(1)}, u32[]{:S(2)}, u32[]{:S(2)}) collective-permute-start(bf16[256,256]{1,0:T(8,128)(2,1)S(1)} %get-tuple-element.58), channel_id=1, source_target_pairs={{0,64},{64,0},{128,192},{192,128},{1,65},{65,1},{129,193},{193,129... | collective-permute-start | bytes 393224 | tf_op jit(solution)/shard_map/ppermute | solution.py:262
  55.7 0.0 collective-permute-done.6.got_ref
  55.7 0.1 shard_map.108
  55.7 0.6 collective-permute-start.7
  56.3 0.2 shard_map.109.noisy_ref
  56.6 4.4 %collective-permute-done.8.dkv1 = bf16[256,256]{1,0:T(8,128)(2,1)S(1)} collective-permute-done((bf16[256,256]{1,0:T(8,128)(2,1)S(1)}, bf16[256,256]{1,0:T(8,128)(2,1)S(1)}, u32[]{:S(2)}, u32[]{:S(2)}) %collective-permute-start.8) | collective-permute-done | bytes 131104 | tf_op jit(solution)/shard_map/ppermute | solution.py:262
  61.0 0.0 collective-permute-done.9.dkv2
  61.0 0.8 %collective-permute-done.10.dkv3 = bf16[256,256]{1,0:T(8,128)(2,1)S(1)} collective-permute-done((bf16[256,256]{1,0:T(8,128)(2,1)S(1)}, bf16[256,256]{1,0:T(8,128)(2,1)S(1)}, u32[]{:S(2)}, u32[]{:S(2)}) %collective-permute-start.10) | collective-permute-done | bytes 131104 | tf_op jit(solution)/shard_map/ppermute | solution.py:262
  61.8 0.0 collective-permute-done.7.got_chip
  61.8 0.3 shard_map.110
  62.1 14.1 %all_to_all.11.got_ref = bf16[16,96,128]{2,1,0:T(8,128)(2,1)S(1)} all-to-all(bf16[16,96,128]{2,1,0:T(8,128)(2,1)S(1)} %shard_map.110), channel_id=1, replica_groups=mesh['y'=4,'zh'=2,'xh'=2,'xl'=2,'c'=2,'zl'=4] {'zh','xl','zl'}, dimensions={0} | all-to-all | bytes 786432 | tf_op jit(solution)/shard_map/all_to_all | solution.py:323
  76.2 0.8 %shard_map.111 = (bf16[32,2048]{1,0:T(8,128)(2,1)}, bf16[32,2048]{1,0:T(8,128)(2,1)}, bf16[32,2048]{1,0:T(8,128)(2,1)}) custom-call(bf16[16,96,128]{2,1,0:T(8,128)(2,1)S(1)} %all_to_all.11.got_ref), custom_call_target="tpu_custom_call" | custom-call | tf_op jit(solution)/shard_map/pallas_call | solution.py:42
Async XLA Ops:
  29.9 10.7 %collective-permute-start = (bf16[528,256]{1,0:T(8,128)(2,1)S(1)}, bf16[528,256]{1,0:T(8,128)(2,1)S(1)}, u32[]{:S(2)}, u32[]{:S(2)}) collective-permute-start(bf16[528,256]{1,0:T(8,128)(2,1)S(1)} %get-tuple-element.41.qd0), channel_id=1, source_target_pairs={{0,16},{4,20},{16,0},{20,4},{1,17},{5,21},{17,1},{21,5},{2,18},{6,... | collective-permute-start | bytes 811016 | tf_op jit(solution)/shard_map/ppermute | solution.py:258
  32.4 6.1 %collective-permute-start.1 = (bf16[256,256]{1,0:T(8,128)(2,1)S(1)}, bf16[256,256]{1,0:T(8,128)(2,1)S(1)}, u32[]{:S(2)}, u32[]{:S(2)}) collective-permute-start(bf16[256,256]{1,0:T(8,128)(2,1)S(1)} %get-tuple-element.35.kv0), channel_id=1, source_target_pairs={{0,192},{64,128},{128,64},{192,0},{1,193},{65,129},{129,65},{193,1... | collective-permute-start | bytes 393224 | tf_op jit(solution)/shard_map/ppermute | solution.py:262
  35.1 5.4 %collective-permute-start.2 = (bf16[256,256]{1,0:T(8,128)(2,1)S(1)}, bf16[256,256]{1,0:T(8,128)(2,1)S(1)}, u32[]{:S(2)}, u32[]{:S(2)}) collective-permute-start(bf16[256,256]{1,0:T(8,128)(2,1)S(1)} %get-tuple-element.35.kv0), channel_id=1, source_target_pairs={{0,128},{64,192},{128,0},{192,64},{1,129},{65,193},{129,1},{193,65... | collective-permute-start | bytes 393224 | tf_op jit(solution)/shard_map/ppermute | solution.py:262
  35.5 5.1 %collective-permute-start.3 = (bf16[256,256]{1,0:T(8,128)(2,1)S(1)}, bf16[256,256]{1,0:T(8,128)(2,1)S(1)}, u32[]{:S(2)}, u32[]{:S(2)}) collective-permute-start(bf16[256,256]{1,0:T(8,128)(2,1)S(1)} %get-tuple-element.35.kv0), channel_id=1, source_target_pairs={{0,64},{64,0},{128,192},{192,128},{1,65},{65,1},{129,193},{193,129... | collective-permute-start | bytes 393224 | tf_op jit(solution)/shard_map/ppermute | solution.py:262
  40.5 7.7 %collective-permute-start.4 = (bf16[528,256]{1,0:T(8,128)(2,1)S(1)}, bf16[528,256]{1,0:T(8,128)(2,1)S(1)}, u32[]{:S(2)}, u32[]{:S(2)}) collective-permute-start(bf16[528,256]{1,0:T(8,128)(2,1)S(1)} %get-tuple-element.41.qd0), channel_id=1, source_target_pairs={{0,4},{4,0},{16,20},{20,16},{1,5},{5,1},{17,21},{21,17},{2,6},{6,2... | collective-permute-start | bytes 811016 | tf_op jit(solution)/shard_map/ppermute | solution.py:258
  45.1 3.1 %collective-permute-start.5 = (bf16[528,256]{1,0:T(8,128)(2,1)S(1)}, bf16[528,256]{1,0:T(8,128)(2,1)S(1)}, u32[]{:S(2)}, u32[]{:S(2)}) collective-permute-start(bf16[528,256]{1,0:T(8,128)(2,1)S(1)} %collective-permute-done.qd2), channel_id=1, source_target_pairs={{0,4},{4,0},{16,20},{20,16},{1,5},{5,1},{17,21},{21,17},{2,6},{6,2... | collective-permute-start | bytes 811016 | tf_op jit(solution)/shard_map/ppermute | solution.py:258
  51.9 3.8 %collective-permute-start.6 = (bf16[2,512,128]{2,1,0:T(8,128)(2,1)S(1)}, bf16[2,512,128]{2,1,0:T(8,128)(2,1)S(1)}, u32[]{:S(2)}, u32[]{:S(2)}) collective-permute-start(bf16[2,512,128]{2,1,0:T(8,128)(2,1)S(1)} %get-tuple-element.52), channel_id=1, source_target_pairs={{0,4},{4,0},{16,20},{20,16},{1,5},{5,1},{17,21},{21,17},{2,6},{6,2... | collective-permute-start | bytes 786440 | tf_op jit(solution)/shard_map/ppermute | solution.py:258
  52.4 8.6 %collective-permute-start.8 = (bf16[256,256]{1,0:T(8,128)(2,1)S(1)}, bf16[256,256]{1,0:T(8,128)(2,1)S(1)}, u32[]{:S(2)}, u32[]{:S(2)}) collective-permute-start(bf16[256,256]{1,0:T(8,128)(2,1)S(1)} %get-tuple-element.56), channel_id=1, source_target_pairs={{0,192},{64,128},{128,64},{192,0},{1,193},{65,129},{129,65},{193,1... | collective-permute-start | bytes 393224 | tf_op jit(solution)/shard_map/ppermute | solution.py:262
  54.1 6.9 %collective-permute-start.9 = (bf16[256,256]{1,0:T(8,128)(2,1)S(1)}, bf16[256,256]{1,0:T(8,128)(2,1)S(1)}, u32[]{:S(2)}, u32[]{:S(2)}) collective-permute-start(bf16[256,256]{1,0:T(8,128)(2,1)S(1)} %get-tuple-element.57), channel_id=1, source_target_pairs={{0,128},{64,192},{128,0},{192,64},{1,129},{65,193},{129,1},{193,65... | collective-permute-start | bytes 393224 | tf_op jit(solution)/shard_map/ppermute | solution.py:262
  54.5 7.3 %collective-permute-start.10 = (bf16[256,256]{1,0:T(8,128)(2,1)S(1)}, bf16[256,256]{1,0:T(8,128)(2,1)S(1)}, u32[]{:S(2)}, u32[]{:S(2)}) collective-permute-start(bf16[256,256]{1,0:T(8,128)(2,1)S(1)} %get-tuple-element.58), channel_id=1, source_target_pairs={{0,64},{64,0},{128,192},{192,128},{1,65},{65,1},{129,193},{193,129... | collective-permute-start | bytes 393224 | tf_op jit(solution)/shard_map/ppermute | solution.py:262
  55.7 6.1 %collective-permute-start.7 = (bf16[512,128]{1,0:T(8,128)(2,1)S(1)}, bf16[512,128]{1,0:T(8,128)(2,1)S(1)}, u32[]{:S(2)}, u32[]{:S(2)}) collective-permute-start(bf16[512,128]{1,0:T(8,128)(2,1)S(1)} %get-tuple-element.54), channel_id=1, source_target_pairs={{0,16},{4,20},{16,0},{20,4},{1,17},{5,21},{17,1},{21,5},{2,18},{6,... | collective-permute-start | bytes 393224 | tf_op jit(solution)/shard_map/ppermute | solution.py:258
